TPU v7x, 32 devices: a whole 2x2x4 slice. The times are simulated.
32 devices in a mesh: scene: 16 (over z, y, core), tile: 2 (over x).
Axes of the slice: x: 2, y: 2, z: 4, core: 2. Of those that a mesh axis runs over, the one named last changes fastest.
Arguments:
- features_in: bfloat16 [16, 4, 64, 4096], P('scene', 'tile'), may hold values from -6 to 6
- strided_weights: bfloat16 [2, 64, 1024], replicated, may hold values from -0.1875 to 0.1875
- dilated_weights: bfloat16 [2, 64, 576], replicated, may hold values from -0.25 to 0.25
- tile_bias: float32 [32, 64], replicated, may hold values from -3 to 3
- cost_cotangent: bfloat16 [16, 4, 1024], P('scene', 'tile'), may hold values from -6 to 6
- footprint_pairing: int32 [8, 4], replicated, may hold values from 0 to 3, each once within a row
- valid_counts: int32 [8], replicated, may hold values from 1 to 4, as said below
- tile_owner: int32 [16], replicated, may hold values from 0 to 31, as said below
Outputs:
- grad_features: bfloat16 [16, 4, 64, 4096], P('scene', 'tile')
- grad_weights: float32 [128, 1600], P('scene')
- grad_bias: float32 [32, 64], P(('scene', 'tile'))
Inputs may be any that keep to these rules, and one draw needn't show every extreme that they name: `footprint_pairing`: row k maps each patch of scene 2k to the patch of scene 2k + 1 that covers its footprint; each row is a permutation. `valid_counts`: patches 0 to count - 1 of both scenes of a pair are live; some pair has all 4 live. `tile_owner`: several scenes may share a tile, and many tiles have no scene.
All inputs are finite; a program needn't handle non-finite values.
Results may differ from a plain program's by a relative error of at most 0.007.
Values may be sent and summed in bfloat16 or wider, within the bound.
No kernel may reach another device: no remote copies, remote signals or barrier semaphores. Data moves between devices by JAX's collectives and lax.ppermute only.
A program may use at most 64 MiB of HBM per device.

v0:
```python
import math

import jax
import jax.numpy as jnp
from jax import lax
from jax.sharding import PartitionSpec as P


def from_partner(x, axis, distance):
    return lax.ppermute(x, axis, [(i, i ^ 1 << distance) for i in range(lax.axis_size(axis))])


def apply_convolution(
    left_operand,
    right_operand,
    window_strides,
    border_padding,
    left_dilation,
    right_dilation,
    dimension_labels,
):
    return lax.conv_general_dilated(
        left_operand,
        right_operand,
        window_strides,
        border_padding,
        lhs_dilation=left_dilation,
        rhs_dilation=right_dilation,
        dimension_numbers=dimension_labels,
        preferred_element_type=jnp.float32,
    )


def silu_slope(pre_act):
    sigmoid_gate = jax.nn.sigmoid(pre_act)
    return sigmoid_gate * (1.0 + pre_act * (1.0 - sigmoid_gate))


def match_rows(pairing_row, branch, first_patch, patch_count):
    total_patches = pairing_row.shape[0]
    all_patches = jnp.arange(total_patches, dtype=jnp.int32)
    inverse = jnp.sum(
        jnp.where(pairing_row[:, None] == all_patches[None, :], all_patches[:, None], 0), axis=0
    )
    positions = first_patch + jnp.arange(patch_count, dtype=jnp.int32)
    return jnp.where(branch == 0, jnp.take(pairing_row, positions), jnp.take(inverse, positions))


def local(
    features_in,
    strided_weights,
    dilated_weights,
    tile_bias,
    cost_cotangent,
    footprint_pairing,
    valid_counts,
    tile_owner,
):
    scene_index = lax.axis_index("scene")
    tile_index = lax.axis_index("tile")
    branch = scene_index % 2
    pair_index = scene_index // 2
    features = features_in[0]
    own_cotangent = cost_cotangent[0]
    patches, channels, cells_in = (features.shape[0], features.shape[1], features.shape[2])
    cells_out = own_cotangent.shape[1]
    grid_side = math.isqrt(cells_in)
    half_side = grid_side // 2
    strided_kernel = lax.dynamic_index_in_dim(strided_weights, branch, 0, keepdims=False).reshape(
        channels, channels, 4, 4
    )
    dilated_kernel = lax.dynamic_index_in_dim(dilated_weights, branch, 0, keepdims=False).reshape(
        channels, channels, 3, 3
    )
    tile_id = lax.dynamic_index_in_dim(tile_owner, scene_index, 0, keepdims=False)
    bias_row = lax.dynamic_index_in_dim(tile_bias, tile_id, 0, keepdims=False)
    plain = ("NCHW", "OIHW", "NCHW")
    flipped = ("NCHW", "IOHW", "NCHW")
    kernel_side = ("CNHW", "IOHW", "CNHW")
    feature_grid = features.reshape(patches, channels, grid_side, grid_side)
    pre_act = (
        apply_convolution(
            feature_grid, strided_kernel, (2, 2), ((1, 1), (1, 1)), (1, 1), (1, 1), plain
        )
        + bias_row[None, :, None, None]
    )
    activation = jax.nn.silu(pre_act).astype(jnp.bfloat16)
    branch_grid = apply_convolution(
        activation, dilated_kernel, (1, 1), ((2, 2), (2, 2)), (1, 1), (2, 2), plain
    ).astype(jnp.bfloat16)
    branch_out = branch_grid.reshape(patches, channels, cells_out)
    pairing_row = lax.dynamic_index_in_dim(footprint_pairing, pair_index, 0, keepdims=False)
    first_patch = tile_index * patches
    swapped_out, swapped_cot = from_partner((branch_out, own_cotangent), "scene", 0)
    partner_out, partner_cot = (
        lax.all_gather(swapped_out, "tile", axis=0, tiled=True),
        lax.all_gather(swapped_cot, "tile", axis=0, tiled=True),
    )
    matched = match_rows(pairing_row, branch, first_patch, patches)
    chosen_out = jnp.take(partner_out, matched, axis=0)
    chosen_cot = jnp.take(partner_cot, matched, axis=0)
    pair_valid = lax.dynamic_index_in_dim(valid_counts, pair_index, 0, keepdims=False)
    live_count = jnp.clip(pair_valid - first_patch, 0, patches)
    live_mask = (jnp.arange(patches, dtype=jnp.int32) < live_count).astype(jnp.float32)
    signal = (own_cotangent.astype(jnp.float32) + chosen_cot.astype(jnp.float32)) * live_mask[
        :, None
    ]
    out_grad = (signal[:, None, :] * chosen_out.astype(jnp.float32)).astype(jnp.bfloat16)
    out_grid = out_grad.reshape(patches, channels, half_side, half_side)
    act_grad = apply_convolution(
        out_grid,
        dilated_kernel[:, :, ::-1, ::-1],
        (1, 1),
        ((2, 2), (2, 2)),
        (1, 1),
        (2, 2),
        flipped,
    )
    grad_dilated = apply_convolution(
        activation, out_grid, (2, 2), ((2, 2), (2, 2)), (1, 1), (1, 1), kernel_side
    )
    pre_grad = act_grad * silu_slope(pre_act)
    bias_grad = jnp.sum(pre_grad, axis=(0, 2, 3))
    pre_narrow = pre_grad.astype(jnp.bfloat16)
    grad_strided = apply_convolution(
        feature_grid, pre_narrow, (1, 1), ((1, 1), (1, 1)), (1, 1), (2, 2), kernel_side
    )
    feature_grad = apply_convolution(
        pre_narrow,
        strided_kernel[:, :, ::-1, ::-1],
        (1, 1),
        ((2, 2), (2, 2)),
        (2, 2),
        (1, 1),
        flipped,
    )
    feature_grads = feature_grad.astype(jnp.bfloat16).reshape(patches, channels, cells_in)
    grad_row = jnp.concatenate(
        [
            grad_strided.reshape(channels, 16 * channels),
            grad_dilated.reshape(channels, 9 * channels),
        ],
        axis=1,
    )
    scenes = lax.axis_size("scene")
    tile_devices = lax.axis_size("tile")
    weight_scale = 1.0 / math.sqrt(scenes * patches * tile_devices * cells_out)
    bias_scale = 1.0 / math.sqrt(patches * tile_devices * cells_out)
    branch_hit = jnp.arange(2, dtype=jnp.int32)[:, None, None] == branch
    weight_term = jnp.where(branch_hit, (grad_row * weight_scale)[None], jnp.float32(0.0)).reshape(
        2 * channels, 25 * channels
    )
    partial_rows = lax.psum_scatter(weight_term, "scene", scatter_dimension=0, tiled=True)
    grad_weights = lax.psum(partial_rows, "tile")
    bias_rows = tile_bias.shape[0] // (scenes * tile_devices)
    scaled_bias = bias_grad * bias_scale
    owned_mask = tile_id == jnp.arange(
        lax.axis_size(("scene", "tile")) * bias_rows, dtype=jnp.int32
    )
    grad_bias = lax.psum_scatter(
        jnp.where(owned_mask[:, None], scaled_bias[None, :], jnp.float32(0.0)),
        ("scene", "tile"),
        scatter_dimension=0,
        tiled=True,
    )
    return (feature_grads[None], grad_weights, grad_bias)


def solution(mesh):
    return jax.shard_map(
        local,
        mesh=mesh,
        in_specs=(
            P("scene", "tile", None, None),
            P(),
            P(),
            P(),
            P("scene", "tile", None),
            P(),
            P(),
            P(),
        ),
        out_specs=(P("scene", "tile", None, None), P("scene", None), P(("scene", "tile"), None)),
        check_vma=False,
    )
```

profile of v0, /device:TPU:0, one launch (start us, length us, event | category | flops | bytes accessed | tf_op | source)
XLA Modules:
  0.0 222.6 jit_solution(17907842562558118879)
XLA Ops:
  7.8 1.2 dynamic_slice.27
  12.5 1.0 copy.169
  13.4 2.3 %reshape_squeeze.3 = bf16[2,64,64,64]{3,2,1,0:T(8,128)(2,1)S(1)} reshape(bf16[1,2,64,4096]{3,2,1,0:T(8,128)(2,1)S(1)} %copy-done.10) | data formatting | bytes 2097152 | tf_op jit(solution)/shard_map/reshape;squeeze | solution.py:80
  15.7 2.9 %copy.200 = bf16[64,64,2,64]{1,0,3,2:T(8,128)(2,1)} copy(bf16[64,64,2,64]{3,1,0,2:T(8,128)(2,1)S(1)} %bitcast.75) | data formatting | bytes 2097152
  18.7 3.4 %fusion.60 = (bf16[64,64,2,80]{1,0,3,2:T(8,128)(2,1)S(1)}, bf16[64,64,2,80]{1,0,3,2:T(8,128)(2,1)S(1)}) fusion(bf16[64,64,2,64]{1,0,3,2:T(8,128)(2,1)} %copy.200), kind=kLoop, calls=%fused_computation.99 | loop fusion | bytes 3670016 | tf_op jit(solution)/shard_map/reshape;squeeze | solution.py:80
  22.1 2.7 %fusion.12 = bf16[64,64,2,8,13]{1,0,4,3,2:T(8,128)(2,1)} fusion(bf16[64,64,2,7,3]{1,0,4,3,2:T(8,128)(2,1)S(1)} %slice.26, bf16[64,64,2,8,10]{1,0,4,3,2:T(8,128)(2,1)S(1)} %bitcast.73), kind=kLoop, calls=%fused_computation.19 | loop fusion | flops 5111808 | bytes 3358720 | tf_op jit(solution)/shard_map/conv_general_dilated | solution.py:22
  24.8 6.3 %copy.167 = bf16[64,64,2,8,13]{0,3,2,4,1:T(8,128)(2,1)} copy(bf16[64,64,2,8,13]{1,0,4,3,2:T(8,128)(2,1)} %fusion.12) | data formatting | bytes 3407872 | tf_op jit(solution)/shard_map/conv_general_dilated | solution.py:22
  32.4 4.8 %fusion.27 = f32[32,16,5,64]{3,1,2,0:T(8,128)S(1)} fusion(bf16[64,64,4,4]{1,0,3,2:T(8,128)(2,1)S(1)} %copy-done.11, bf16[64,64,2,8,13]{0,3,2,4,1:T(8,128)(2,1)} %copy.167, f32[64]{0:T(128)S(1)} %fusion.52, pred[16,5]{0,1:T(8,128)(4,1)S(1)} %copy-done.16), kind=kOutput, calls=%fused_computation.39 | convolution fusion | flops 330629120 | bytes 2490704 | tf_op jit(solution)/shard_map/conv_general_dilated | solution.py:22
  38.3 1.7 convolution_convert_fusion.1
  40.2 1.0 copy.173
  41.4 1.2 iota_compare_fusion.9
  43.4 3.6 %fusion.58 = (bf16[64,64,2,8,9]{1,0,4,3,2:T(8,128)(2,1)}, bf16[64,64,2,8,9]{1,0,4,3,2:T(8,128)(2,1)}) fusion(bf16[64,64,2,8,10]{1,0,4,3,2:T(8,128)(2,1)S(1)} %bitcast.70), kind=kLoop, calls=%fused_computation.97 | loop fusion | bytes 4718592 | tf_op jit(solution)/shard_map/reshape;squeeze | solution.py:80
  49.8 4.2 %fusion.15 = (bf16[64,64,2,8,10]{1,0,4,3,2:T(8,128)(2,1)}, bf16[64,64,2,8,10]{1,0,4,3,2:T(8,128)(2,1)S(1)}) fusion(bf16[64,64,2,7,1]{1,0,4,3,2:T(8,128)(2,1)} %get-tuple-element.10, bf16[64,64,2,8,9]{1,0,4,3,2:T(8,128)(2,1)} %get-tuple-element.8, bf16[64,64,2,7,1]{1,0,4,3,2:T(8,128)(2,1)} %get-tuple-element.12, bf16[64,64,2,8,9]{1,0,4,3,2:T(8,128)(2,1)} %get-tuple-element.9), kind=kLoop, calls=%fused_computation.22 | loop fusion | flops 7864320 | bytes 5210112 | tf_op jit(solution)/shard_map/reshape;squeeze | solution.py:80
  55.7 2.3 %fusion.17 = bf16[64,64,2,8,10]{1,0,4,3,2:T(8,128)(2,1)} fusion(bf16[64,64,2,7,1]{1,0,4,3,2:T(8,128)(2,1)S(1)} %get-tuple-element.11, bf16[64,64,2,8,9]{1,0,4,3,2:T(8,128)(2,1)S(1)} %slice.38), kind=kLoop, calls=%fused_computation.24 | loop fusion | flops 3932160 | bytes 2605056 | tf_op jit(solution)/shard_map/reshape;squeeze | solution.py:80
  58.1 4.6 %copy.187 = bf16[64,64,2,8,10]{0,3,2,4,1:T(8,128)(2,1)} copy(bf16[64,64,2,8,10]{1,0,4,3,2:T(8,128)(2,1)} %copy-done.2) | data formatting | bytes 2621440 | tf_op jit(solution)/shard_map/reshape;squeeze | solution.py:80
  63.6 2.9 %copy.189 = bf16[64,64,16,10,1]{0,2,4,3,1:T(8,128)(2,1)} copy(bf16[64,64,16,10,1]{1,0,3,2,4:T(8,128)(2,1)S(1)} %bitcast.71) | data formatting | bytes 2621440 | tf_op jit(solution)/shard_map/reshape;squeeze | solution.py:80
  66.5 4.8 %copy.185 = bf16[64,64,2,8,10]{0,3,2,4,1:T(8,128)(2,1)} copy(bf16[64,64,2,8,10]{1,0,4,3,2:T(8,128)(2,1)} %get-tuple-element.21) | data formatting | bytes 2621440 | tf_op jit(solution)/shard_map/reshape;squeeze | solution.py:80
  71.3 3.0 %copy.188 = bf16[64,64,2,8,10]{0,3,2,4,1:T(8,128)(2,1)} copy(bf16[64,64,2,8,10]{1,0,4,3,2:T(8,128)(2,1)S(1)} %copy-done.3) | data formatting | bytes 2621440 | tf_op jit(solution)/shard_map/reshape;squeeze | solution.py:80
  75.5 5.1 %all-gather = bf16[2,2,1024]{2,1,0:T(2,128)(2,1)S(1)} all-gather(bf16[1,2,1024]{2,1,0:T(2,128)(2,1)S(1)} %bitcast.91), channel_id=1, replica_groups=mesh['scene'=16,'tile'=2] {'tile'}, dimensions={0}, use_global_device_ids=true | all-gather | bytes 12288 | tf_op jit(solution)/shard_map/all_gather | solution.py:97
  81.4 1.2 copy.174
  82.6 8.2 %all_gather.7 = bf16[4,64,1024]{2,1,0:T(8,128)(2,1)S(1)} all-gather(bf16[2,64,1024]{2,1,0:T(8,128)(2,1)S(1)} %copy.174), channel_id=1, replica_groups=mesh['scene'=16,'tile'=2] {'tile'}, dimensions={0}, use_global_device_ids=true | all-gather | bytes 786432 | tf_op jit(solution)/shard_map/all_gather | solution.py:96
  92.6 3.1 %fusion.49 = f32[64,64,3,3]{0,1,3,2:T(8,128)S(1)} fusion(bf16[32,2,32,64]{3,0,2,1:T(8,128)(2,1)S(1)} %slice.40, bf16[2,64,32,32]{1,3,2,0:T(8,128)(2,1)S(1)} %multiply_convert_fusion.1), kind=kOutput, calls=%fused_computation.66 | convolution fusion | flops 138674176 | bytes 671744 | tf_op jit(solution)/shard_map/conv_general_dilated | solution.py:22
  97.3 1.5 convert_select_fusion
  100.2 4.3 %convolution_convert_fusion = bf16[64,16,8,64]{3,1,2,0:T(8,128)(2,1)} fusion(bf16[64,64,4,4]{1,0,3,2:T(8,128)(2,1)S(1)} %copy-done.12, bf16[32,2,8,6,64]{4,0,3,2,1:T(8,128)(2,1)S(1)} %fusion.43), kind=kOutput, calls=%fused_computation.31 | convolution fusion | flops 264765440 | bytes 1572864 | tf_op jit(solution)/shard_map/conv_general_dilated | solution.py:22
  104.9 5.0 %fusion = f32[64,64,4,4,1]{0,1,3,4,2:T(8,128)S(1)} fusion(bf16[64,64,16,10,1]{0,2,4,3,1:T(8,128)(2,1)S(1)} %bitcast.84, bf16[64,64,16,10,1]{0,2,4,3,1:T(8,128)(2,1)S(1)} %bitcast.82, bf16[64,64,16,10,1]{0,2,4,3,1:T(8,128)(2,1)S(1)} %copy-done.5, bf16[64,64,16,10,1]{0,2,4,3,1:T(8,128)(2,1)S(1)} %bitcast.83, bf16[32,16,5,64]{3,1,2,0:T(8,128)(2,1)S(1)} %get-tuple-element.19), kind=kOutput, calls=%fused_computation.4 | convolution fusion | flops 351272960 | bytes 5832704 | tf_op jit(solution)/shard_map/conv_general_dilated | solution.py:22
  110.5 1.0 bitcast_select_fusion
  111.6 2.1 copy.182
  113.8 2.9 %copy.183 = bf16[2,64,64,64]{3,2,1,0:T(8,128)(2,1)} copy(bf16[2,64,64,64]{1,3,0,2:T(8,128)(2,1)S(1)} %bitcast.74) | data formatting | bytes 2097152 | tf_op jit(solution)/shard_map/convert_element_type | solution.py:137
  116.7 4.2 %broadcast_in_dim_reshape.3 = bf16[1,2,64,4096]{3,2,1,0:T(8,128)(2,1)} reshape(bf16[2,64,64,64]{3,2,1,0:T(8,128)(2,1)} %copy.183) | data formatting | bytes 2097152 | tf_op jit(solution)/shard_map/broadcast_in_dim;reshape | solution.py:166
  120.9 40.9 %all-reduce.1 = f32[32,64]{1,0:T(8,128)S(1)} all-reduce(f32[32,64]{1,0:T(8,128)S(1)} %broadcast_select_fusion), channel_id=3, replica_groups=mesh['scene'=16,'tile'=2] {'scene','tile'}, use_global_device_ids=true, to_apply=%region_4.6.clone | all-reduce | flops 2048 | bytes 16384
  162.4 43.3 %all-reduce.4.cloned.1.call-done = f32[128,1600]{1,0:T(8,128)} async-done(((f32[128,1600]{1,0:T(8,128)}), f32[128,1600]{1,0:T(8,128)}) %all-reduce.4.cloned.1.call-update) | async-done | bytes 819216
  206.5 9.3 %psum.7 = f32[8,1600]{1,0:T(8,128)} all-reduce(f32[8,1600]{1,0:T(8,128)S(1)} %constant_dynamic-slice_fusion.4), channel_id=1, replica_groups=mesh['scene'=16,'tile'=2] {'tile'}, use_global_device_ids=true, to_apply=%region_2.4 | all-reduce | flops 12800 | bytes 102400 | tf_op jit(solution)/shard_map/psum | solution.py:154
  (108 shorter events, 18.9 us)
Async XLA Ops:
  7.2 5.1 %copy-start = (bf16[2,64,1024]{2,1,0:T(8,128)(2,1)S(1)}, bf16[2,64,1024]{2,1,0:T(8,128)(2,1)}, u32[]{:S(2)}) copy-start(bf16[2,64,1024]{2,1,0:T(8,128)(2,1)} %param.11) | copy-start | bytes 786436
  7.2 6.3 %copy-start.10 = (bf16[1,2,64,4096]{3,2,1,0:T(8,128)(2,1)S(1)}, bf16[1,2,64,4096]{3,2,1,0:T(8,128)(2,1)}, u32[]{:S(2)}) copy-start(bf16[1,2,64,4096]{3,2,1,0:T(8,128)(2,1)} %param.10) | copy-start | bytes 3145732
  7.2 198.5 %all-reduce.4.cloned.1.call-start = ((), (), s32[]{:S(2)}) async-start(), calls=%async_computation | async-start | bytes 1703936
  7.2 68.3 %collective-permute-start = (bf16[2,1024]{1,0:T(2,128)(2,1)}, bf16[2,1024]{1,0:T(2,128)(2,1)S(1)}, u32[]{:S(2)}, u32[]{:S(2)}) collective-permute-start(bf16[2,1024]{1,0:T(2,128)(2,1)} %bitcast.90), channel_id=1, source_target_pairs={{0,2},{2,0},{4,6},{6,4},{8,10},{10,8},{12,14},{14,12},{16,18},{18,... | collective-permute-start | bytes 12296 | tf_op jit(solution)/shard_map/ppermute | solution.py:10
  24.8 7.6 %copy-start.11 = (bf16[64,64,4,4]{1,0,3,2:T(8,128)(2,1)S(1)}, bf16[64,64,4,4]{1,0,3,2:T(8,128)(2,1)}, u32[]{:S(2)}) copy-start(bf16[64,64,4,4]{1,0,3,2:T(8,128)(2,1)} %copy.169) | copy-start | bytes 393220
  24.8 7.6 %copy-start.16 = (pred[16,5]{0,1:T(8,128)(4,1)S(1)}, pred[16,5]{0,1:T(8,128)(4,1)}, u32[]{:S(2)}) copy-start(pred[16,5]{0,1:T(8,128)(4,1)} %constant.130) | copy-start | bytes 244
  37.2 2.8 %copy-start.8 = (f32[32,16,5,64]{3,1,2,0:T(8,128)}, f32[32,16,5,64]{3,1,2,0:T(8,128)S(1)}, u32[]{:S(2)}) copy-start(f32[32,16,5,64]{3,1,2,0:T(8,128)S(1)} %fusion.27) | copy-start | bytes 1966084
  37.2 1.1 copy-start.13
  41.2 40.2 %collective-permute-start.1 = (bf16[2,64,1024]{1,2,0:T(8,128)(2,1)}, bf16[2,64,1024]{1,2,0:T(8,128)(2,1)}, u32[]{:S(2)}, u32[]{:S(2)}) collective-permute-start(bf16[2,64,1024]{1,2,0:T(8,128)(2,1)} %bitcast.13), channel_id=1, source_target_pairs={{0,2},{2,0},{4,6},{6,4},{8,10},{10,8},{12,14},{14,12},{16,18},{18,... | collective-permute-start | bytes 786440 | tf_op jit(solution)/shard_map/ppermute | solution.py:10
  43.3 3.6 %copy-start.20 = (s32[8]{0:T(128)S(1)}, s32[8]{0:T(128)}, u32[]{:S(2)}) copy-start(s32[8]{0:T(128)} %param.16) | copy-start | bytes 100
  43.3 4.9 %copy-start.17 = (s32[8,4]{0,1:T(4,128)S(1)}, s32[8,4]{0,1:T(4,128)}, u32[]{:S(2)}) copy-start(s32[8,4]{0,1:T(4,128)} %param.15) | copy-start | bytes 388
  54.0 1.6 copy-start.2
  55.7 2.3 %copy-start.15 = (bf16[1,2,1024]{2,1,0:T(2,128)(2,1)S(1)}, bf16[1,2,1024]{2,1,0:T(2,128)(2,1)}, u32[]{:S(2)}) copy-start(bf16[1,2,1024]{2,1,0:T(2,128)(2,1)} %param.14) | copy-start | bytes 12292
  66.5 4.8 %copy-start.3 = (bf16[64,64,2,8,10]{1,0,4,3,2:T(8,128)(2,1)S(1)}, bf16[64,64,2,8,10]{1,0,4,3,2:T(8,128)(2,1)}, u32[]{:S(2)}) copy-start(bf16[64,64,2,8,10]{1,0,4,3,2:T(8,128)(2,1)} %fusion.17) | copy-start | bytes 3932164
  71.3 3.0 %copy-start.21 = (u32[32]{0:T(128)S(1)}, u32[32]{0:T(128)}, u32[]{:S(2)}) copy-start(u32[32]{0:T(128)} %constant.138) | copy-start | bytes 388
  96.0 1.3 copy-start.9
  96.0 1.3 copy-start.14
  99.2 1.0 copy-start.12
  100.2 4.3 %copy-start.4 = (bf16[64,64,2,8,10]{0,3,2,4,1:T(8,128)(2,1)S(1)}, bf16[64,64,2,8,10]{0,3,2,4,1:T(8,128)(2,1)}, u32[]{:S(2)}) copy-start(bf16[64,64,2,8,10]{0,3,2,4,1:T(8,128)(2,1)} %copy.187) | copy-start | bytes 3932164
  100.2 4.3 %copy-start.5 = (bf16[64,64,16,10,1]{0,2,4,3,1:T(8,128)(2,1)S(1)}, bf16[64,64,16,10,1]{0,2,4,3,1:T(8,128)(2,1)}, u32[]{:S(2)}) copy-start(bf16[64,64,16,10,1]{0,2,4,3,1:T(8,128)(2,1)} %copy.189) | copy-start | bytes 3932164
  100.2 4.3 %copy-start.6 = (bf16[64,64,2,8,10]{0,3,2,4,1:T(8,128)(2,1)S(1)}, bf16[64,64,2,8,10]{0,3,2,4,1:T(8,128)(2,1)}, u32[]{:S(2)}) copy-start(bf16[64,64,2,8,10]{0,3,2,4,1:T(8,128)(2,1)} %copy.185) | copy-start | bytes 3932164
  100.2 4.7 %copy-start.7 = (bf16[64,64,2,8,10]{0,3,2,4,1:T(8,128)(2,1)S(1)}, bf16[64,64,2,8,10]{0,3,2,4,1:T(8,128)(2,1)}, u32[]{:S(2)}) copy-start(bf16[64,64,2,8,10]{0,3,2,4,1:T(8,128)(2,1)} %copy.188) | copy-start | bytes 3932164
  109.9 0.7 copy-start.18
  113.7 102.0 %copy-start.1 = (bf16[2,64,1024]{2,1,0:T(8,128)(2,1)S(1)}, bf16[2,64,1024]{2,1,0:T(8,128)(2,1)}, u32[]{:S(2)}) copy-start(bf16[2,64,1024]{2,1,0:T(8,128)(2,1)} %param.11) | copy-start | bytes 786436
  116.7 4.2 %copy-start.19 = (pred[32]{0:T(512)(128)(4,1)S(1)}, pred[32]{0:T(512)(128)(4,1)}, u32[]{:S(2)}) copy-start(pred[32]{0:T(512)(128)(4,1)} %iota_compare_fusion.9) | copy-start | bytes 100
Sparse Core Ops, SparseCore 0:
  111.7 93.9 all-reduce.3
where the time goes:
time: 223 us
  blocking collectives  63.5 us (28%)
  local copies, waits for them, and re-layouts  63.3 us (28%)
  waiting for transfers between devices  43.3 us (19%)
  matrix products  20.3 us (9%)
  between operations  17.7 us (8%)
  other arithmetic  13.8 us (6%)
    unnamed x2, waiting for transfers between devices  43.3 us
    unnamed x1, blocking collectives  40.9 us
    another operation x9, local copies, waits for them, and re-layouts, local(): feature_grid = features.reshape(patches, channels, grid_side, grid_side)  26.1 us
    conv_general_dilated x6, matrix products, apply_convolution(): lax.conv_general_dilated(left_operand, right_operand, window_strides, bor...  20.3 us
    psum x1, blocking collectives, local(): grad_weights = lax.psum(partial_rows, 'tile')  9.26 us
    unnamed x51, local copies, waits for them, and re-layouts  8.39 us
    all_gather x1, blocking collectives, local(): lax.all_gather(swapped_out, 'tile', axis=0, tiled=True)  8.16 us
    conv_general_dilated x5, local copies, waits for them, and re-layouts, apply_convolution(): lax.conv_general_dilated(left_operand, right_operand, window_strides, bor...  6.89 us
  transfers between devices with their start and end apart: 3, of which 1 were waited for; matrix products, arithmetic and copies ran while one was open for 33% of the time, Pallas kernels for 0%

commit v1 on v0

v1 whole, which is shorter than its diff:
```python
import functools
import math

import jax
import jax.numpy as jnp
from jax import lax
from jax.experimental import pallas as pl
from jax.experimental.pallas import tpu as pltpu
from jax.sharding import PartitionSpec as P

CH = 64
ROW_TAPS = 4
DIL_TAPS = 9
BLOCKS = 14
SHIFTS = [(dr, dc) for dr in (-1, 0, 1) for dc in (-1, 0, 1)]
F32 = jnp.float32
BF16 = jnp.bfloat16
VMEM_LIMIT = 40 * 1024 * 1024


def shift_index(dr, dc):
    return (dr + 1) * 3 + dc + 1


def dot(a, b):
    return lax.dot_general(a, b, (((1,), (0,)), ((), ())), preferred_element_type=F32)


def dot_nt(a, b):
    return lax.dot_general(a, b, (((1,), (1,)), ((), ())), preferred_element_type=F32)


def shifted_masks(side, reach):
    cell = lax.broadcasted_iota(jnp.int32, (1, side * side), 1)
    row, col = cell // side, cell % side
    masks = {}
    for dr, dc in SHIFTS:
        ok = (
            (row + dr * reach >= 0)
            & (row + dr * reach < side)
            & (col + dc * reach >= 0)
            & (col + dc * reach < side)
        )
        masks[dr, dc] = ok.astype(F32).astype(BF16)
    return masks


def shifted(x, dr, dc, side, reach, masks):
    if dr == 0 and dc == 0:
        return x
    cells = side * side
    return pltpu.roll(x, (-(dr * side + dc) * reach) % cells, 1) * masks[dr, dc]


def phase_matrix(side, transposed):
    size = 16 * side
    dims = (size, size)
    source = lax.broadcasted_iota(jnp.int32, dims, 1 if transposed else 0)
    target = lax.broadcasted_iota(jnp.int32, dims, 0 if transposed else 1)
    phase, cell = target // (4 * side), target % (4 * side)
    row, col = cell // side, cell % side
    wanted = (2 * row + phase // 2) * (2 * side) + 2 * col + phase % 2
    return jnp.where(source == wanted, 1.0, 0.0).astype(BF16)


TAP_LINES = {0: (1, -1), 1: (0, 0), 2: (1, 0), 3: (0, 1)}


def tap_matrices(weight, taps, scratch):
    wide = weight.astype(F32)
    scratch[0 : CH * taps, 0:CH] = wide.T
    return [scratch[pl.ds(tap, CH, stride=taps), 0:CH] for tap in range(taps)]


def forward_kernel(
    owner_ref, x_ref, ws_ref, wd_ref, bias_ref, cot_ref, ph_ref, pre_ref, act_ref, send_ref, wscr, im_scr
):
    patches, side = x_ref.shape[0], math.isqrt(x_ref.shape[2]) // 2
    cells = side * side
    scene = lax.axis_index("scene")
    branch = scene % 2
    split = phase_matrix(side, False)
    run = 16 * side
    runs = x_ref.shape[2] // run
    mats = tap_matrices(ws_ref[branch], 16, wscr)
    w_strided = jnp.concatenate(mats, axis=0).T.astype(BF16)
    mats = tap_matrices(wd_ref[branch], 9, wscr)
    w_dilated = jnp.concatenate(mats, axis=0).T.astype(BF16)
    bias_row = bias_ref[pl.ds(owner_ref[scene], 1), :]
    bias_col = jnp.broadcast_to(bias_row, (8, CH)).T[:, 0:1]
    near = shifted_masks(side, 1)
    far = shifted_masks(side, 2)
    for p in range(patches):
        for q in range(runs):
            part = dot(x_ref[p, :, q * run : (q + 1) * run], split).astype(BF16)
            for phase in range(4):
                ph_ref[p, phase * CH : (phase + 1) * CH, q * 4 * side : (q + 1) * 4 * side] = part[
                    :, phase * 4 * side : (phase + 1) * 4 * side
                ]
        for rt in range(4):
            for ct in range(4):
                (pr, dr), (pc, dc) = TAP_LINES[rt], TAP_LINES[ct]
                phase, tap = pr * 2 + pc, rt * 4 + ct
                im_scr[tap * CH : (tap + 1) * CH, :] = shifted(
                    ph_ref[p, phase * CH : (phase + 1) * CH, :], dr, dc, side, 1, near
                )
        pre = dot(w_strided, im_scr[...]) + bias_col
        pre_ref[p] = pre
        act = (pre * (1.0 / (1.0 + jnp.exp(-pre)))).astype(BF16)
        act_ref[p] = act
        for tap, (dr, dc) in enumerate(SHIFTS):
            im_scr[tap * CH : (tap + 1) * CH, :] = shifted(act, dr, dc, side, 2, far)
        out = dot(w_dilated, im_scr[0 : DIL_TAPS * CH, :])
        send_ref[p * CH : (p + 1) * CH, :] = out.astype(BF16)
    cot = cot_ref[...].astype(F32)
    cot = jnp.concatenate([cot, jnp.zeros((16 - patches, cells), F32)], axis=0)
    send_ref[patches * CH :, :] = cot.astype(BF16)


def prepare_kernel(pre_ref, ws_ref, wd_ref, slope_ref, wf_ref, wt_ref, wscr):
    branch = lax.axis_index("scene") % 2
    for p in range(pre_ref.shape[0]):
        pre = pre_ref[p]
        gate = 1.0 / (1.0 + jnp.exp(-pre))
        slope_ref[p] = gate * (1.0 + pre * (1.0 - gate))
    mats = tap_matrices(ws_ref[branch], 16, wscr)
    blocks = {}
    for rt in range(4):
        for ct in range(4):
            (pr, dr), (pc, dc) = TAP_LINES[rt], TAP_LINES[ct]
            blocks[pr * 2 + pc, shift_index(-dr, -dc)] = mats[rt * 4 + ct]
    zero = jnp.zeros((CH, CH), F32)
    for phase in range(4):
        row = [blocks.get((phase, s), zero) for s in range(9)]
        wf_ref[phase * CH : (phase + 1) * CH, :] = jnp.concatenate(row, axis=1).astype(BF16)
    mats = tap_matrices(wd_ref[branch], 9, wscr)
    wt_ref[...] = jnp.concatenate(mats[::-1], axis=1).astype(BF16)


def backward_kernel(
    pairing_ref, valid_ref, near_ref, far_ref, cot_ref, act_ref, slope_ref, ph_ref, wt_ref,
    pre_b_ref, *refs, chunked, weight_scale, bias_scale,
):
    if chunked:
        keep_ref, give_ref, shift_scr, dil_scr, grad_acc, grad_scr = refs
    else:
        grad_scr, shift_scr, dil_scr, grad_acc = refs
    patches, side = act_ref.shape[0], math.isqrt(act_ref.shape[2])
    total = pairing_ref.shape[1]
    scene, tile = lax.axis_index("scene"), lax.axis_index("tile")
    branch, pair = scene % 2, scene // 2
    first = tile * patches
    near, far = shifted_masks(side, 1), shifted_masks(side, 2)
    bias = jnp.zeros((CH, 1), F32)
    for p in range(patches):
        position = first + p
        direct = pairing_ref[pair, position]
        inverse = jnp.int32(0)
        for i in range(total):
            inverse = inverse + jnp.where(pairing_ref[pair, i] == position, i, 0)
        match = jnp.where(branch == 0, direct, inverse)
        local, here = match % patches, match // patches == tile
        start = pl.multiple_of(local * CH, CH)
        partner = jnp.where(here, near_ref[pl.ds(start, CH), :], far_ref[pl.ds(start, CH), :])
        cots_near = near_ref[patches * CH :, :].astype(F32)
        cots_far = far_ref[patches * CH :, :].astype(F32)
        cots = jnp.where(here, cots_near, cots_far)
        pick = lax.broadcasted_iota(jnp.int32, cots.shape, 0) == local
        partner_cot = jnp.sum(jnp.where(pick, cots, 0.0), axis=0, keepdims=True)
        live = jnp.where(position < valid_ref[pair], 1.0, 0.0)
        signal = (cot_ref[p : p + 1, :].astype(F32) + partner_cot) * live
        out_grad = (signal * partner.astype(F32)).astype(BF16)
        for tap, (dr, dc) in enumerate(SHIFTS):
            shift_scr[tap * CH : (tap + 1) * CH, :] = shifted(out_grad, dr, dc, side, 2, far)
        act_grad = dot(wt_ref[...], shift_scr[...])
        act = act_ref[p]
        dil = dot_nt(shift_scr[...], jnp.concatenate([act, act], axis=0))
        pre_grad = act_grad * slope_ref[p]
        bias = bias + jnp.sum(pre_grad, axis=1, keepdims=True)
        pre_b = pre_grad.astype(BF16)
        pre_b_ref[p] = pre_b
        for s, (dr, dc) in enumerate(SHIFTS):
            shift_scr[s * CH : (s + 1) * CH, :] = shifted(pre_b, dr, dc, side, 1, near)
        strided = dot_nt(shift_scr[...], ph_ref[p])
        if p == 0:
            dil_scr[...] = dil
            grad_acc[...] = strided
        else:
            dil_scr[...] += dil
            grad_acc[...] += strided
    lower = lax.broadcasted_iota(jnp.int32, (CH, 2 * CH), 1) < CH

    def strided_piece(pr, shift, low):
        return grad_acc[shift * CH : (shift + 1) * CH, pr * 2 * CH : (pr + 1) * 2 * CH]

    for rt in range(4):
        pr, dr = TAP_LINES[rt]
        for k in range(2):
            low_dc, high_dc = (0, 0) if k == 0 else (1, -1)
            low = strided_piece(pr, shift_index(-dr, -low_dc), True)
            high = strided_piece(pr, shift_index(-dr, -high_dc), False)
            grad_scr[rt * 2 + k] = jnp.where(lower, low, high) * weight_scale
    for j in range(5):
        low = dil_scr[(8 - 2 * j) * CH : (9 - 2 * j) * CH, :]
        high = dil_scr[(7 - 2 * j) * CH : (8 - 2 * j) * CH, :] if j < 4 else jnp.zeros_like(low)
        grad_scr[8 + j] = jnp.where(lower, low, high) * weight_scale
    bias_wide = jnp.concatenate([jnp.broadcast_to(bias, (CH, 8)).T, jnp.zeros((8, CH), F32)], axis=1)
    top = lax.broadcasted_iota(jnp.int32, (8, 2 * CH), 0) == 0
    bias_rows = jnp.where(top, bias_wide * bias_scale, 0.0)
    if not chunked:
        grad_scr[BLOCKS - 1] = jnp.concatenate([bias_rows] * 8, axis=0)
        return
    for ref, core in ((keep_ref, branch), (give_ref, 1 - branch)):
        for half in range(2):
            pieces = []
            for block in range(BLOCKS - 1):
                for y in range(2):
                    row = pl.multiple_of((half * 4 + y * 2 + core) * 8, 8)
                    pieces.append(grad_scr[block, pl.ds(row, 8), :])
            pieces += [bias_rows, jnp.zeros((8, 2 * CH), F32)]
            ref[half] = jnp.concatenate(pieces, axis=0).astype(BF16)


def spread_kernel(owner_ref, keep_ref, got_ref, own_ref, one_ref, two_ref, three_ref, *, bias_rows):
    scene = lax.axis_index("scene")
    core, z = scene % 2, scene // 4
    rows = keep_ref.shape[1]
    bias_at = rows - 16
    mine = keep_ref[0, bias_at:, :].astype(F32)[0:1, :]
    theirs = got_ref[0, bias_at:, :].astype(F32)[0:1, :]
    index = lax.broadcasted_iota(jnp.int32, (16, 2 * CH), 0)
    for distance, ref in ((0, own_ref), (1, one_ref), (2, two_ref), (3, three_ref)):
        target = z ^ distance
        kept = target // 2 == core
        ref[...] = jnp.where(kept, keep_ref[target % 2], got_ref[target % 2])
        bias = jnp.zeros((16, 2 * CH), F32)
        for source, vector in ((scene, mine), (scene ^ 1, theirs)):
            owner = owner_ref[source]
            place = owner // (2 * bias_rows)
            row = (place // 2 % 2) * 8 + owner % (2 * bias_rows)
            hit = (place % 2 == core) & (place // 4 == target)
            bias = bias + jnp.where(index == jnp.where(hit, row, -1), vector, 0.0)
        ref[bias_at:, :] = bias.astype(BF16)


def join_kernel(own_ref, a_ref, b_ref, c_ref, keep_ref, stay_ref, cross_ref, scr):
    y = lax.axis_index("scene") // 2 % 2
    scr[...] = (own_ref[...].astype(F32) + a_ref[...].astype(F32)) + (
        b_ref[...].astype(F32) + c_ref[...].astype(F32)
    )

    def chunk(which):
        return jnp.concatenate(
            [scr[pl.ds(pl.multiple_of(block * 16 + which * 8, 8), 8), :] for block in range(BLOCKS)], axis=0
        )

    kept = chunk(y)
    keep_ref[...] = kept
    stay_ref[...] = kept.astype(BF16)
    cross_ref[...] = chunk(1 - y).astype(BF16)


def finish_kernel(own_ref, a_ref, b_ref, c_ref, weights_ref, bias_ref, strided_scr, dilated_scr):
    tile = lax.axis_index("tile")
    total = (own_ref[...] + a_ref[...].astype(F32)) + (b_ref[...].astype(F32) + c_ref[...].astype(F32))
    bias = total[(BLOCKS - 1) * 8 :, :]
    index = lax.broadcasted_iota(jnp.int32, bias.shape, 0)
    bias_ref[...] = jnp.sum(jnp.where(index == tile, bias, 0.0), axis=0, keepdims=True)[:, 0:CH]
    width = 2 * CH
    turned = jnp.concatenate([total, jnp.zeros((width - BLOCKS * 8, width), F32)], axis=0).T
    for block in range(BLOCKS - 1):
        lined = turned if block == 0 else pltpu.roll(turned, width - block * 8, 1)
        for half in range(2):
            piece = lined[half * CH : (half + 1) * CH, :]
            if block < 8:
                tap = block // 2 * 4 + ((1, 2), (3, 0))[block % 2][half]
                strided_scr[pl.ds(tap, CH, stride=16), :] = piece
            elif (block - 8) * 2 + half < DIL_TAPS:
                dilated_scr[pl.ds((block - 8) * 2 + half, CH, stride=DIL_TAPS), :] = piece
    weights_ref[:, 0 : 16 * CH] = strided_scr[...].T[0:8, :]
    weights_ref[:, 16 * CH :] = dilated_scr[...].T[0:8, :]


def feature_kernel(pre_b_ref, wf_ref, out_ref, shift_scr):
    patches, side = pre_b_ref.shape[0], math.isqrt(pre_b_ref.shape[2])
    near = shifted_masks(side, 1)
    merge = phase_matrix(side, True)
    run = 16 * side
    for p in range(patches):
        pre_b = pre_b_ref[p]
        for s, (dr, dc) in enumerate(SHIFTS):
            shift_scr[s * CH : (s + 1) * CH, :] = shifted(pre_b, dr, dc, side, 1, near)
        phases = dot(wf_ref[...], shift_scr[...]).astype(BF16)
        for q in range(out_ref.shape[2] // run):
            part = jnp.concatenate(
                [
                    phases[phase * CH : (phase + 1) * CH, q * 4 * side : (q + 1) * 4 * side]
                    for phase in range(4)
                ],
                axis=1,
            )
            out_ref[p, :, q * run : (q + 1) * run] = dot(part, merge).astype(BF16)


def call(kernel, outs, ins, scratch, *args, flops=0):
    vmem, smem = pl.BlockSpec(memory_space=pltpu.VMEM), pl.BlockSpec(memory_space=pltpu.SMEM)
    return pl.pallas_call(
        kernel,
        out_shape=[jax.ShapeDtypeStruct(shape, kind) for shape, kind in outs],
        in_specs=[smem if space == "s" else vmem for space in ins],
        out_specs=[vmem] * len(outs),
        scratch_shapes=[pltpu.VMEM(shape, kind) for shape, kind in scratch],
        compiler_params=pltpu.CompilerParams(vmem_limit_bytes=VMEM_LIMIT),
        cost_estimate=pl.CostEstimate(flops=flops, bytes_accessed=1 << 20, transcendentals=0),
    )(*args)


def scene_xor(x, distance):
    return lax.ppermute(x, "scene", [(i, i ^ distance) for i in range(lax.axis_size("scene"))])


def device_xor(x, scene_distance, tile_distance):
    tiles, scenes = lax.axis_size("tile"), lax.axis_size("scene")
    pairs = [
        (s * tiles + t, (s ^ scene_distance) * tiles + (t ^ tile_distance))
        for s in range(scenes)
        for t in range(tiles)
    ]
    return lax.ppermute(x, ("scene", "tile"), pairs)


def reduce_anywhere(blocks, tile_owner, bias_rows):
    channels = blocks.shape[1]
    scene = lax.axis_index("scene")
    scenes, tiles = lax.axis_size("scene"), lax.axis_size("tile")
    halves = blocks.reshape(BLOCKS, channels, 2, channels)
    strided, dilated = [None] * 16, []
    for block in range(8):
        for half in range(2):
            strided[block // 2 * 4 + ((1, 2), (3, 0))[block % 2][half]] = halves[block, :, half]
    for tap in range(DIL_TAPS):
        dilated.append(halves[8 + tap // 2, :, tap % 2])
    row = jnp.concatenate(
        [
            jnp.stack(strided, axis=-1).reshape(channels, 16 * channels),
            jnp.stack(dilated, axis=-1).reshape(channels, DIL_TAPS * channels),
        ],
        axis=1,
    )
    hit = jnp.arange(2, dtype=jnp.int32)[:, None, None] == scene % 2
    term = jnp.where(hit, row[None], 0.0).reshape(2 * channels, 25 * channels)
    weights = lax.psum(lax.psum_scatter(term, "scene", scatter_dimension=0, tiled=True), "tile")
    tile_id = lax.dynamic_index_in_dim(tile_owner, scene, 0, keepdims=False)
    owned = jnp.arange(scenes * tiles * bias_rows, dtype=jnp.int32) == tile_id
    bias = jnp.where(owned[:, None], halves[BLOCKS - 1, 0, 0][None, :], 0.0)
    return weights, lax.psum_scatter(bias, ("scene", "tile"), scatter_dimension=0, tiled=True)


def local(
    features_in,
    strided_weights,
    dilated_weights,
    tile_bias,
    cost_cotangent,
    footprint_pairing,
    valid_counts,
    tile_owner,
):
    features, own_cot = features_in[0], cost_cotangent[0]
    patches, channels, cells_in = features.shape
    cells = own_cot.shape[1]
    scenes, tiles = lax.axis_size("scene"), lax.axis_size("tile")
    weight_scale = 1.0 / math.sqrt(scenes * patches * tiles * cells)
    bias_scale = 1.0 / math.sqrt(patches * tiles * cells)
    bias_rows = tile_bias.shape[0] // (scenes * tiles)
    grid = (patches, channels, cells)
    wscr = ((16 * channels, 2 * channels), F32)
    phases, pre, act, send = call(
        forward_kernel,
        [((patches, 4 * channels, cells), BF16), (grid, F32), (grid, BF16), ((patches * channels + 16, cells), BF16)],
        "svvvvv",
        [wscr, ((16 * channels, cells), BF16)],
        tile_owner, features, strided_weights, dilated_weights, tile_bias, own_cot,
        flops=10**9,
    )
    far = device_xor(send, 1, 1)
    near = scene_xor(send, 1)
    slope, w_feature, w_act = call(
        prepare_kernel,
        [(grid, F32), ((4 * channels, 9 * channels), BF16), ((channels, 9 * channels), BF16)],
        "vvv",
        [wscr],
        pre, strided_weights, dilated_weights,
        flops=10**9,
    )
    chunked = scenes == 16 and tiles == 2 and bias_rows == 1
    block_shape = ((BLOCKS, channels, 128), F32)
    half_shape = ((2, BLOCKS * 16, 128), BF16)
    scratch = [
        ((9 * channels, cells), BF16),
        ((9 * channels, 128), F32),
        ((9 * channels, 4 * channels), F32),
    ]
    pre_b, *grads = call(
        functools.partial(
            backward_kernel, chunked=chunked, weight_scale=weight_scale, bias_scale=bias_scale
        ),
        [(grid, BF16)] + ([half_shape] * 2 if chunked else [block_shape]),
        "ssvvvvvvv",
        scratch + ([block_shape] if chunked else []),
        footprint_pairing, valid_counts, near, far, own_cot, act, slope, phases, w_act,
        flops=10**9,
    )
    if not chunked:
        (feature_grads,) = call(
            feature_kernel,
            [(features.shape, BF16)],
            "vv",
            [((9 * channels, cells), BF16)],
            pre_b, w_feature,
            flops=10**9,
        )
        return (feature_grads[None],) + reduce_anywhere(grads[0], tile_owner, bias_rows)
    keep, give = grads
    got = scene_xor(give, 1)
    own, one, two, three = call(
        functools.partial(spread_kernel, bias_rows=bias_rows),
        [((BLOCKS * 16, 128), BF16)] * 4,
        "svv",
        [],
        tile_owner, keep, got,
    )
    two, three, one = scene_xor(two, 8), scene_xor(three, 12), scene_xor(one, 4)
    (feature_grads,) = call(
        feature_kernel,
        [(features.shape, BF16)],
        "vv",
        [((9 * channels, cells), BF16)],
        pre_b, w_feature,
        flops=10**9,
    )
    kept, stay, cross = call(
        join_kernel,
        [((BLOCKS * 8, 128), F32), ((BLOCKS * 8, 128), BF16), ((BLOCKS * 8, 128), BF16)],
        "vvvv",
        [((BLOCKS * 16, 128), F32)],
        own, one, two, three,
    )
    by_y, by_xy, by_x = device_xor(cross, 2, 0), device_xor(cross, 2, 1), device_xor(stay, 0, 1)
    grad_weights, grad_bias = call(
        finish_kernel,
        [((8, 25 * channels), F32), ((1, channels), F32)],
        "vvvv",
        [((16 * channels, 128), F32), ((9 * channels, 128), F32)],
        kept, by_y, by_xy, by_x,
    )
    return (feature_grads[None], grad_weights, grad_bias)


def solution(mesh):
    return jax.shard_map(
        local,
        mesh=mesh,
        in_specs=(
            P("scene", "tile", None, None),
            P(),
            P(),
            P(),
            P("scene", "tile", None),
            P(),
            P(),
            P(),
        ),
        out_specs=(P("scene", "tile", None, None), P("scene", None), P(("scene", "tile"), None)),
        check_vma=False,
    )
```

time: 223 us -> 45.2 us (0.20)
  blocking collectives: 63.5 us -> 0 us
  local copies, waits for them, and re-layouts: 63.3 us -> 5.89 us
  waiting for transfers between devices: 43.3 us -> 13.6 us
  matrix products: 20.3 us -> 0 us
  between operations: 17.7 us -> 0.71 us
  other arithmetic: 13.8 us -> 0 us
  Pallas kernels: 0 us -> 13.4 us
  starting transfers between devices: 0.71 us -> 11.3 us
    unnamed x2 -> x0, waiting for transfers between devices: 43.3 us -> none
    unnamed x1 -> x0, blocking collectives: 40.9 us -> none
    another operation x10 -> x0, local copies, waits for them, and re-layouts: 30.2 us -> none  [the longest x9 26.1 us: local(): feature_grid = features.reshape(patches, channels, grid_side, grid_side)]
    conv_general_dilated x6 -> x0, matrix products: 20.3 us -> none  [apply_convolution(): lax.conv_general_dilated(left_operand, right_operand, window_strides, bor...]
    ppermute x2 -> x9, waiting for transfers between devices: 0.01 us -> 13.6 us  [the longest x5 6.93 us: scene_xor(): lax.ppermute(x, 'scene', [(i, i ^ distance) for i in range(lax.axis_size(...]
    pallas_call x0 -> x7, Pallas kernels: none -> 13.4 us  [call(): pl.pallas_call(kernel, out_shape=[jax.ShapeDtypeStruct(shape, kind) for s...]
    all_gather x2 -> x0, blocking collectives: 13.3 us -> none  [the longest x1 8.16 us: local(): lax.all_gather(swapped_out, 'tile', axis=0, tiled=True)]
    ppermute x2 -> x9, starting transfers between devices: 0.67 us -> 11.3 us  [the longest x4 6.17 us: device_xor(): return lax.ppermute(x, ('scene', 'tile'), pairs)]
  transfers between devices with their start and end apart: 3 -> 9, of which waited for: 1 -> 4; matrix products, arithmetic and copies ran while one was open for 33% -> 0% of each run, Pallas kernels for 0% -> 9%
where the time goes in v1:
time: 45.2 us; the launch traced here: 44.9 us
  waiting for transfers between devices  13.6 us (30%)
  Pallas kernels  13.4 us (30%)
  starting transfers between devices  11.3 us (25%)
  local copies, waits for them, and re-layouts  5.89 us (13%)
  between operations  0.71 us (2%)
    pallas_call x7, Pallas kernels, call(): pl.pallas_call(kernel, out_shape=[jax.ShapeDtypeStruct(shape, kind) for s...  13.4 us
    ppermute x5, waiting for transfers between devices, scene_xor(): lax.ppermute(x, 'scene', [(i, i ^ distance) for i in range(lax.axis_size(...  6.93 us
    ppermute x4, waiting for transfers between devices, device_xor(): return lax.ppermute(x, ('scene', 'tile'), pairs)  6.65 us
    ppermute x4, starting transfers between devices, device_xor(): return lax.ppermute(x, ('scene', 'tile'), pairs)  6.17 us
    unnamed x23, local copies, waits for them, and re-layouts  5.89 us
    ppermute x5, starting transfers between devices, scene_xor(): lax.ppermute(x, 'scene', [(i, i ^ distance) for i in range(lax.axis_size(...  5.14 us
  transfers between devices with their start and end apart: 9, of which 4 were waited for; matrix products, arithmetic and copies ran while one was open for 0% of the time, Pallas kernels for 9%

profile of v1, /device:TPU:0, one launch (start us, length us, event | category | flops | bytes accessed | tf_op | source)
XLA Modules:
  0.0 44.9 jit_solution(13811119398483564494)
XLA Ops:
  0.6 0.6 %copy-done = s32[16]{0:T(128)S(1)} copy-done((s32[16]{0:T(128)S(1)}, s32[16]{0:T(128)}, u32[]{:S(2)}) %copy-start) | copy-done | bytes 88
  1.3 1.2 %copy-done.1 = bf16[1,2,64,4096]{3,2,1,0:T(8,128)(2,1)S(1)} copy-done((bf16[1,2,64,4096]{3,2,1,0:T(8,128)(2,1)S(1)}, bf16[1,2,64,4096]{3,2,1,0:T(8,128)(2,1)}, u32[]{:S(2)}) %copy-start.1) | copy-done | bytes 1048600
  2.5 0.9 %copy-done.2 = bf16[2,64,1024]{2,1,0:T(8,128)(2,1)S(1)} copy-done((bf16[2,64,1024]{2,1,0:T(8,128)(2,1)S(1)}, bf16[2,64,1024]{2,1,0:T(8,128)(2,1)}, u32[]{:S(2)}) %copy-start.2) | copy-done | bytes 262168
  3.5 0.9 %copy-done.4 = bf16[2,64,576]{2,1,0:T(8,128)(2,1)S(1)} copy-done((bf16[2,64,576]{2,1,0:T(8,128)(2,1)S(1)}, bf16[2,64,576]{2,1,0:T(8,128)(2,1)}, u32[]{:S(2)}) %copy-start.4) | copy-done | bytes 147480
  4.4 0.7 %copy-done.6 = f32[32,64]{1,0:T(8,128)S(1)} copy-done((f32[32,64]{1,0:T(8,128)S(1)}, f32[32,64]{1,0:T(8,128)}, u32[]{:S(2)}) %copy-start.6) | copy-done | bytes 8216
  5.1 0.7 %copy-done.7 = bf16[1,2,1024]{2,1,0:T(2,128)(2,1)S(1)} copy-done((bf16[1,2,1024]{2,1,0:T(2,128)(2,1)S(1)}, bf16[1,2,1024]{2,1,0:T(2,128)(2,1)}, u32[]{:S(2)}) %copy-start.7) | copy-done | bytes 4120
  5.8 4.4 %shard_map.103 = (bf16[2,256,1024]{2,1,0:T(8,128)(2,1)S(1)}, f32[2,64,1024]{2,1,0:T(8,128)S(1)}, bf16[2,64,1024]{2,1,0:T(8,128)(2,1)S(1)}, bf16[144,1024]{1,0:T(8,128)(2,1)S(1)}) custom-call(s32[16]{0:T(128)S(1)} %copy-done, bf16[2,64,4096]{2,1,0:T(8,128)(2,1)S(1)} %bitcast.3, bf16[2,64,1024]{2,1,0:T(8,128)(2,1)S(1)} %copy-done.2, ...), custom_call_target="tpu_custom_call" | custom-call | flops 1000000000 | bytes 1048576 | tf_op jit(solution)/shard_map/pallas_call | solution.py:307
  10.2 0.5 %collective-permute-start = (bf16[144,1024]{1,0:T(8,128)(2,1)S(1)}, bf16[144,1024]{1,0:T(8,128)(2,1)S(1)}, u32[]{:S(2)}, u32[]{:S(2)}) collective-permute-start(bf16[144,1024]{1,0:T(8,128)(2,1)S(1)} %get-tuple-element.22), channel_id=1, source_target_pairs={{0,2},{2,0},{4,6},{6,4},{8,10},{10,8},{12,14},{14,12},{16,18},{18,... | collective-permute-start | bytes 884744 | tf_op jit(solution)/shard_map/ppermute | solution.py:319
  10.7 2.6 %collective-permute-start.1 = (bf16[144,1024]{1,0:T(8,128)(2,1)S(1)}, bf16[144,1024]{1,0:T(8,128)(2,1)S(1)}, u32[]{:S(2)}, u32[]{:S(2)}) collective-permute-start(bf16[144,1024]{1,0:T(8,128)(2,1)S(1)} %get-tuple-element.22), channel_id=1, source_target_pairs={{0,3},{1,2},{2,1},{3,0},{4,7},{5,6},{6,5},{7,4},{8,11},{9,10},{10,... | collective-permute-start | bytes 884744 | tf_op jit(solution)/shard_map/ppermute | solution.py:329
  13.3 0.1 copy.11.pairing_ref
  13.4 0.5 %shard_map.104 = (f32[2,64,1024]{2,1,0:T(8,128)S(1)}, bf16[256,576]{1,0:T(8,128)(2,1)S(1)}, bf16[64,576]{1,0:T(8,128)(2,1)S(1)}) custom-call(f32[2,64,1024]{2,1,0:T(8,128)S(1)} %get-tuple-element.24.pre_ref, bf16[2,64,1024]{2,1,0:T(8,128)(2,1)S(1)} %copy-done.3, bf16[2,64,576]{2,1,0:T(8,128)(2,1)S(1)} %copy-done.5), custom_call_target="tpu_custom_call" | custom-call | flops 1000000000 | bytes 1048576 | tf_op jit(solution)/shard_map/pallas_call | solution.py:307
  14.0 0.0 copy-start.8
  14.0 0.0 collective-permute-done.near_ref
  14.0 6.6 %collective-permute-done.1.far_ref = bf16[144,1024]{1,0:T(8,128)(2,1)S(1)} collective-permute-done((bf16[144,1024]{1,0:T(8,128)(2,1)S(1)}, bf16[144,1024]{1,0:T(8,128)(2,1)S(1)}, u32[]{:S(2)}, u32[]{:S(2)}) %collective-permute-start.1) | collective-permute-done | bytes 294944 | tf_op jit(solution)/shard_map/ppermute | solution.py:329
  20.6 0.7 %copy-done.9 = s32[8]{0:T(128)S(1)} copy-done((s32[8]{0:T(128)S(1)}, s32[8]{0:T(128)}, u32[]{:S(2)}) %copy-start.9) | copy-done | bytes 56
  21.3 2.9 %shard_map.105 = (bf16[2,64,1024]{2,1,0:T(8,128)(2,1)S(1)}, bf16[2,224,128]{2,1,0:T(8,128)(2,1)S(1)}, bf16[2,224,128]{2,1,0:T(8,128)(2,1)S(1)}) custom-call(s32[8,4]{1,0:T(8,128)S(1)} %copy.11.pairing_ref, s32[8]{0:T(128)S(1)} %copy-done.9, bf16[144,1024]{1,0:T(8,128)(2,1)S(1)} %collective-permute-done.near_ref, ...), custom_call_target="tpu_custom_call" | custom-call | flops 1000000000 | bytes 1048576 | tf_op jit(solution)/shard_map/pallas_call | solution.py:307
  24.2 0.2 collective-permute-start.2
  24.3 1.2 %collective-permute-done.2.got_ref = bf16[2,224,128]{2,1,0:T(8,128)(2,1)S(1)} collective-permute-done((bf16[2,224,128]{2,1,0:T(8,128)(2,1)S(1)}, bf16[2,224,128]{2,1,0:T(8,128)(2,1)S(1)}, u32[]{:S(2)}, u32[]{:S(2)}) %collective-permute-start.2) | collective-permute-done | bytes 114720 | tf_op jit(solution)/shard_map/ppermute | solution.py:319
  25.6 0.7 %shard_map.107 = (bf16[224,128]{1,0:T(8,128)(2,1)S(1)}, bf16[224,128]{1,0:T(8,128)(2,1)S(1)}, bf16[224,128]{1,0:T(8,128)(2,1)S(1)}, bf16[224,128]{1,0:T(8,128)(2,1)S(1)}) custom-call(s32[16]{0:T(128)S(1)} %copy-done, bf16[2,224,128]{2,1,0:T(8,128)(2,1)S(1)} %get-tuple-element.30.keep_ref, bf16[2,224,128]{2,1,0:T(8,128)(2,1)S(1)} %collective-permute-done.2.got_ref), custom_call_target="tpu_custom_call" | custom-call | bytes 1048576 | tf_op jit(solution)/shard_map/pallas_call | solution.py:307
  26.3 1.6 %collective-permute-start.3 = (bf16[224,128]{1,0:T(8,128)(2,1)S(1)}, bf16[224,128]{1,0:T(8,128)(2,1)S(1)}, u32[]{:S(2)}, u32[]{:S(2)}) collective-permute-start(bf16[224,128]{1,0:T(8,128)(2,1)S(1)} %get-tuple-element.33), channel_id=1, source_target_pairs={{0,8},{2,10},{4,12},{6,14},{8,0},{10,2},{12,4},{14,6},{16,24},{18,... | collective-permute-start | bytes 172040 | tf_op jit(solution)/shard_map/ppermute | solution.py:319
  27.9 2.6 %collective-permute-start.4 = (bf16[224,128]{1,0:T(8,128)(2,1)S(1)}, bf16[224,128]{1,0:T(8,128)(2,1)S(1)}, u32[]{:S(2)}, u32[]{:S(2)}) collective-permute-start(bf16[224,128]{1,0:T(8,128)(2,1)S(1)} %get-tuple-element.34), channel_id=1, source_target_pairs={{0,16},{2,18},{4,20},{6,22},{8,24},{10,26},{12,28},{14,30},{16,0},... | collective-permute-start | bytes 172040 | tf_op jit(solution)/shard_map/ppermute | solution.py:319
  30.5 0.3 collective-permute-start.5
  30.8 0.0 collective-permute-done.3.a_ref
  30.8 3.7 %collective-permute-done.4.b_ref = bf16[224,128]{1,0:T(8,128)(2,1)S(1)} collective-permute-done((bf16[224,128]{1,0:T(8,128)(2,1)S(1)}, bf16[224,128]{1,0:T(8,128)(2,1)S(1)}, u32[]{:S(2)}, u32[]{:S(2)}) %collective-permute-start.4) | collective-permute-done | bytes 57376 | tf_op jit(solution)/shard_map/ppermute | solution.py:319
  34.4 2.1 %collective-permute-done.5.c_ref = bf16[224,128]{1,0:T(8,128)(2,1)S(1)} collective-permute-done((bf16[224,128]{1,0:T(8,128)(2,1)S(1)}, bf16[224,128]{1,0:T(8,128)(2,1)S(1)}, u32[]{:S(2)}, u32[]{:S(2)}) %collective-permute-start.5) | collective-permute-done | bytes 57376 | tf_op jit(solution)/shard_map/ppermute | solution.py:319
  36.5 1.6 %collective-permute-start.6 = (bf16[112,128]{1,0:T(8,128)(2,1)S(1)}, bf16[112,128]{1,0:T(8,128)(2,1)S(1)}, u32[]{:S(2)}, u32[]{:S(2)}) collective-permute-start(bf16[112,128]{1,0:T(8,128)(2,1)S(1)} %get-tuple-element.37), channel_id=1, source_target_pairs={{0,4},{1,5},{2,6},{3,7},{4,0},{5,1},{6,2},{7,3},{8,12},{9,13},{10,... | collective-permute-start | bytes 86024 | tf_op jit(solution)/shard_map/ppermute | solution.py:329
  38.1 1.4 %collective-permute-start.7 = (bf16[112,128]{1,0:T(8,128)(2,1)S(1)}, bf16[112,128]{1,0:T(8,128)(2,1)S(1)}, u32[]{:S(2)}, u32[]{:S(2)}) collective-permute-start(bf16[112,128]{1,0:T(8,128)(2,1)S(1)} %get-tuple-element.37), channel_id=1, source_target_pairs={{0,5},{1,4},{2,7},{3,6},{4,1},{5,0},{6,3},{7,2},{8,13},{9,12},{10,... | collective-permute-start | bytes 86024 | tf_op jit(solution)/shard_map/ppermute | solution.py:329
  39.5 0.5 %collective-permute-start.8 = (bf16[112,128]{1,0:T(8,128)(2,1)S(1)}, bf16[112,128]{1,0:T(8,128)(2,1)S(1)}, u32[]{:S(2)}, u32[]{:S(2)}) collective-permute-start(bf16[112,128]{1,0:T(8,128)(2,1)S(1)} %get-tuple-element.38), channel_id=1, source_target_pairs={{0,1},{1,0},{2,3},{3,2},{4,5},{5,4},{6,7},{7,6},{8,9},{9,8},{10,11... | collective-permute-start | bytes 86024 | tf_op jit(solution)/shard_map/ppermute | solution.py:329
  40.1 3.6 %shard_map.106 = bf16[2,64,4096]{2,1,0:T(8,128)(2,1)} custom-call(bf16[2,64,1024]{2,1,0:T(8,128)(2,1)S(1)} %get-tuple-element.28.pre_b_ref, bf16[256,576]{1,0:T(8,128)(2,1)S(1)} %get-tuple-element.29.wf_ref), custom_call_target="tpu_custom_call" | custom-call | flops 1000000000 | bytes 1048576 | tf_op jit(solution)/shard_map/pallas_call | solution.py:307
  43.7 0.0 collective-permute-done.6.a_ref
  43.7 0.0 collective-permute-done.7.b_ref
  43.7 1.2 %shard_map.109 = (f32[8,1600]{1,0:T(8,128)}, f32[1,64]{1,0:T(1,128)}) custom-call(f32[112,128]{1,0:T(8,128)S(1)} %get-tuple-element.36.own_ref, bf16[112,128]{1,0:T(8,128)(2,1)S(1)} %collective-permute-done.6.a_ref, bf16[112,128]{1,0:T(8,128)(2,1)S(1)} %collective-permute-done.7.b_ref, bf16[112,128]{1,0:T(8,128)(2,1)S(1)} %collective-permute-done.8.c_ref), custom_call_target="tpu_custom_call" | custom-call | bytes 1048576 | tf_op jit(solution)/shard_map/pallas_call | solution.py:307
  (16 shorter events, 0.1 us)
Async XLA Ops:
  0.6 0.7 %copy-start = (s32[16]{0:T(128)S(1)}, s32[16]{0:T(128)}, u32[]{:S(2)}) copy-start(s32[16]{0:T(128)} %owner_ref.3) | copy-start | bytes 196
  1.3 1.2 %copy-start.1 = (bf16[1,2,64,4096]{3,2,1,0:T(8,128)(2,1)S(1)}, bf16[1,2,64,4096]{3,2,1,0:T(8,128)(2,1)}, u32[]{:S(2)}) copy-start(bf16[1,2,64,4096]{3,2,1,0:T(8,128)(2,1)} %param.8) | copy-start | bytes 3145732
  2.5 0.9 %copy-start.2 = (bf16[2,64,1024]{2,1,0:T(8,128)(2,1)S(1)}, bf16[2,64,1024]{2,1,0:T(8,128)(2,1)}, u32[]{:S(2)}) copy-start(bf16[2,64,1024]{2,1,0:T(8,128)(2,1)} %ws_ref.3) | copy-start | bytes 786436
  3.5 0.9 %copy-start.4 = (bf16[2,64,576]{2,1,0:T(8,128)(2,1)S(1)}, bf16[2,64,576]{2,1,0:T(8,128)(2,1)}, u32[]{:S(2)}) copy-start(bf16[2,64,576]{2,1,0:T(8,128)(2,1)} %wd_ref.3) | copy-start | bytes 442372
  4.4 0.7 %copy-start.6 = (f32[32,64]{1,0:T(8,128)S(1)}, f32[32,64]{1,0:T(8,128)}, u32[]{:S(2)}) copy-start(f32[32,64]{1,0:T(8,128)} %bias_ref.1) | copy-start | bytes 24580
  5.1 0.7 %copy-start.7 = (bf16[1,2,1024]{2,1,0:T(2,128)(2,1)S(1)}, bf16[1,2,1024]{2,1,0:T(2,128)(2,1)}, u32[]{:S(2)}) copy-start(bf16[1,2,1024]{2,1,0:T(2,128)(2,1)} %param.12) | copy-start | bytes 12292
  5.8 7.6 %copy-start.10 = (s32[8,4]{0,1:T(4,128)S(1)}, s32[8,4]{0,1:T(4,128)}, u32[]{:S(2)}) copy-start(s32[8,4]{0,1:T(4,128)} %param.13) | copy-start | bytes 388
  5.8 7.6 %copy-start.3 = (bf16[2,64,1024]{2,1,0:T(8,128)(2,1)S(1)}, bf16[2,64,1024]{2,1,0:T(8,128)(2,1)}, u32[]{:S(2)}) copy-start(bf16[2,64,1024]{2,1,0:T(8,128)(2,1)} %ws_ref.3) | copy-start | bytes 786436
  5.8 7.6 %copy-start.5 = (bf16[2,64,576]{2,1,0:T(8,128)(2,1)S(1)}, bf16[2,64,576]{2,1,0:T(8,128)(2,1)}, u32[]{:S(2)}) copy-start(bf16[2,64,576]{2,1,0:T(8,128)(2,1)} %wd_ref.3) | copy-start | bytes 442372
  10.2 3.8 %collective-permute-start = (bf16[144,1024]{1,0:T(8,128)(2,1)S(1)}, bf16[144,1024]{1,0:T(8,128)(2,1)S(1)}, u32[]{:S(2)}, u32[]{:S(2)}) collective-permute-start(bf16[144,1024]{1,0:T(8,128)(2,1)S(1)} %get-tuple-element.22), channel_id=1, source_target_pairs={{0,2},{2,0},{4,6},{6,4},{8,10},{10,8},{12,14},{14,12},{16,18},{18,... | collective-permute-start | bytes 884744 | tf_op jit(solution)/shard_map/ppermute | solution.py:319
  10.7 9.9 %collective-permute-start.1 = (bf16[144,1024]{1,0:T(8,128)(2,1)S(1)}, bf16[144,1024]{1,0:T(8,128)(2,1)S(1)}, u32[]{:S(2)}, u32[]{:S(2)}) collective-permute-start(bf16[144,1024]{1,0:T(8,128)(2,1)S(1)} %get-tuple-element.22), channel_id=1, source_target_pairs={{0,3},{1,2},{2,1},{3,0},{4,7},{5,6},{6,5},{7,4},{8,11},{9,10},{10,... | collective-permute-start | bytes 884744 | tf_op jit(solution)/shard_map/ppermute | solution.py:329
  14.0 6.7 %copy-start.8 = (bf16[1,2,1024]{2,1,0:T(2,128)(2,1)S(1)}, bf16[1,2,1024]{2,1,0:T(2,128)(2,1)}, u32[]{:S(2)}) copy-start(bf16[1,2,1024]{2,1,0:T(2,128)(2,1)} %param.12) | copy-start | bytes 12292
  20.6 0.7 %copy-start.9 = (s32[8]{0:T(128)S(1)}, s32[8]{0:T(128)}, u32[]{:S(2)}) copy-start(s32[8]{0:T(128)} %valid_ref.1) | copy-start | bytes 100
  24.2 1.4 %collective-permute-start.2 = (bf16[2,224,128]{2,1,0:T(8,128)(2,1)S(1)}, bf16[2,224,128]{2,1,0:T(8,128)(2,1)S(1)}, u32[]{:S(2)}, u32[]{:S(2)}) collective-permute-start(bf16[2,224,128]{2,1,0:T(8,128)(2,1)S(1)} %get-tuple-element.31), channel_id=1, source_target_pairs={{0,2},{2,0},{4,6},{6,4},{8,10},{10,8},{12,14},{14,12},{16,18},{18,... | collective-permute-start | bytes 344072 | tf_op jit(solution)/shard_map/ppermute | solution.py:319
  26.3 4.5 %collective-permute-start.3 = (bf16[224,128]{1,0:T(8,128)(2,1)S(1)}, bf16[224,128]{1,0:T(8,128)(2,1)S(1)}, u32[]{:S(2)}, u32[]{:S(2)}) collective-permute-start(bf16[224,128]{1,0:T(8,128)(2,1)S(1)} %get-tuple-element.33), channel_id=1, source_target_pairs={{0,8},{2,10},{4,12},{6,14},{8,0},{10,2},{12,4},{14,6},{16,24},{18,... | collective-permute-start | bytes 172040 | tf_op jit(solution)/shard_map/ppermute | solution.py:319
  27.9 6.5 %collective-permute-start.4 = (bf16[224,128]{1,0:T(8,128)(2,1)S(1)}, bf16[224,128]{1,0:T(8,128)(2,1)S(1)}, u32[]{:S(2)}, u32[]{:S(2)}) collective-permute-start(bf16[224,128]{1,0:T(8,128)(2,1)S(1)} %get-tuple-element.34), channel_id=1, source_target_pairs={{0,16},{2,18},{4,20},{6,22},{8,24},{10,26},{12,28},{14,30},{16,0},... | collective-permute-start | bytes 172040 | tf_op jit(solution)/shard_map/ppermute | solution.py:319
  30.5 6.0 %collective-permute-start.5 = (bf16[224,128]{1,0:T(8,128)(2,1)S(1)}, bf16[224,128]{1,0:T(8,128)(2,1)S(1)}, u32[]{:S(2)}, u32[]{:S(2)}) collective-permute-start(bf16[224,128]{1,0:T(8,128)(2,1)S(1)} %get-tuple-element.35), channel_id=1, source_target_pairs={{0,24},{2,26},{4,28},{6,30},{8,16},{10,18},{12,20},{14,22},{16,8},... | collective-permute-start | bytes 172040 | tf_op jit(solution)/shard_map/ppermute | solution.py:319
  36.5 7.2 %collective-permute-start.6 = (bf16[112,128]{1,0:T(8,128)(2,1)S(1)}, bf16[112,128]{1,0:T(8,128)(2,1)S(1)}, u32[]{:S(2)}, u32[]{:S(2)}) collective-permute-start(bf16[112,128]{1,0:T(8,128)(2,1)S(1)} %get-tuple-element.37), channel_id=1, source_target_pairs={{0,4},{1,5},{2,6},{3,7},{4,0},{5,1},{6,2},{7,3},{8,12},{9,13},{10,... | collective-permute-start | bytes 86024 | tf_op jit(solution)/shard_map/ppermute | solution.py:329
  38.1 5.6 %collective-permute-start.7 = (bf16[112,128]{1,0:T(8,128)(2,1)S(1)}, bf16[112,128]{1,0:T(8,128)(2,1)S(1)}, u32[]{:S(2)}, u32[]{:S(2)}) collective-permute-start(bf16[112,128]{1,0:T(8,128)(2,1)S(1)} %get-tuple-element.37), channel_id=1, source_target_pairs={{0,5},{1,4},{2,7},{3,6},{4,1},{5,0},{6,3},{7,2},{8,13},{9,12},{10,... | collective-permute-start | bytes 86024 | tf_op jit(solution)/shard_map/ppermute | solution.py:329
  39.5 4.2 %collective-permute-start.8 = (bf16[112,128]{1,0:T(8,128)(2,1)S(1)}, bf16[112,128]{1,0:T(8,128)(2,1)S(1)}, u32[]{:S(2)}, u32[]{:S(2)}) collective-permute-start(bf16[112,128]{1,0:T(8,128)(2,1)S(1)} %get-tuple-element.38), channel_id=1, source_target_pairs={{0,1},{1,0},{2,3},{3,2},{4,5},{5,4},{6,7},{7,6},{8,9},{9,8},{10,11... | collective-permute-start | bytes 86024 | tf_op jit(solution)/shard_map/ppermute | solution.py:329

commit v2 on v1

v2 whole, which is shorter than its diff:
```python
import functools
import math

import jax
import jax.numpy as jnp
from jax import lax
from jax.experimental import pallas as pl
from jax.experimental.pallas import tpu as pltpu
from jax.sharding import PartitionSpec as P

CH = 64
ROW_TAPS = 4
DIL_TAPS = 9
BLOCKS = 14
SHIFTS = [(dr, dc) for dr in (-1, 0, 1) for dc in (-1, 0, 1)]
F32 = jnp.float32
BF16 = jnp.bfloat16
VMEM_LIMIT = 24 * 1024 * 1024


def shift_index(dr, dc):
    return (dr + 1) * 3 + dc + 1


def dot(a, b):
    return lax.dot_general(a, b, (((1,), (0,)), ((), ())), preferred_element_type=F32)


def dot_nt(a, b):
    return lax.dot_general(a, b, (((1,), (1,)), ((), ())), preferred_element_type=F32)


def shifted_masks(side, reach):
    cell = lax.broadcasted_iota(jnp.int32, (1, side * side), 1)
    row, col = cell // side, cell % side
    masks = {}
    for dr, dc in SHIFTS:
        ok = (
            (row + dr * reach >= 0)
            & (row + dr * reach < side)
            & (col + dc * reach >= 0)
            & (col + dc * reach < side)
        )
        masks[dr, dc] = ok.astype(F32).astype(BF16)
    return masks


def shifted(x, dr, dc, side, reach, masks):
    if dr == 0 and dc == 0:
        return x
    cells = side * side
    return pltpu.roll(x, (-(dr * side + dc) * reach) % cells, 1) * masks[dr, dc]


def phase_matrix(side, transposed):
    size = 16 * side
    dims = (size, size)
    source = lax.broadcasted_iota(jnp.int32, dims, 1 if transposed else 0)
    target = lax.broadcasted_iota(jnp.int32, dims, 0 if transposed else 1)
    phase, cell = target // (4 * side), target % (4 * side)
    row, col = cell // side, cell % side
    wanted = (2 * row + phase // 2) * (2 * side) + 2 * col + phase % 2
    return jnp.where(source == wanted, 1.0, 0.0).astype(BF16)


TAP_LINES = {0: (1, -1), 1: (0, 0), 2: (1, 0), 3: (0, 1)}


def tap_matrices(weight, taps, scratch):
    wide = weight.astype(F32)
    scratch[0 : CH * taps, 0:CH] = wide.T
    return [scratch[pl.ds(tap, CH, stride=taps), 0:CH] for tap in range(taps)]


def forward_patch(x_ref, cot, w_strided, w_dilated, bias_col, ph_ref, pre_ref, act_ref, send_ref, im_scr):
    side = math.isqrt(x_ref.shape[1]) // 2
    run, lanes = 16 * side, side * side // 128
    split = phase_matrix(side, False)
    near, far = shifted_masks(side, 1), shifted_masks(side, 2)
    runs = x_ref.shape[1] // run
    stacked = jnp.concatenate([x_ref[:, q * run : (q + 1) * run] for q in range(runs)], axis=0)
    parts = dot(stacked, split).astype(BF16)
    for q in range(runs):
        for phase in range(4):
            ph_ref[phase * CH : (phase + 1) * CH, q * 4 * side : (q + 1) * 4 * side] = parts[
                q * CH : (q + 1) * CH, phase * 4 * side : (phase + 1) * 4 * side
            ]
    for rt in range(4):
        for ct in range(4):
            (pr, dr), (pc, dc) = TAP_LINES[rt], TAP_LINES[ct]
            phase, tap = pr * 2 + pc, rt * 4 + ct
            im_scr[tap * CH : (tap + 1) * CH, :] = shifted(
                ph_ref[phase * CH : (phase + 1) * CH, :], dr, dc, side, 1, near
            )
    pre = dot(w_strided, im_scr[...]) + bias_col
    pre_ref[...] = pre
    act = (pre * (1.0 / (1.0 + jnp.exp(-pre)))).astype(BF16)
    act_ref[...] = act
    for tap, (dr, dc) in enumerate(SHIFTS):
        im_scr[tap * CH : (tap + 1) * CH, :] = shifted(act, dr, dc, side, 2, far)
    out = dot(w_dilated, im_scr[0 : DIL_TAPS * CH, :]).astype(BF16)
    for lane in range(lanes):
        send_ref[lane * CH : (lane + 1) * CH, :] = out[:, lane * 128 : (lane + 1) * 128]
    rows = [cot[:, lane * 128 : (lane + 1) * 128] for lane in range(lanes)]
    rows.append(jnp.zeros((16 - lanes, 128), F32))
    send_ref[lanes * CH :, :] = jnp.concatenate(rows, axis=0).astype(BF16)


def first_kernel(
    owner_hbm, x_hbm, ws_hbm, wd_hbm, bias_hbm, cot_hbm,
    ph_ref, pre_ref, act_ref, send_ref, strided_ref, dilated_ref, bias_ref,
    x_ref, ws_ref, wd_ref, cot_ref, table_ref, owner_ref, wscr, im_scr, sems,
):
    scene = lax.axis_index("scene")
    branch = scene % 2
    copies = [
        pltpu.make_async_copy(source, target, sems.at[i])
        for i, (source, target) in enumerate(
            [
                (ws_hbm.at[branch], ws_ref),
                (wd_hbm.at[branch], wd_ref),
                (x_hbm.at[0], x_ref),
                (owner_hbm, owner_ref),
                (bias_hbm, table_ref),
                (cot_hbm, cot_ref),
            ]
        )
    ]
    for copy in copies:
        copy.start()
    copies[0].wait()
    mats = tap_matrices(ws_ref[...], 16, wscr)
    strided_ref[...] = jnp.concatenate(mats, axis=0).T.astype(BF16)
    copies[1].wait()
    mats = tap_matrices(wd_ref[...], 9, wscr)
    dilated_ref[...] = jnp.concatenate(mats, axis=0).T.astype(BF16)
    for copy in copies[2:]:
        copy.wait()
    bias_row = table_ref[pl.ds(owner_ref[scene], 1), :]
    bias_ref[...] = jnp.broadcast_to(jnp.broadcast_to(bias_row, (8, CH)).T[:, 0:1], (CH, 128))
    forward_patch(
        x_ref, cot_ref[...].astype(F32)[0:1, :], strided_ref[...], dilated_ref[...], bias_ref[:, 0:1],
        ph_ref, pre_ref, act_ref, send_ref, im_scr,
    )


def later_kernel(
    x_ref, cot_ref, w_strided_ref, w_dilated_ref, bias_ref, *refs, patch
):
    ph_ref, pre_ref, act_ref, send_ref, im_scr = refs[-5:]
    forward_patch(
        x_ref.at[patch], cot_ref[...].astype(F32)[patch : patch + 1, :], w_strided_ref[...], w_dilated_ref[...],
        bias_ref[:, 0:1], ph_ref, pre_ref, act_ref, send_ref, im_scr,
    )


def prepare_kernel(pairing_ref, valid_ref, owner_ref, ws_ref, wd_ref, *refs, bias_rows):
    patches = (len(refs) - 5) // 2
    pre_refs, slope_refs = refs[:patches], refs[patches : 2 * patches]
    wf_ref, wt_ref, select_ref, place_ref, wscr = refs[2 * patches :]
    scene, tile = lax.axis_index("scene"), lax.axis_index("tile")
    branch, pair = scene % 2, scene // 2
    for pre_ref, slope_ref in zip(pre_refs, slope_refs):
        pre = pre_ref[...]
        gate = 1.0 / (1.0 + jnp.exp(-pre))
        slope_ref[...] = gate * (1.0 + pre * (1.0 - gate))
    mats = tap_matrices(ws_ref[branch], 16, wscr)
    blocks = {}
    for rt in range(4):
        for ct in range(4):
            (pr, dr), (pc, dc) = TAP_LINES[rt], TAP_LINES[ct]
            blocks[pr * 2 + pc, shift_index(-dr, -dc)] = mats[rt * 4 + ct]
    zero = jnp.zeros((CH, CH), F32)
    for phase in range(4):
        row = [blocks.get((phase, s), zero) for s in range(9)]
        wf_ref[phase * CH : (phase + 1) * CH, :] = jnp.concatenate(row, axis=1).astype(BF16)
    mats = tap_matrices(wd_ref[branch], 9, wscr)
    wt_ref[...] = jnp.concatenate(mats[::-1], axis=1).astype(BF16)
    total = pairing_ref.shape[1]
    row = lax.broadcasted_iota(jnp.int32, select_ref.shape, 0)
    select = jnp.zeros(select_ref.shape, F32)
    for p in range(patches):
        position = tile * patches + p
        matched, inverse = pairing_ref[pair, position], jnp.int32(0)
        for i in range(total):
            inverse = inverse + jnp.where(pairing_ref[pair, i] == position, i, 0)
        matched = jnp.where(branch == 0, matched, inverse)
        chosen = p * total + jnp.where(matched // patches == tile, 0, patches) + matched % patches
        live = jnp.where(position < valid_ref[pair], patches * total + p, -1)
        select = jnp.where((row == chosen) | (row == live), 1.0, select)
    select_ref[...] = select
    row = lax.broadcasted_iota(jnp.int32, place_ref.shape, 0)
    here = scene // 2 % 4
    place = jnp.zeros(place_ref.shape, F32)
    for k, source in enumerate((scene, scene ^ 1)):
        owner = owner_ref[source]
        target = owner // (2 * bias_rows)
        half = jnp.where(target // 8 == branch, 0, 1)
        wanted = k * 64 + ((target // 2 % 4) ^ here) * 16 + half * 8 + owner % (2 * bias_rows)
        place = jnp.where(row == jnp.where(target % 2 == branch, wanted, -1), 1.0, place)
    place_ref[...] = place


def backward_kernel(select_ref, wt_ref, *refs, patches, chunked, weight_scale, bias_scale):
    near_refs, far_refs, own_refs, act_refs, slope_refs, ph_refs = (
        refs[k * patches : (k + 1) * patches] for k in range(6)
    )
    pre_b_refs, refs = refs[6 * patches : 7 * patches], refs[7 * patches :]
    if chunked:
        keep_ref, give_ref, shift_scr, dil_scr, grad_acc, grad_scr = refs
    else:
        grad_scr, shift_scr, dil_scr, grad_acc = refs
    side = math.isqrt(act_refs[0].shape[1])
    lanes = side * side // 128
    scene = lax.axis_index("scene")
    branch = scene % 2
    near, far = shifted_masks(side, 1), shifted_masks(side, 2)
    bias = jnp.zeros((CH, 1), F32)
    candidates = list(near_refs) + list(far_refs)
    count = len(candidates)
    for p in range(patches):
        partner = None
        for k, ref in enumerate(candidates):
            term = ref[...] * select_ref[p * count + k : p * count + k + 1, :].astype(BF16)
            partner = term if partner is None else partner + term
        live = select_ref[patches * count + p : patches * count + p + 1, :]
        cots = own_refs[p][lanes * CH :, :].astype(F32) + partner[lanes * CH :, :].astype(F32)
        signal = cots * live
        out_grad = jnp.concatenate(
            [
                (signal[j : j + 1, :] * partner[j * CH : (j + 1) * CH, :].astype(F32)).astype(BF16)
                for j in range(lanes)
            ],
            axis=1,
        )
        for tap, (dr, dc) in enumerate(SHIFTS):
            shift_scr[tap * CH : (tap + 1) * CH, :] = shifted(out_grad, dr, dc, side, 2, far)
        act_grad = dot(wt_ref[...], shift_scr[...])
        act = act_refs[p][...]
        dil = dot_nt(shift_scr[...], jnp.concatenate([act, act], axis=0))
        pre_grad = act_grad * slope_refs[p][...]
        bias = bias + jnp.sum(pre_grad, axis=1, keepdims=True)
        pre_b = pre_grad.astype(BF16)
        pre_b_refs[p][...] = pre_b
        for s, (dr, dc) in enumerate(SHIFTS):
            shift_scr[s * CH : (s + 1) * CH, :] = shifted(pre_b, dr, dc, side, 1, near)
        strided = dot_nt(shift_scr[...], ph_refs[p][...])
        if p == 0:
            dil_scr[...] = dil
            grad_acc[...] = strided
        else:
            dil_scr[...] += dil
            grad_acc[...] += strided
    lower = lax.broadcasted_iota(jnp.int32, (CH, 2 * CH), 1) < CH

    def strided_piece(pr, shift):
        return grad_acc[shift * CH : (shift + 1) * CH, pr * 2 * CH : (pr + 1) * 2 * CH]

    for rt in range(4):
        pr, dr = TAP_LINES[rt]
        for k in range(2):
            low_dc, high_dc = (0, 0) if k == 0 else (1, -1)
            low = strided_piece(pr, shift_index(-dr, -low_dc))
            high = strided_piece(pr, shift_index(-dr, -high_dc))
            grad_scr[rt * 2 + k] = jnp.where(lower, low, high) * weight_scale
    for j in range(5):
        low = dil_scr[(8 - 2 * j) * CH : (9 - 2 * j) * CH, :]
        high = dil_scr[(7 - 2 * j) * CH : (8 - 2 * j) * CH, :] if j < 4 else jnp.zeros_like(low)
        grad_scr[8 + j] = jnp.where(lower, low, high) * weight_scale
    bias_wide = jnp.concatenate([jnp.broadcast_to(bias, (CH, 8)).T, jnp.zeros((8, CH), F32)], axis=1)
    bias_wide = bias_wide * bias_scale
    if not chunked:
        grad_scr[BLOCKS - 1] = jnp.concatenate([bias_wide] * 8, axis=0)
        return
    here = scene // 2 % 4
    for ref, core in ((keep_ref, branch), (give_ref, 1 - branch)):
        for d in range(4):
            row = pl.multiple_of(((here ^ d) * 2 + core) * 8, 8)
            pieces = [grad_scr[block, pl.ds(row, 8), :] for block in range(BLOCKS - 1)]
            ref[d] = jnp.concatenate(pieces + [bias_wide], axis=0).astype(BF16)


def spread_kernel(place_ref, keep_ref, got_ref, *out_refs):
    rows = keep_ref.shape[1]
    top = lax.broadcasted_iota(jnp.int32, (16, 128), 0) < 8
    mine = keep_ref[0, rows - 16 :, :].astype(F32)[8:9, :]
    theirs = got_ref[0, rows - 16 :, :].astype(F32)[8:9, :]
    for d, out_ref in enumerate(out_refs):
        for half, ref in enumerate((keep_ref, got_ref)):
            at = d * 16 + half * 8
            bias = place_ref[at : at + 8, :] * mine + place_ref[64 + at : 72 + at, :] * theirs
            last = ref[d, rows - 16 :, :].astype(F32)
            last = jnp.where(top, last, jnp.concatenate([bias, bias], axis=0))
            out_ref[half * rows : (half + 1) * rows - 16, :] = ref[d, : rows - 16, :]
            out_ref[(half + 1) * rows - 16 : (half + 1) * rows, :] = last.astype(BF16)


def join_kernel(own_ref, a_ref, b_ref, c_ref, keep_ref, stay_ref, cross_ref):
    scene = lax.axis_index("scene")
    rows = keep_ref.shape[0]
    total = (own_ref[...].astype(F32) + a_ref[...].astype(F32)) + (
        b_ref[...].astype(F32) + c_ref[...].astype(F32)
    )
    mine, theirs = total[:rows, :], total[rows:, :]
    first = scene // 8 == scene % 2
    kept = jnp.where(first, mine, theirs)
    keep_ref[...] = kept
    stay_ref[...] = kept.astype(BF16)
    cross_ref[...] = jnp.where(first, theirs, mine).astype(BF16)


def finish_kernel(own_ref, a_ref, b_ref, c_ref, weights_ref, bias_ref, strided_scr, dilated_scr):
    tile = lax.axis_index("tile")
    total = (own_ref[...] + a_ref[...].astype(F32)) + (b_ref[...].astype(F32) + c_ref[...].astype(F32))
    bias = total[(BLOCKS - 1) * 8 :, :]
    index = lax.broadcasted_iota(jnp.int32, bias.shape, 0)
    bias_ref[...] = jnp.sum(jnp.where(index == tile, bias, 0.0), axis=0, keepdims=True)[:, 0:CH]
    width = 2 * CH
    turned = jnp.concatenate([total, jnp.zeros((width - BLOCKS * 8, width), F32)], axis=0).T
    for block in range(BLOCKS - 1):
        lined = turned if block == 0 else pltpu.roll(turned, width - block * 8, 1)
        for half in range(2):
            piece = lined[half * CH : (half + 1) * CH, :]
            if block < 8:
                tap = block // 2 * 4 + ((1, 2), (3, 0))[block % 2][half]
                strided_scr[pl.ds(tap, CH, stride=16), :] = piece
            elif (block - 8) * 2 + half < DIL_TAPS:
                dilated_scr[pl.ds((block - 8) * 2 + half, CH, stride=DIL_TAPS), :] = piece
    weights_ref[:, 0 : 16 * CH] = strided_scr[...].T[0:8, :]
    weights_ref[:, 16 * CH :] = dilated_scr[...].T[0:8, :]


def feature_kernel(pre_b_ref, wf_ref, *refs, patch):
    out_hbm, shift_scr, out_scr, sem = refs[-4:]
    side = math.isqrt(pre_b_ref.shape[1])
    near = shifted_masks(side, 1)
    merge = phase_matrix(side, True)
    run, wide = 16 * side, 4 * side
    pre_b = pre_b_ref[...]
    for s, (dr, dc) in enumerate(SHIFTS):
        shift_scr[s * CH : (s + 1) * CH, :] = shifted(pre_b, dr, dc, side, 1, near)
    phases = dot(wf_ref[...], shift_scr[...]).astype(BF16)
    runs = out_scr.shape[1] // run
    stacked = jnp.concatenate(
        [
            jnp.concatenate(
                [phases[k * CH : (k + 1) * CH, q * wide : (q + 1) * wide] for k in range(4)], axis=1
            )
            for q in range(runs)
        ],
        axis=0,
    )
    merged = dot(stacked, merge).astype(BF16)
    for q in range(runs):
        out_scr[:, q * run : (q + 1) * run] = merged[q * CH : (q + 1) * CH, :]
    copy = pltpu.make_async_copy(out_scr, out_hbm.at[patch], sem)
    copy.start()
    copy.wait()


SPACES = {"s": pltpu.SMEM, "v": pltpu.VMEM, "h": pltpu.HBM, "a": pl.ANY}


def call(kernel, outs, ins, scratch, *args, flops=0, out_space="v", aliases=None):
    args = [
        pltpu.with_memory_space_constraint(arg, pltpu.HBM) if space == "h" else arg
        for space, arg in zip(ins, args)
    ]
    return pl.pallas_call(
        kernel,
        out_shape=[jax.ShapeDtypeStruct(shape, kind) for shape, kind in outs],
        in_specs=[pl.BlockSpec(memory_space=SPACES[space]) for space in ins],
        out_specs=[pl.BlockSpec(memory_space=SPACES[out_space])] * len(outs),
        scratch_shapes=[pltpu.VMEM(*item) if isinstance(item, tuple) else item for item in scratch],
        input_output_aliases=aliases or {},
        compiler_params=pltpu.CompilerParams(vmem_limit_bytes=VMEM_LIMIT),
        cost_estimate=pl.CostEstimate(flops=flops, bytes_accessed=1 << 20, transcendentals=0),
    )(*args)


def scene_xor(x, distance):
    return lax.ppermute(x, "scene", [(i, i ^ distance) for i in range(lax.axis_size("scene"))])


def device_xor(x, scene_distance, tile_distance):
    tiles, scenes = lax.axis_size("tile"), lax.axis_size("scene")
    pairs = [
        (s * tiles + t, (s ^ scene_distance) * tiles + (t ^ tile_distance))
        for s in range(scenes)
        for t in range(tiles)
    ]
    return lax.ppermute(x, ("scene", "tile"), pairs)


def reduce_anywhere(blocks, tile_owner, bias_rows):
    channels = blocks.shape[1]
    scene = lax.axis_index("scene")
    scenes, tiles = lax.axis_size("scene"), lax.axis_size("tile")
    halves = blocks.reshape(BLOCKS, channels, 2, channels)
    strided, dilated = [None] * 16, []
    for block in range(8):
        for half in range(2):
            strided[block // 2 * 4 + ((1, 2), (3, 0))[block % 2][half]] = halves[block, :, half]
    for tap in range(DIL_TAPS):
        dilated.append(halves[8 + tap // 2, :, tap % 2])
    row = jnp.concatenate(
        [
            jnp.stack(strided, axis=-1).reshape(channels, 16 * channels),
            jnp.stack(dilated, axis=-1).reshape(channels, DIL_TAPS * channels),
        ],
        axis=1,
    )
    hit = jnp.arange(2, dtype=jnp.int32)[:, None, None] == scene % 2
    term = jnp.where(hit, row[None], 0.0).reshape(2 * channels, 25 * channels)
    weights = lax.psum(lax.psum_scatter(term, "scene", scatter_dimension=0, tiled=True), "tile")
    tile_id = lax.dynamic_index_in_dim(tile_owner, scene, 0, keepdims=False)
    owned = jnp.arange(scenes * tiles * bias_rows, dtype=jnp.int32) == tile_id
    bias = jnp.where(owned[:, None], halves[BLOCKS - 1, 0, 0][None, :], 0.0)
    return weights, lax.psum_scatter(bias, ("scene", "tile"), scatter_dimension=0, tiled=True)


def local(
    features_in,
    strided_weights,
    dilated_weights,
    tile_bias,
    cost_cotangent,
    footprint_pairing,
    valid_counts,
    tile_owner,
):
    features, own_cot = features_in[0], cost_cotangent[0]
    patches, channels, cells_in = features.shape
    cells = own_cot.shape[1]
    scenes, tiles = lax.axis_size("scene"), lax.axis_size("tile")
    weight_scale = 1.0 / math.sqrt(scenes * patches * tiles * cells)
    bias_scale = 1.0 / math.sqrt(patches * tiles * cells)
    bias_rows = tile_bias.shape[0] // (scenes * tiles)
    grid = (channels, cells)
    payload = (cells * channels // 128 + 16, 128)
    chunked = scenes == 16 and tiles == 2 and patches == 2 and bias_rows == 1
    wscr = ((16 * channels, 2 * channels), F32)
    im_scr = ((16 * channels, cells), BF16)
    patch_outs = [((4 * channels, cells), BF16), (grid, F32), (grid, BF16), (payload, BF16)]
    first_outs = patch_outs + [
        ((channels, 16 * channels), BF16),
        ((channels, 9 * channels), BF16),
        ((channels, 128), F32),
    ]
    *part, w_strided, w_dilated, bias_col = call(
        first_kernel,
        first_outs,
        "hhhhhh",
        [
            ((channels, cells_in), BF16),
            (strided_weights.shape[1:], BF16),
            (dilated_weights.shape[1:], BF16),
            (own_cot.shape, BF16),
            (tile_bias.shape, F32),
            pltpu.SMEM(tile_owner.shape, jnp.int32),
            wscr,
            im_scr,
            pltpu.SemaphoreType.DMA((6,)),
        ],
        tile_owner, features, strided_weights, dilated_weights, tile_bias, own_cot,
        flops=10**9,
    )
    parts, far, near = [part], [device_xor(part[3], 1, 1)], [scene_xor(part[3], 1)]
    for p in range(1, patches):
        part = call(
            functools.partial(later_kernel, patch=p),
            patch_outs,
            "vvvvv" + "a" * len(near),
            [im_scr],
            features, own_cot, w_strided, w_dilated, bias_col, *near,
            flops=10**9,
        )
        parts.append(part)
        far.append(device_xor(part[3], 1, 1))
        near.append(scene_xor(part[3], 1))
    phases, pre, act, send = zip(*parts)
    *slope, w_feature, w_act, select, place = call(
        functools.partial(prepare_kernel, bias_rows=bias_rows),
        [(grid, F32)] * patches
        + [
            ((4 * channels, 9 * channels), BF16),
            ((channels, 9 * channels), BF16),
            ((16, 128), F32),
            ((128, 128), F32),
        ],
        "sssvv" + "v" * patches,
        [wscr],
        footprint_pairing, valid_counts, tile_owner, strided_weights, dilated_weights, *pre,
        flops=10**9,
    )
    block_shape = ((BLOCKS, channels, 128), F32)
    half_shape = ((4, BLOCKS * 8, 128), BF16)
    scratch = [
        ((9 * channels, cells), BF16),
        ((9 * channels, 128), F32),
        ((9 * channels, 4 * channels), F32),
    ]
    results = call(
        functools.partial(
            backward_kernel, patches=patches, chunked=chunked, weight_scale=weight_scale, bias_scale=bias_scale
        ),
        [(grid, BF16)] * patches + ([half_shape] * 2 if chunked else [block_shape]),
        "v" * (2 + 6 * patches),
        scratch + ([block_shape] if chunked else []),
        select, w_act, *near, *far, *send, *act, *slope, *phases,
        flops=10**9,
    )
    pre_b, grads = results[:patches], results[patches:]

    def features_of(p, base):
        return call(
            functools.partial(feature_kernel, patch=p),
            [(features.shape, BF16)],
            "vv" if base is None else "vvh",
            [
                ((9 * channels, cells), BF16),
                ((channels, cells_in), BF16),
                pltpu.SemaphoreType.DMA,
            ],
            *((pre_b[p], w_feature) if base is None else (pre_b[p], w_feature, base)),
            flops=10**9,
            out_space="h",
            aliases=None if base is None else {2: 0},
        )[0]

    if not chunked:
        feature_grads = None
        for p in range(patches):
            feature_grads = features_of(p, feature_grads)
        return (feature_grads[None],) + reduce_anywhere(grads[0], tile_owner, bias_rows)
    keep, give = grads
    got = scene_xor(give, 1)
    stage = ((2 * BLOCKS * 8, 128), BF16)
    own, by_y, by_z, by_zy = call(spread_kernel, [stage] * 4, "vvv", [], place, keep, got)
    by_zy, by_z, by_y = scene_xor(by_zy, 6), scene_xor(by_z, 4), scene_xor(by_y, 2)
    feature_grads = features_of(0, None)
    feature_grads, own = lax.optimization_barrier((feature_grads, own))
    chunk = (BLOCKS * 8, 128)
    kept, stay, cross = call(
        join_kernel,
        [(chunk, F32), (chunk, BF16), (chunk, BF16)],
        "vvvv",
        [],
        own, by_y, by_z, by_zy,
    )
    by_zx, by_z, by_x = device_xor(cross, 8, 1), device_xor(cross, 8, 0), device_xor(stay, 0, 1)
    feature_grads = features_of(1, feature_grads)
    grad_weights, grad_bias = call(
        finish_kernel,
        [((8, 25 * channels), F32), ((1, channels), F32)],
        "vvvv",
        [((16 * channels, 128), F32), ((9 * channels, 128), F32)],
        kept, by_zx, by_z, by_x,
    )
    return (feature_grads[None], grad_weights, grad_bias)


def solution(mesh):
    return jax.shard_map(
        local,
        mesh=mesh,
        in_specs=(
            P("scene", "tile", None, None),
            P(),
            P(),
            P(),
            P("scene", "tile", None),
            P(),
            P(),
            P(),
        ),
        out_specs=(P("scene", "tile", None, None), P("scene", None), P(("scene", "tile"), None)),
        check_vma=False,
    )
```

time: 45.2 us -> 35.8 us (0.79)
  waiting for transfers between devices: 13.6 us -> 8.01 us
  local copies, waits for them, and re-layouts: 5.89 us -> 0.77 us
  starting transfers between devices: 11.3 us -> 13 us
    unnamed x23 -> x15, local copies, waits for them, and re-layouts: 5.89 us -> 0.77 us
    ppermute x5 -> x6, waiting for transfers between devices: 6.93 us -> 3.8 us  [scene_xor(): lax.ppermute(x, 'scene', [(i, i ^ distance) for i in range(lax.axis_size(...]
    ppermute x4 -> x5, waiting for transfers between devices: 6.65 us -> 4.21 us  [device_xor(): return lax.ppermute(x, ('scene', 'tile'), pairs)]
    ppermute x4 -> x5, starting transfers between devices: 6.17 us -> 8.33 us  [device_xor(): return lax.ppermute(x, ('scene', 'tile'), pairs)]
    ppermute x5 -> x6, starting transfers between devices: 5.14 us -> 4.68 us  [scene_xor(): lax.ppermute(x, 'scene', [(i, i ^ distance) for i in range(lax.axis_size(...]
    pallas_call x7 -> x9, Pallas kernels: 13.4 us -> 13.1 us  [call(): pl.pallas_call(kernel, out_shape=[jax.ShapeDtypeStruct(shape, kind) for s...]
  transfers between devices with their start and end apart: 9 -> 11, of which waited for: 4 -> 6; matrix products, arithmetic and copies ran while one was open for 0% -> 0% of each run, Pallas kernels for 9% -> 18%
where the time goes in v2:
time: 35.8 us; the launch traced here: 35.6 us
  Pallas kernels  13.1 us (37%)
  starting transfers between devices  13 us (36%)
  waiting for transfers between devices  8.01 us (22%)
  local copies, waits for them, and re-layouts  0.77 us (2%)
  between operations  0.77 us (2%)
    pallas_call x9, Pallas kernels, call(): pl.pallas_call(kernel, out_shape=[jax.ShapeDtypeStruct(shape, kind) for s...  13.1 us
    ppermute x5, starting transfers between devices, device_xor(): return lax.ppermute(x, ('scene', 'tile'), pairs)  8.33 us
    ppermute x6, starting transfers between devices, scene_xor(): lax.ppermute(x, 'scene', [(i, i ^ distance) for i in range(lax.axis_size(...  4.68 us
    ppermute x5, waiting for transfers between devices, device_xor(): return lax.ppermute(x, ('scene', 'tile'), pairs)  4.21 us
    ppermute x6, waiting for transfers between devices, scene_xor(): lax.ppermute(x, 'scene', [(i, i ^ distance) for i in range(lax.axis_size(...  3.8 us
    unnamed x15, local copies, waits for them, and re-layouts  0.77 us
  transfers between devices with their start and end apart: 11, of which 6 were waited for; matrix products, arithmetic and copies ran while one was open for 0% of the time, Pallas kernels for 18%

profile of v2, /device:TPU:0, one launch (start us, length us, event | category | flops | bytes accessed | tf_op | source)
XLA Modules:
  0.0 35.6 jit_solution(16977809024887035180)
XLA Ops:
  0.6 3.2 %shard_map.103 = (bf16[256,1024]{1,0:T(8,128)(2,1)S(1)}, f32[64,1024]{1,0:T(8,128)S(1)}, bf16[64,1024]{1,0:T(8,128)(2,1)S(1)}, bf16[528,128]{1,0:T(8,128)(2,1)S(...) custom-call(s32[16]{0:T(128)} %owner_ref.1, bf16[2,64,4096]{2,1,0:T(8,128)(2,1)} %bitcast.3, ...), custom_call_target="tpu_custom_call" | custom-call | flops 1000000000 | bytes 1048576 | tf_op jit(solution)/shard_map/pallas_call | solution.py:369
  3.9 0.0 copy-start.3
  3.9 0.5 %collective-permute-start = (bf16[528,128]{1,0:T(8,128)(2,1)S(1)}, bf16[528,128]{1,0:T(8,128)(2,1)S(1)}, u32[]{:S(2)}, u32[]{:S(2)}) collective-permute-start(bf16[528,128]{1,0:T(8,128)(2,1)S(1)} %get-tuple-element.39.refs_4_), channel_id=1, source_target_pairs={{0,2},{2,0},{4,6},{6,4},{8,10},{10,8},{12,14},{14,12},{16,18},{18,... | collective-permute-start | bytes 405512 | tf_op jit(solution)/shard_map/ppermute | solution.py:382
  4.4 2.6 %collective-permute-start.2 = (bf16[528,128]{1,0:T(8,128)(2,1)S(1)}, bf16[528,128]{1,0:T(8,128)(2,1)S(1)}, u32[]{:S(2)}, u32[]{:S(2)}) collective-permute-start(bf16[528,128]{1,0:T(8,128)(2,1)S(1)} %get-tuple-element.39.refs_4_), channel_id=1, source_target_pairs={{0,3},{1,2},{2,1},{3,0},{4,7},{5,6},{6,5},{7,4},{8,11},{9,10},{10,... | collective-permute-start | bytes 405512 | tf_op jit(solution)/shard_map/ppermute | solution.py:392
  7.0 0.0 collective-permute-done.refs_0_
  7.0 0.0 copy-start.6
  7.0 0.0 copy-start.1
  7.0 0.0 copy-start.2
  7.1 1.5 %shard_map.104 = (bf16[256,1024]{1,0:T(8,128)(2,1)S(1)}, f32[64,1024]{1,0:T(8,128)S(1)}, bf16[64,1024]{1,0:T(8,128)(2,1)S(1)}, bf16[528,128]{1,0:T(8,128)(2,1)S(1)}) custom-call(bf16[2,64,4096]{2,1,0:T(8,128)(2,1)S(1)} %bitcast.4, bf16[2,1024]{1,0:T(2,128)(2,1)S(1)} %bitcast.6, bf16[64,1024]{1,0:T(8,128)(2,1)S(1)} %get-tuple-element.36.w_strided_ref, ...), custom_call_target="tpu_custom_call" | custom-call | flops 1000000000 | bytes 1048576 | tf_op jit(solution)/shard_map/pallas_call | solution.py:369
  8.5 0.1 collective-permute-start.1
  8.7 1.3 %collective-permute-start.3 = (bf16[528,128]{1,0:T(8,128)(2,1)S(1)}, bf16[528,128]{1,0:T(8,128)(2,1)S(1)}, u32[]{:S(2)}, u32[]{:S(2)}) collective-permute-start(bf16[528,128]{1,0:T(8,128)(2,1)S(1)} %get-tuple-element.43.refs_5_), channel_id=1, source_target_pairs={{0,3},{1,2},{2,1},{3,0},{4,7},{5,6},{6,5},{7,4},{8,11},{9,10},{10,... | collective-permute-start | bytes 405512 | tf_op jit(solution)/shard_map/ppermute | solution.py:392
  9.9 0.1 copy.12.pairing_ref
  10.0 0.6 %copy-done.4 = s32[8]{0:T(128)S(1)} copy-done((s32[8]{0:T(128)S(1)}, s32[8]{0:T(128)}, u32[]{:S(2)}) %copy-start.4) | copy-done | bytes 56
  10.7 0.0 copy-done.5
  10.7 1.2 %shard_map.105 = (f32[64,1024]{1,0:T(8,128)S(1)}, f32[64,1024]{1,0:T(8,128)S(1)}, bf16[256,576]{1,0:T(8,128)(2,1)S(1)}, bf16[64,576]{1,0:T(8,128)(2,1)S(1)}, f32...) custom-call(s32[8,4]{1,0:T(8,128)S(1)} %copy.12.pairing_ref, s32[8]{0:T(128)S(1)} %copy-done.4, s32[16]{0:T(128)S(1)} %copy-done.5, ...), custom_call_target="tpu_custom_call" | custom-call | flops 1000000000 | bytes 1048576 | tf_op jit(solution)/shard_map/pallas_call | solution.py:369
  11.9 2.1 %collective-permute-done.3.refs_3_ = bf16[528,128]{1,0:T(8,128)(2,1)S(1)} collective-permute-done((bf16[528,128]{1,0:T(8,128)(2,1)S(1)}, bf16[528,128]{1,0:T(8,128)(2,1)S(1)}, u32[]{:S(2)}, u32[]{:S(2)}) %collective-permute-start.3) | collective-permute-done | bytes 135200 | tf_op jit(solution)/shard_map/ppermute | solution.py:392
  14.0 2.3 %shard_map.106 = (bf16[64,1024]{1,0:T(8,128)(2,1)S(1)}, bf16[64,1024]{1,0:T(8,128)(2,1)S(1)}, bf16[4,112,128]{2,1,0:T(8,128)(2,1)S(1)}, bf16[4,112,128]{2,1,0:T(8,128)(2,1)S(1)}) custom-call(f32[16,128]{1,0:T(8,128)S(1)} %get-tuple-element.41.select_ref, bf16[64,576]{1,0:T(8,128)(2,1)S(1)} %get-tuple-element.42.wt_ref, ...), custom_call_target="tpu_custom_call" | custom-call | flops 1000000000 | bytes 1048576 | tf_op jit(solution)/shard_map/pallas_call | solution.py:369
  16.3 0.5 %collective-permute-start.4 = (bf16[4,112,128]{2,1,0:T(8,128)(2,1)S(1)}, bf16[4,112,128]{2,1,0:T(8,128)(2,1)S(1)}, u32[]{:S(2)}, u32[]{:S(2)}) collective-permute-start(bf16[4,112,128]{2,1,0:T(8,128)(2,1)S(1)} %get-tuple-element.55), channel_id=1, source_target_pairs={{0,2},{2,0},{4,6},{6,4},{8,10},{10,8},{12,14},{14,12},{16,18},{18,... | collective-permute-start | bytes 344072 | tf_op jit(solution)/shard_map/ppermute | solution.py:382
  16.7 1.0 %collective-permute-done.4.got_ref = bf16[4,112,128]{2,1,0:T(8,128)(2,1)S(1)} collective-permute-done((bf16[4,112,128]{2,1,0:T(8,128)(2,1)S(1)}, bf16[4,112,128]{2,1,0:T(8,128)(2,1)S(1)}, u32[]{:S(2)}, u32[]{:S(2)}) %collective-permute-start.4) | collective-permute-done | bytes 114720 | tf_op jit(solution)/shard_map/ppermute | solution.py:382
  17.7 1.6 %collective-permute-start.5 = (bf16[224,128]{1,0:T(8,128)(2,1)S(1)}, bf16[224,128]{1,0:T(8,128)(2,1)S(1)}, u32[]{:S(2)}, u32[]{:S(2)}) collective-permute-start(bf16[224,128]{1,0:T(8,128)(2,1)S(1)} %get-tuple-element.59), channel_id=1, source_target_pairs={{0,4},{2,6},{4,0},{6,2},{8,12},{10,14},{12,8},{14,10},{16,20},{18,... | collective-permute-start | bytes 172040 | tf_op jit(solution)/shard_map/ppermute | solution.py:382
  19.3 1.6 %collective-permute-start.6 = (bf16[224,128]{1,0:T(8,128)(2,1)S(1)}, bf16[224,128]{1,0:T(8,128)(2,1)S(1)}, u32[]{:S(2)}, u32[]{:S(2)}) collective-permute-start(bf16[224,128]{1,0:T(8,128)(2,1)S(1)} %get-tuple-element.60), channel_id=1, source_target_pairs={{0,8},{2,10},{4,12},{6,14},{8,0},{10,2},{12,4},{14,6},{16,24},{18,... | collective-permute-start | bytes 172040 | tf_op jit(solution)/shard_map/ppermute | solution.py:382
  20.9 0.4 %collective-permute-start.7 = (bf16[224,128]{1,0:T(8,128)(2,1)S(1)}, bf16[224,128]{1,0:T(8,128)(2,1)S(1)}, u32[]{:S(2)}, u32[]{:S(2)}) collective-permute-start(bf16[224,128]{1,0:T(8,128)(2,1)S(1)} %get-tuple-element.61), channel_id=1, source_target_pairs={{0,12},{2,14},{4,8},{6,10},{8,4},{10,6},{12,0},{14,2},{16,28},{18,... | collective-permute-start | bytes 172040 | tf_op jit(solution)/shard_map/ppermute | solution.py:382
  21.3 1.8 %shard_map.107.refs_0_ = bf16[2,64,4096]{2,1,0:T(8,128)(2,1)} custom-call(bf16[64,1024]{1,0:T(8,128)(2,1)S(1)} %get-tuple-element.52.pre_b_ref, bf16[256,576]{1,0:T(8,128)(2,1)S(1)} %get-tuple-element.51.wf_ref), custom_call_target="tpu_custom_call" | custom-call | flops 1000000000 | bytes 1048576 | tf_op jit(solution)/shard_map/pallas_call | solution.py:369
  23.2 0.6 %collective-permute-done.6.b_ref = bf16[224,128]{1,0:T(8,128)(2,1)S(1)} collective-permute-done((bf16[224,128]{1,0:T(8,128)(2,1)S(1)}, bf16[224,128]{1,0:T(8,128)(2,1)S(1)}, u32[]{:S(2)}, u32[]{:S(2)}) %collective-permute-start.6) | collective-permute-done | bytes 57376 | tf_op jit(solution)/shard_map/ppermute | solution.py:382
  23.8 2.2 %collective-permute-done.7.c_ref = bf16[224,128]{1,0:T(8,128)(2,1)S(1)} collective-permute-done((bf16[224,128]{1,0:T(8,128)(2,1)S(1)}, bf16[224,128]{1,0:T(8,128)(2,1)S(1)}, u32[]{:S(2)}, u32[]{:S(2)}) %collective-permute-start.7) | collective-permute-done | bytes 57376 | tf_op jit(solution)/shard_map/ppermute | solution.py:382
  26.0 3.4 %collective-permute-start.8 = (bf16[112,128]{1,0:T(8,128)(2,1)S(1)}, bf16[112,128]{1,0:T(8,128)(2,1)S(1)}, u32[]{:S(2)}, u32[]{:S(2)}) collective-permute-start(bf16[112,128]{1,0:T(8,128)(2,1)S(1)} %get-tuple-element.63), channel_id=1, source_target_pairs={{0,17},{1,16},{2,19},{3,18},{4,21},{5,20},{6,23},{7,22},{8,25},{9,... | collective-permute-start | bytes 86024 | tf_op jit(solution)/shard_map/ppermute | solution.py:392
  29.5 0.3 collective-permute-start.9
  29.8 0.7 %collective-permute-start.10 = (bf16[112,128]{1,0:T(8,128)(2,1)S(1)}, bf16[112,128]{1,0:T(8,128)(2,1)S(1)}, u32[]{:S(2)}, u32[]{:S(2)}) collective-permute-start(bf16[112,128]{1,0:T(8,128)(2,1)S(1)} %get-tuple-element.64), channel_id=1, source_target_pairs={{0,1},{1,0},{2,3},{3,2},{4,5},{5,4},{6,7},{7,6},{8,9},{9,8},{10,11... | collective-permute-start | bytes 86024 | tf_op jit(solution)/shard_map/ppermute | solution.py:392
  30.5 1.8 %shard_map.109 = bf16[2,64,4096]{2,1,0:T(8,128)(2,1)} custom-call(bf16[64,1024]{1,0:T(8,128)(2,1)S(1)} %get-tuple-element.50.pre_b_ref, bf16[256,576]{1,0:T(8,128)(2,1)S(1)} %get-tuple-element.51.wf_ref, bf16[2,64,4096]{2,1,0:T(8,128)(2,1)} %shard_map.107.refs_0_), custom_call_target="tpu_custom_call", output_to_operand_aliasing={{}: (2, {})} | custom-call | flops 1000000000 | bytes 1048576 | tf_op jit(solution)/shard_map/pallas_call | solution.py:369
  32.3 1.3 %collective-permute-done.10.c_ref = bf16[112,128]{1,0:T(8,128)(2,1)S(1)} collective-permute-done((bf16[112,128]{1,0:T(8,128)(2,1)S(1)}, bf16[112,128]{1,0:T(8,128)(2,1)S(1)}, u32[]{:S(2)}, u32[]{:S(2)}) %collective-permute-start.10) | collective-permute-done | bytes 28704 | tf_op jit(solution)/shard_map/ppermute | solution.py:392
  33.7 0.8 %collective-permute-done.9.b_ref = bf16[112,128]{1,0:T(8,128)(2,1)S(1)} collective-permute-done((bf16[112,128]{1,0:T(8,128)(2,1)S(1)}, bf16[112,128]{1,0:T(8,128)(2,1)S(1)}, u32[]{:S(2)}, u32[]{:S(2)}) %collective-permute-start.9) | collective-permute-done | bytes 28704 | tf_op jit(solution)/shard_map/ppermute | solution.py:392
  34.4 1.2 %shard_map.111 = (f32[8,1600]{1,0:T(8,128)}, f32[1,64]{1,0:T(1,128)}) custom-call(f32[112,128]{1,0:T(8,128)S(1)} %get-tuple-element.62.own_ref, bf16[112,128]{1,0:T(8,128)(2,1)S(1)} %collective-permute-done.8.a_ref, bf16[112,128]{1,0:T(8,128)(2,1)S(1)} %collective-permute-done.9.b_ref, bf16[112,128]{1,0:T(8,128)(2,1)S(1)} %collective-permute-done.10.c_ref), custom_call_target="tpu_custom_call" | custom-call | bytes 1048576 | tf_op jit(solution)/shard_map/pallas_call | solution.py:369
  (14 shorter events, 0.1 us)
Async XLA Ops:
  0.6 6.4 %copy-start = (bf16[1,2,64,4096]{3,2,1,0:T(8,128)(2,1)S(1)}, bf16[1,2,64,4096]{3,2,1,0:T(8,128)(2,1)}, u32[]{:S(2)}) copy-start(bf16[1,2,64,4096]{3,2,1,0:T(8,128)(2,1)} %param.8) | copy-start | bytes 3145732
  3.9 3.2 %copy-start.3 = (bf16[1,2,1024]{2,1,0:T(2,128)(2,1)S(1)}, bf16[1,2,1024]{2,1,0:T(2,128)(2,1)}, u32[]{:S(2)}) copy-start(bf16[1,2,1024]{2,1,0:T(2,128)(2,1)} %param.12) | copy-start | bytes 12292
  3.9 3.1 %collective-permute-start = (bf16[528,128]{1,0:T(8,128)(2,1)S(1)}, bf16[528,128]{1,0:T(8,128)(2,1)S(1)}, u32[]{:S(2)}, u32[]{:S(2)}) collective-permute-start(bf16[528,128]{1,0:T(8,128)(2,1)S(1)} %get-tuple-element.39.refs_4_), channel_id=1, source_target_pairs={{0,2},{2,0},{4,6},{6,4},{8,10},{10,8},{12,14},{14,12},{16,18},{18,... | collective-permute-start | bytes 405512 | tf_op jit(solution)/shard_map/ppermute | solution.py:382
  4.4 7.5 %collective-permute-start.2 = (bf16[528,128]{1,0:T(8,128)(2,1)S(1)}, bf16[528,128]{1,0:T(8,128)(2,1)S(1)}, u32[]{:S(2)}, u32[]{:S(2)}) collective-permute-start(bf16[528,128]{1,0:T(8,128)(2,1)S(1)} %get-tuple-element.39.refs_4_), channel_id=1, source_target_pairs={{0,3},{1,2},{2,1},{3,0},{4,7},{5,6},{6,5},{7,4},{8,11},{9,10},{10,... | collective-permute-start | bytes 405512 | tf_op jit(solution)/shard_map/ppermute | solution.py:392
  7.0 2.9 %copy-start.6 = (s32[8,4]{0,1:T(4,128)S(1)}, s32[8,4]{0,1:T(4,128)}, u32[]{:S(2)}) copy-start(s32[8,4]{0,1:T(4,128)} %param.13) | copy-start | bytes 388
  7.0 3.0 %copy-start.1 = (bf16[2,64,1024]{2,1,0:T(8,128)(2,1)S(1)}, bf16[2,64,1024]{2,1,0:T(8,128)(2,1)}, u32[]{:S(2)}) copy-start(bf16[2,64,1024]{2,1,0:T(8,128)(2,1)} %ws_ref.1) | copy-start | bytes 786436
  7.0 3.0 %copy-start.2 = (bf16[2,64,576]{2,1,0:T(8,128)(2,1)S(1)}, bf16[2,64,576]{2,1,0:T(8,128)(2,1)}, u32[]{:S(2)}) copy-start(bf16[2,64,576]{2,1,0:T(8,128)(2,1)} %wd_ref.1) | copy-start | bytes 442372
  8.5 3.3 %collective-permute-start.1 = (bf16[528,128]{1,0:T(8,128)(2,1)S(1)}, bf16[528,128]{1,0:T(8,128)(2,1)S(1)}, u32[]{:S(2)}, u32[]{:S(2)}) collective-permute-start(bf16[528,128]{1,0:T(8,128)(2,1)S(1)} %get-tuple-element.43.refs_5_), channel_id=1, source_target_pairs={{0,2},{2,0},{4,6},{6,4},{8,10},{10,8},{12,14},{14,12},{16,18},{18,... | collective-permute-start | bytes 405512 | tf_op jit(solution)/shard_map/ppermute | solution.py:382
  8.7 5.3 %collective-permute-start.3 = (bf16[528,128]{1,0:T(8,128)(2,1)S(1)}, bf16[528,128]{1,0:T(8,128)(2,1)S(1)}, u32[]{:S(2)}, u32[]{:S(2)}) collective-permute-start(bf16[528,128]{1,0:T(8,128)(2,1)S(1)} %get-tuple-element.43.refs_5_), channel_id=1, source_target_pairs={{0,3},{1,2},{2,1},{3,0},{4,7},{5,6},{6,5},{7,4},{8,11},{9,10},{10,... | collective-permute-start | bytes 405512 | tf_op jit(solution)/shard_map/ppermute | solution.py:392
  10.0 0.7 %copy-start.4 = (s32[8]{0:T(128)S(1)}, s32[8]{0:T(128)}, u32[]{:S(2)}) copy-start(s32[8]{0:T(128)} %valid_ref.1) | copy-start | bytes 100
  10.0 0.7 %copy-start.5 = (s32[16]{0:T(128)S(1)}, s32[16]{0:T(128)}, u32[]{:S(2)}) copy-start(s32[16]{0:T(128)} %owner_ref.1) | copy-start | bytes 196
  16.3 1.4 %collective-permute-start.4 = (bf16[4,112,128]{2,1,0:T(8,128)(2,1)S(1)}, bf16[4,112,128]{2,1,0:T(8,128)(2,1)S(1)}, u32[]{:S(2)}, u32[]{:S(2)}) collective-permute-start(bf16[4,112,128]{2,1,0:T(8,128)(2,1)S(1)} %get-tuple-element.55), channel_id=1, source_target_pairs={{0,2},{2,0},{4,6},{6,4},{8,10},{10,8},{12,14},{14,12},{16,18},{18,... | collective-permute-start | bytes 344072 | tf_op jit(solution)/shard_map/ppermute | solution.py:382
  17.7 5.4 %collective-permute-start.5 = (bf16[224,128]{1,0:T(8,128)(2,1)S(1)}, bf16[224,128]{1,0:T(8,128)(2,1)S(1)}, u32[]{:S(2)}, u32[]{:S(2)}) collective-permute-start(bf16[224,128]{1,0:T(8,128)(2,1)S(1)} %get-tuple-element.59), channel_id=1, source_target_pairs={{0,4},{2,6},{4,0},{6,2},{8,12},{10,14},{12,8},{14,10},{16,20},{18,... | collective-permute-start | bytes 172040 | tf_op jit(solution)/shard_map/ppermute | solution.py:382
  19.3 4.5 %collective-permute-start.6 = (bf16[224,128]{1,0:T(8,128)(2,1)S(1)}, bf16[224,128]{1,0:T(8,128)(2,1)S(1)}, u32[]{:S(2)}, u32[]{:S(2)}) collective-permute-start(bf16[224,128]{1,0:T(8,128)(2,1)S(1)} %get-tuple-element.60), channel_id=1, source_target_pairs={{0,8},{2,10},{4,12},{6,14},{8,0},{10,2},{12,4},{14,6},{16,24},{18,... | collective-permute-start | bytes 172040 | tf_op jit(solution)/shard_map/ppermute | solution.py:382
  20.9 5.1 %collective-permute-start.7 = (bf16[224,128]{1,0:T(8,128)(2,1)S(1)}, bf16[224,128]{1,0:T(8,128)(2,1)S(1)}, u32[]{:S(2)}, u32[]{:S(2)}) collective-permute-start(bf16[224,128]{1,0:T(8,128)(2,1)S(1)} %get-tuple-element.61), channel_id=1, source_target_pairs={{0,12},{2,14},{4,8},{6,10},{8,4},{10,6},{12,0},{14,2},{16,28},{18,... | collective-permute-start | bytes 172040 | tf_op jit(solution)/shard_map/ppermute | solution.py:382
  26.0 7.6 %collective-permute-start.8 = (bf16[112,128]{1,0:T(8,128)(2,1)S(1)}, bf16[112,128]{1,0:T(8,128)(2,1)S(1)}, u32[]{:S(2)}, u32[]{:S(2)}) collective-permute-start(bf16[112,128]{1,0:T(8,128)(2,1)S(1)} %get-tuple-element.63), channel_id=1, source_target_pairs={{0,17},{1,16},{2,19},{3,18},{4,21},{5,20},{6,23},{7,22},{8,25},{9,... | collective-permute-start | bytes 86024 | tf_op jit(solution)/shard_map/ppermute | solution.py:392
  29.5 5.0 %collective-permute-start.9 = (bf16[112,128]{1,0:T(8,128)(2,1)S(1)}, bf16[112,128]{1,0:T(8,128)(2,1)S(1)}, u32[]{:S(2)}, u32[]{:S(2)}) collective-permute-start(bf16[112,128]{1,0:T(8,128)(2,1)S(1)} %get-tuple-element.63), channel_id=1, source_target_pairs={{0,16},{1,17},{2,18},{3,19},{4,20},{5,21},{6,22},{7,23},{8,24},{9,... | collective-permute-start | bytes 86024 | tf_op jit(solution)/shard_map/ppermute | solution.py:392
  29.8 3.9 %collective-permute-start.10 = (bf16[112,128]{1,0:T(8,128)(2,1)S(1)}, bf16[112,128]{1,0:T(8,128)(2,1)S(1)}, u32[]{:S(2)}, u32[]{:S(2)}) collective-permute-start(bf16[112,128]{1,0:T(8,128)(2,1)S(1)} %get-tuple-element.64), channel_id=1, source_target_pairs={{0,1},{1,0},{2,3},{3,2},{4,5},{5,4},{6,7},{7,6},{8,9},{9,8},{10,11... | collective-permute-start | bytes 86024 | tf_op jit(solution)/shard_map/ppermute | solution.py:392

commit v3 on v2

v3 whole, which is shorter than its diff:
```python
import functools
import math

import jax
import jax.numpy as jnp
from jax import lax
from jax.experimental import pallas as pl
from jax.experimental.pallas import tpu as pltpu
from jax.sharding import PartitionSpec as P

CH = 64
ROW_TAPS = 4
DIL_TAPS = 9
BLOCKS = 14
SHIFTS = [(dr, dc) for dr in (-1, 0, 1) for dc in (-1, 0, 1)]
F32 = jnp.float32
BF16 = jnp.bfloat16
VMEM_LIMIT = 24 * 1024 * 1024


def shift_index(dr, dc):
    return (dr + 1) * 3 + dc + 1


def dot(a, b):
    return lax.dot_general(a, b, (((1,), (0,)), ((), ())), preferred_element_type=F32)


def dot_nt(a, b):
    return lax.dot_general(a, b, (((1,), (1,)), ((), ())), preferred_element_type=F32)


def shifted_masks(side, reach):
    cell = lax.broadcasted_iota(jnp.int32, (1, side * side), 1)
    row, col = cell // side, cell % side
    masks = {}
    for dr, dc in SHIFTS:
        ok = (
            (row + dr * reach >= 0)
            & (row + dr * reach < side)
            & (col + dc * reach >= 0)
            & (col + dc * reach < side)
        )
        masks[dr, dc] = ok.astype(F32).astype(BF16)
    return masks


def shifted(x, dr, dc, side, reach, masks):
    if dr == 0 and dc == 0:
        return x
    cells = side * side
    return pltpu.roll(x, (-(dr * side + dc) * reach) % cells, 1) * masks[dr, dc]


def phase_matrix(side, transposed):
    size = 16 * side
    dims = (size, size)
    source = lax.broadcasted_iota(jnp.int32, dims, 1 if transposed else 0)
    target = lax.broadcasted_iota(jnp.int32, dims, 0 if transposed else 1)
    phase, cell = target // (4 * side), target % (4 * side)
    row, col = cell // side, cell % side
    wanted = (2 * row + phase // 2) * (2 * side) + 2 * col + phase % 2
    return jnp.where(source == wanted, 1.0, 0.0).astype(BF16)


TAP_LINES = {0: (1, -1), 1: (0, 0), 2: (1, 0), 3: (0, 1)}


def tap_matrices(weight, taps, scratch):
    wide = weight.astype(F32)
    scratch[0 : CH * taps, 0:CH] = wide.T
    return [scratch[pl.ds(tap, CH, stride=taps), 0:CH] for tap in range(taps)]


def forward_patch(x_ref, cot, w_strided, w_dilated, bias_col, ph_ref, pre_ref, act_ref, send_ref, im_scr):
    side = math.isqrt(x_ref.shape[1]) // 2
    run, lanes = 16 * side, side * side // 128
    split = phase_matrix(side, False)
    near, far = shifted_masks(side, 1), shifted_masks(side, 2)
    runs = x_ref.shape[1] // run
    stacked = jnp.concatenate([x_ref[:, q * run : (q + 1) * run] for q in range(runs)], axis=0)
    parts = dot(stacked, split).astype(BF16)
    for q in range(runs):
        for phase in range(4):
            ph_ref[phase * CH : (phase + 1) * CH, q * 4 * side : (q + 1) * 4 * side] = parts[
                q * CH : (q + 1) * CH, phase * 4 * side : (phase + 1) * 4 * side
            ]
    for rt in range(4):
        for ct in range(4):
            (pr, dr), (pc, dc) = TAP_LINES[rt], TAP_LINES[ct]
            phase, tap = pr * 2 + pc, rt * 4 + ct
            im_scr[tap * CH : (tap + 1) * CH, :] = shifted(
                ph_ref[phase * CH : (phase + 1) * CH, :], dr, dc, side, 1, near
            )
    pre = dot(w_strided, im_scr[...]) + bias_col
    pre_ref[...] = pre
    act = (pre * (1.0 / (1.0 + jnp.exp(-pre)))).astype(BF16)
    act_ref[...] = act
    for tap, (dr, dc) in enumerate(SHIFTS):
        im_scr[tap * CH : (tap + 1) * CH, :] = shifted(act, dr, dc, side, 2, far)
    out = dot(w_dilated, im_scr[0 : DIL_TAPS * CH, :]).astype(BF16)
    for lane in range(lanes):
        send_ref[lane * CH : (lane + 1) * CH, :] = out[:, lane * 128 : (lane + 1) * 128]
    rows = [cot[:, lane * 128 : (lane + 1) * 128] for lane in range(lanes)]
    rows.append(jnp.zeros((16 - lanes, 128), F32))
    send_ref[lanes * CH :, :] = jnp.concatenate(rows, axis=0).astype(BF16)


def first_kernel(
    owner_hbm, x_hbm, ws_hbm, wd_hbm, bias_hbm, cot_hbm,
    ph_ref, pre_ref, act_ref, send_ref, strided_ref, dilated_ref, bias_ref,
    x_ref, ws_ref, wd_ref, cot_ref, table_ref, owner_ref, wscr, im_scr, sems,
):
    scene = lax.axis_index("scene")
    branch = scene % 2
    copies = [
        pltpu.make_async_copy(source, target, sems.at[i])
        for i, (source, target) in enumerate(
            [
                (x_hbm.at[0], x_ref),
                (ws_hbm.at[branch], ws_ref),
                (wd_hbm.at[branch], wd_ref),
                (owner_hbm, owner_ref),
                (bias_hbm, table_ref),
                (cot_hbm, cot_ref),
            ]
        )
    ]
    for copy in copies:
        copy.start()
    for copy in copies:
        copy.wait()
    mats = tap_matrices(ws_ref[...], 16, wscr)
    strided_ref[...] = jnp.concatenate(mats, axis=0).T.astype(BF16)
    mats = tap_matrices(wd_ref[...], 9, wscr)
    dilated_ref[...] = jnp.concatenate(mats, axis=0).T.astype(BF16)
    bias_row = table_ref[pl.ds(owner_ref[scene], 1), :]
    bias_ref[...] = jnp.broadcast_to(jnp.broadcast_to(bias_row, (8, CH)).T[:, 0:1], (CH, 128))
    forward_patch(
        x_ref, cot_ref[...].astype(F32)[0:1, :], strided_ref[...], dilated_ref[...], bias_ref[:, 0:1],
        ph_ref, pre_ref, act_ref, send_ref, im_scr,
    )


def later_kernel(
    x_ref, cot_ref, w_strided_ref, w_dilated_ref, bias_ref, sent_ref,
    ph_ref, pre_ref, act_ref, send_ref, both_ref, im_scr,
):
    forward_patch(
        x_ref.at[1], cot_ref[...].astype(F32)[1:2, :], w_strided_ref[...], w_dilated_ref[...],
        bias_ref[:, 0:1], ph_ref, pre_ref, act_ref, send_ref, im_scr,
    )
    both_ref[0] = sent_ref[...]
    both_ref[1] = send_ref[...]


def prepare_kernel(
    pairing_hbm, valid_hbm, owner_hbm, ws_ref, wd_ref, *refs, bias_rows
):
    pre_refs, act_refs, ph_refs, send_refs = (refs[2 * k : 2 * k + 2] for k in range(4))
    (
        slope_first, slope_second, act_first, act_second, ph_first, ph_second,
        wf_ref, wt_ref, select_ref, place_ref, cot_ref,
        pairing_ref, valid_ref, owner_ref, wscr, sems,
    ) = refs[8:]
    copies = [
        pltpu.make_async_copy(source, target, sems.at[i])
        for i, (source, target) in enumerate(
            [(pairing_hbm, pairing_ref), (valid_hbm, valid_ref), (owner_hbm, owner_ref)]
        )
    ]
    for copy in copies:
        copy.start()
    scene, tile = lax.axis_index("scene"), lax.axis_index("tile")
    branch, pair = scene % 2, scene // 2
    mats = tap_matrices(ws_ref[branch], 16, wscr)
    blocks = {}
    for rt in range(4):
        for ct in range(4):
            (pr, dr), (pc, dc) = TAP_LINES[rt], TAP_LINES[ct]
            blocks[pr * 2 + pc, shift_index(-dr, -dc)] = mats[rt * 4 + ct]
    zero = jnp.zeros((CH, CH), F32)
    for phase in range(4):
        row = [blocks.get((phase, s), zero) for s in range(9)]
        wf_ref[phase * CH : (phase + 1) * CH, :] = jnp.concatenate(row, axis=1).astype(BF16)
    mats = tap_matrices(wd_ref[branch], 9, wscr)
    wt_ref[...] = jnp.concatenate(mats[::-1], axis=1).astype(BF16)
    slopes = []
    for pre_ref in pre_refs:
        pre = pre_ref[...]
        gate = 1.0 / (1.0 + jnp.exp(-pre))
        slopes.append(gate * (1.0 + pre * (1.0 - gate)))
    for copy in copies:
        copy.wait()
    total = pairing_ref.shape[0]
    matches = []
    for p in range(2):
        position = tile * 2 + p
        matched, inverse = pairing_ref[position, pair], jnp.int32(0)
        for i in range(total):
            inverse = inverse + jnp.where(pairing_ref[i, pair] == position, i, 0)
        matched = jnp.where(branch == 0, matched, inverse)
        matches.append(jnp.where(matched // 2 == tile, 0, 2) + matched % 2)
    swapped = matches[0] == 3
    slope_first[...] = jnp.where(swapped, slopes[1], slopes[0])
    slope_second[...] = jnp.where(swapped, slopes[0], slopes[1])
    for first, second, pairs in ((act_first, act_second, act_refs), (ph_first, ph_second, ph_refs)):
        first[...] = jnp.where(swapped, pairs[1][...], pairs[0][...])
        second[...] = jnp.where(swapped, pairs[0][...], pairs[1][...])
    rows = send_refs[0].shape[0] - 16
    cots = [ref[rows:, :].astype(F32) for ref in send_refs]
    cot_ref[0:16, :] = jnp.where(swapped, cots[1], cots[0])
    cot_ref[16:32, :] = jnp.where(swapped, cots[0], cots[1])
    row = lax.broadcasted_iota(jnp.int32, select_ref.shape, 0)
    select = jnp.zeros(select_ref.shape, F32)
    for p in range(2):
        position = jnp.where(swapped, 1 - p, p)
        live = jnp.where(tile * 2 + p < valid_ref[pair], 8 + position, -1)
        select = jnp.where((row == position * 4 + matches[p]) | (row == live), 1.0, select)
    select_ref[...] = jnp.where(row == jnp.where(swapped, 10, -1), 1.0, select)
    row = lax.broadcasted_iota(jnp.int32, place_ref.shape, 0)
    here = scene // 2 % 4
    place = jnp.zeros(place_ref.shape, F32)
    for k, source in enumerate((scene, scene ^ 1)):
        owner = owner_ref[source]
        target = owner // (2 * bias_rows)
        half = jnp.where(target // 8 == branch, 0, 1)
        wanted = k * 64 + ((target // 2 % 4) ^ here) * 16 + half * 8 + owner % (2 * bias_rows)
        place = jnp.where(row == jnp.where(target % 2 == branch, wanted, -1), 1.0, place)
    place_ref[...] = place


def strided_product(pre_b, ph_ref, shift_scr):
    side = math.isqrt(pre_b.shape[1])
    near = shifted_masks(side, 1)
    for s, (dr, dc) in enumerate(SHIFTS):
        shift_scr[s * CH : (s + 1) * CH, :] = shifted(pre_b, dr, dc, side, 1, near)
    return dot_nt(shift_scr[...], ph_ref[...])


def backward_patch(position, candidates, select_ref, cot_ref, wt_ref, act_ref, slope_ref, shift_scr):
    side = math.isqrt(act_ref.shape[1])
    lanes = side * side // 128
    far = shifted_masks(side, 2)
    partner = None
    for k, payload in enumerate(candidates):
        term = payload * select_ref[position * 4 + k : position * 4 + k + 1, :].astype(BF16)
        partner = term if partner is None else partner + term
    live = select_ref[8 + position : 9 + position, :]
    signal = (cot_ref[position * 16 : position * 16 + 16, :] + partner[lanes * CH :, :].astype(F32)) * live
    out_grad = jnp.concatenate(
        [
            (signal[j : j + 1, :] * partner[j * CH : (j + 1) * CH, :].astype(F32)).astype(BF16)
            for j in range(lanes)
        ],
        axis=1,
    )
    for tap, (dr, dc) in enumerate(SHIFTS):
        shift_scr[tap * CH : (tap + 1) * CH, :] = shifted(out_grad, dr, dc, side, 2, far)
    act_grad = dot(wt_ref[...], shift_scr[...])
    act = act_ref[...]
    dilated = dot_nt(shift_scr[...], jnp.concatenate([act, act], axis=0))
    pre_grad = act_grad * slope_ref[...]
    bias = jnp.sum(pre_grad, axis=1, keepdims=True)
    return pre_grad.astype(BF16), bias, dilated


def backward_first_kernel(
    far0_ref, near_ref, select_ref, cot_ref, wt_ref, act_ref, slope_ref, ph_ref,
    pre_b_ref, bias_ref, dilated_ref, strided_ref, shift_scr,
):
    pre_b, bias, dilated = backward_patch(
        0, (near_ref[0], near_ref[1], far0_ref[...]), select_ref, cot_ref, wt_ref, act_ref, slope_ref, shift_scr
    )
    pre_b_ref[...] = pre_b
    bias_ref[...] = jnp.broadcast_to(bias, bias_ref.shape)
    dilated_ref[...] = dilated
    strided_ref[...] = strided_product(pre_b, ph_ref, shift_scr)


def backward_second_kernel(
    far1_ref, far0_ref, near_ref, select_ref, cot_ref, wt_ref, act_ref, slope_ref, ph_ref,
    other_ref, bias_ref, dilated_ref, strided_ref, *refs, chunked,
):
    pre_b0_ref, pre_b1_ref = refs[:2]
    if chunked:
        keep_ref, give_ref, shift_scr, dil_scr, grad_acc, grad_scr = refs[2:]
    else:
        grad_scr, bias_out_ref, shift_scr, dil_scr, grad_acc = refs[2:]
    pre_b, bias, dilated = backward_patch(
        1, (near_ref[0], near_ref[1], far0_ref[...], far1_ref[...]),
        select_ref, cot_ref, wt_ref, act_ref, slope_ref, shift_scr,
    )
    swapped = select_ref[10:11, 0:1].astype(BF16)
    straight = 1.0 - swapped
    pre_b0_ref[...] = other_ref[...] * straight + pre_b * swapped
    pre_b1_ref[...] = other_ref[...] * swapped + pre_b * straight
    dil_scr[...] = dilated + dilated_ref[...]
    grad_acc[...] = strided_product(pre_b, ph_ref, shift_scr) + strided_ref[...]
    lower = lax.broadcasted_iota(jnp.int32, (CH, 2 * CH), 1) < CH

    def strided_piece(pr, shift):
        return grad_acc[shift * CH : (shift + 1) * CH, pr * 2 * CH : (pr + 1) * 2 * CH]

    for rt in range(4):
        pr, dr = TAP_LINES[rt]
        for k in range(2):
            low_dc, high_dc = (0, 0) if k == 0 else (1, -1)
            low = strided_piece(pr, shift_index(-dr, -low_dc))
            high = strided_piece(pr, shift_index(-dr, -high_dc))
            grad_scr[rt * 2 + k] = low if k == 0 else jnp.where(lower, low, high)
    for j in range(5):
        low = dil_scr[(8 - 2 * j) * CH : (9 - 2 * j) * CH, :]
        high = dil_scr[(7 - 2 * j) * CH : (8 - 2 * j) * CH, :] if j < 4 else jnp.zeros_like(low)
        grad_scr[8 + j] = jnp.where(lower, low, high)
    bias_wide = (bias + bias_ref[...]).T[0:8, :]
    bias_wide = jnp.concatenate([bias_wide, jnp.zeros_like(bias_wide)], axis=1)
    if not chunked:
        bias_out_ref[...] = bias_wide
        return
    scene = lax.axis_index("scene")
    here, branch = scene // 2 % 4, scene % 2
    for ref, core in ((keep_ref, branch), (give_ref, 1 - branch)):
        for d in range(4):
            row = pl.multiple_of(((here ^ d) * 2 + core) * 8, 8)
            pieces = [grad_scr[block, pl.ds(row, 8), :] for block in range(BLOCKS - 1)]
            ref[d] = jnp.concatenate(pieces + [bias_wide], axis=0).astype(BF16)


def spread_kernel(place_ref, keep_ref, got_ref, *out_refs):
    rows = keep_ref.shape[1]
    top = lax.broadcasted_iota(jnp.int32, (16, 128), 0) < 8
    mine = keep_ref[0, rows - 16 :, :].astype(F32)[8:9, :]
    theirs = got_ref[0, rows - 16 :, :].astype(F32)[8:9, :]
    for d, out_ref in enumerate(out_refs):
        for half, ref in enumerate((keep_ref, got_ref)):
            at = d * 16 + half * 8
            bias = place_ref[at : at + 8, :] * mine + place_ref[64 + at : 72 + at, :] * theirs
            last = ref[d, rows - 16 :, :].astype(F32)
            last = jnp.where(top, last, jnp.concatenate([bias, bias], axis=0))
            out_ref[half * rows : (half + 1) * rows - 16, :] = ref[d, : rows - 16, :]
            out_ref[(half + 1) * rows - 16 : (half + 1) * rows, :] = last.astype(BF16)


def join_kernel(own_ref, a_ref, b_ref, c_ref, keep_ref, stay_ref, cross_ref):
    scene = lax.axis_index("scene")
    rows = keep_ref.shape[0]
    total = (own_ref[...].astype(F32) + a_ref[...].astype(F32)) + (
        b_ref[...].astype(F32) + c_ref[...].astype(F32)
    )
    mine, theirs = total[:rows, :], total[rows:, :]
    first = scene // 8 == scene % 2
    kept = jnp.where(first, mine, theirs)
    keep_ref[...] = kept
    stay_ref[...] = kept.astype(BF16)
    cross_ref[...] = jnp.where(first, theirs, mine).astype(BF16)


def finish_kernel(
    own_ref, a_ref, b_ref, c_ref, late_ref, features_in_hbm, weights_hbm, bias_hbm, features_hbm,
    weights_ref, bias_ref, tap_scr, turn_scr, dilated_scr, sems, *, weight_scale, bias_scale,
):
    tile = lax.axis_index("tile")
    late = pltpu.make_async_copy(late_ref, features_hbm.at[1], sems.at[0])
    late.start()
    total = (own_ref[...] + a_ref[...].astype(F32)) + (b_ref[...].astype(F32) + c_ref[...].astype(F32))
    bias = total[(BLOCKS - 1) * 8 :, :] * bias_scale
    index = lax.broadcasted_iota(jnp.int32, bias.shape, 0)
    bias_ref[...] = jnp.sum(jnp.where(index == tile, bias, 0.0), axis=0, keepdims=True)[:, 0:CH]
    bias_out = pltpu.make_async_copy(bias_ref, bias_hbm, sems.at[1])
    bias_out.start()
    total = total * weight_scale
    other = pltpu.roll(total, CH, 1)
    for block in range(8):
        for half, source in enumerate((total, other)):
            tap = block // 2 * 4 + ((1, 2), (3, 0))[block % 2][half]
            tap_scr[pl.ds(tap, 8, stride=16), :] = source[block * 8 : block * 8 + 8, :]
    lines = tap_scr[...].T[0:CH, :].reshape(8, 8, 128)
    sub = lax.broadcasted_iota(jnp.int32, lines.shape, 1)
    chunk = lax.broadcasted_iota(jnp.int32, lines.shape, 2) // 16
    for step in (1, 2, 4):
        up = pltpu.roll(pltpu.roll(lines, 8 - step, 1), 16 * step, 2)
        down = pltpu.roll(pltpu.roll(lines, step, 1), 128 - 16 * step, 2)
        high, wide = sub // step % 2, chunk // step % 2
        lines = jnp.where(high == wide, lines, jnp.where(high == 0, up, down))
    for block in range(8):
        weights_ref[:, block * 128 : (block + 1) * 128] = lines[block]
    strided_part, dilated_part = pl.ds(0, 16 * CH), pl.ds(16 * CH, DIL_TAPS * CH)
    strided_out = pltpu.make_async_copy(weights_ref.at[:, strided_part], weights_hbm.at[:, strided_part], sems.at[2])
    strided_out.start()
    turn_scr[0:40, :] = total[64:104, :]
    turned = turn_scr[...].T
    for tap in range(DIL_TAPS):
        half = tap % 2
        dilated_scr[pl.ds(tap, CH, stride=DIL_TAPS), :] = turned[half * CH : (half + 1) * CH, :]
    spread = dilated_scr[...].T
    tap = lax.broadcasted_iota(jnp.int32, (8, DIL_TAPS * CH), 1) % DIL_TAPS
    result = spread[0:8, :]
    for j in range(1, 5):
        result = jnp.where(tap // 2 == j, spread[8 * j : 8 * j + 8, :], result)
    weights_ref[:, 16 * CH :] = result
    dilated_out = pltpu.make_async_copy(weights_ref.at[:, dilated_part], weights_hbm.at[:, dilated_part], sems.at[3])
    dilated_out.start()
    for copy in (late, bias_out, strided_out, dilated_out):
        copy.wait()


def feature_patch(pre_b_ref, wf_ref, out_ref, shift_scr):
    side = math.isqrt(pre_b_ref.shape[1])
    near = shifted_masks(side, 1)
    merge = phase_matrix(side, True)
    run, wide = 16 * side, 4 * side
    pre_b = pre_b_ref[...]
    for s, (dr, dc) in enumerate(SHIFTS):
        shift_scr[s * CH : (s + 1) * CH, :] = shifted(pre_b, dr, dc, side, 1, near)
    phases = dot(wf_ref[...], shift_scr[...]).astype(BF16)
    runs = out_ref.shape[1] // run
    stacked = jnp.concatenate(
        [
            jnp.concatenate(
                [phases[k * CH : (k + 1) * CH, q * wide : (q + 1) * wide] for k in range(4)], axis=1
            )
            for q in range(runs)
        ],
        axis=0,
    )
    merged = dot(stacked, merge).astype(BF16)
    for q in range(runs):
        out_ref[:, q * run : (q + 1) * run] = merged[q * CH : (q + 1) * CH, :]


def feature_first_kernel(pre_b_ref, wf_ref, out_ref, shift_scr):
    feature_patch(pre_b_ref, wf_ref, out_ref, shift_scr)


def feature_second_kernel(pre_b_ref, wf_ref, first_ref, out_ref, features_hbm, shift_scr, sem):
    copy = pltpu.make_async_copy(first_ref, features_hbm.at[0], sem)
    copy.start()
    feature_patch(pre_b_ref, wf_ref, out_ref, shift_scr)
    copy.wait()


SPACES = {"s": pltpu.SMEM, "v": pltpu.VMEM, "h": pltpu.HBM, "a": pl.ANY}


def call(kernel, outs, ins, scratch, *args, flops=0, out_spaces="", aliases=None):
    args = [
        pltpu.with_memory_space_constraint(arg, pltpu.HBM) if space == "h" else arg
        for space, arg in zip(ins, args)
    ]
    return pl.pallas_call(
        kernel,
        out_shape=[jax.ShapeDtypeStruct(shape, kind) for shape, kind in outs],
        in_specs=[pl.BlockSpec(memory_space=SPACES[space]) for space in ins],
        out_specs=[pl.BlockSpec(memory_space=SPACES[space]) for space in out_spaces or "v" * len(outs)],
        scratch_shapes=[pltpu.VMEM(*item) if isinstance(item, tuple) else item for item in scratch],
        input_output_aliases=aliases or {},
        compiler_params=pltpu.CompilerParams(vmem_limit_bytes=VMEM_LIMIT),
        cost_estimate=pl.CostEstimate(flops=flops, bytes_accessed=1 << 20, transcendentals=0),
    )(*args)


def device_pairs(x, pairs):
    tiles = lax.axis_size("tile")
    flat = [(source[0] * tiles + source[1], target[0] * tiles + target[1]) for source, target in pairs]
    return lax.ppermute(x, ("scene", "tile"), flat)


def scene_xor(x, distance):
    return lax.ppermute(x, "scene", [(i, i ^ distance) for i in range(lax.axis_size("scene"))])


def device_xor(x, scene_distance, tile_distance):
    scenes, tiles = range(lax.axis_size("scene")), range(lax.axis_size("tile"))
    return device_pairs(
        x, [((s, t), (s ^ scene_distance, t ^ tile_distance)) for s in scenes for t in tiles]
    )


def reduce_anywhere(blocks, bias_row, tile_owner, bias_rows, weight_scale, bias_scale):
    channels = blocks.shape[1]
    scene = lax.axis_index("scene")
    scenes, tiles = lax.axis_size("scene"), lax.axis_size("tile")
    halves = blocks.reshape(BLOCKS - 1, channels, 2, channels)
    strided, dilated = [None] * 16, []
    for block in range(8):
        for half in range(2):
            strided[block // 2 * 4 + ((1, 2), (3, 0))[block % 2][half]] = halves[block, :, half]
    for tap in range(DIL_TAPS):
        dilated.append(halves[8 + tap // 2, :, tap % 2])
    row = jnp.concatenate(
        [
            jnp.stack(strided, axis=-1).reshape(channels, 16 * channels),
            jnp.stack(dilated, axis=-1).reshape(channels, DIL_TAPS * channels),
        ],
        axis=1,
    )
    hit = jnp.arange(2, dtype=jnp.int32)[:, None, None] == scene % 2
    term = jnp.where(hit, row[None] * weight_scale, 0.0).reshape(2 * channels, 25 * channels)
    weights = lax.psum(lax.psum_scatter(term, "scene", scatter_dimension=0, tiled=True), "tile")
    tile_id = lax.dynamic_index_in_dim(tile_owner, scene, 0, keepdims=False)
    owned = jnp.arange(scenes * tiles * bias_rows, dtype=jnp.int32) == tile_id
    bias = jnp.where(owned[:, None], bias_row[None, :channels] * bias_scale, 0.0)
    return weights, lax.psum_scatter(bias, ("scene", "tile"), scatter_dimension=0, tiled=True)


def local(
    features_in,
    strided_weights,
    dilated_weights,
    tile_bias,
    cost_cotangent,
    footprint_pairing,
    valid_counts,
    tile_owner,
):
    features, own_cot = features_in[0], cost_cotangent[0]
    patches, channels, cells_in = features.shape
    cells = own_cot.shape[1]
    scenes, tiles = lax.axis_size("scene"), lax.axis_size("tile")
    weight_scale = 1.0 / math.sqrt(scenes * patches * tiles * cells)
    bias_scale = 1.0 / math.sqrt(patches * tiles * cells)
    bias_rows = tile_bias.shape[0] // (scenes * tiles)
    grid = (channels, cells)
    payload = (cells * channels // 128 + 16, 128)
    chunked = scenes == 16 and tiles == 2 and patches == 2 and bias_rows == 1
    wscr = ((16 * channels, 2 * channels), F32)
    im_scr = ((16 * channels, cells), BF16)
    patch_outs = [((4 * channels, cells), BF16), (grid, F32), (grid, BF16), (payload, BF16)]
    first_outs = patch_outs + [
        ((channels, 16 * channels), BF16),
        ((channels, 9 * channels), BF16),
        ((channels, 128), F32),
    ]
    *part, w_strided, w_dilated, bias_col = call(
        first_kernel,
        first_outs,
        "hhhhhh",
        [
            ((channels, cells_in), BF16),
            (strided_weights.shape[1:], BF16),
            (dilated_weights.shape[1:], BF16),
            (own_cot.shape, BF16),
            (tile_bias.shape, F32),
            pltpu.SMEM(tile_owner.shape, jnp.int32),
            wscr,
            im_scr,
            pltpu.SemaphoreType.DMA((6,)),
        ],
        tile_owner, features, strided_weights, dilated_weights, tile_bias, own_cot,
        flops=10**9,
    )
    far = [device_xor(part[3], 1, 1)]
    *late, both = call(
        later_kernel,
        patch_outs + [((2,) + payload, BF16)],
        "vvvvvv",
        [im_scr],
        features, own_cot, w_strided, w_dilated, bias_col, part[3],
        flops=10**10,
    )
    far.append(device_xor(late[3], 1, 1))
    near = scene_xor(both, 1)
    phases, pre, act, send = zip(part, late)
    ordered = [(grid, F32)] * 2 + [(grid, BF16)] * 2 + [((4 * channels, cells), BF16)] * 2
    *both, w_feature, w_act, select, place, cots = call(
        functools.partial(prepare_kernel, bias_rows=bias_rows),
        ordered
        + [
            ((4 * channels, 9 * channels), BF16),
            ((channels, 9 * channels), BF16),
            ((16, 128), F32),
            ((128, 128), F32),
            ((32, 128), F32),
        ],
        "hhhvvvvvvvvvv",
        [
            pltpu.SMEM(footprint_pairing.shape[::-1], jnp.int32),
            pltpu.SMEM(valid_counts.shape, jnp.int32),
            pltpu.SMEM(tile_owner.shape, jnp.int32),
            wscr,
            pltpu.SemaphoreType.DMA((3,)),
        ],
        footprint_pairing.T, valid_counts, tile_owner, strided_weights, dilated_weights,
        *pre, *act, *phases, *send,
        flops=10**10,
    )
    slope, act, phases = both[0:2], both[2:4], both[4:6]
    shift_scr = ((9 * channels, cells), BF16)
    sums = [((9 * channels, 128), F32), ((9 * channels, 4 * channels), F32)]
    first = call(
        backward_first_kernel,
        [(grid, BF16), ((channels, 128), F32)] + sums,
        "v" * 8,
        [shift_scr],
        far[0], near, select, cots, w_act, act[0], slope[0], phases[0],
        flops=10**9,
    )
    block_shape = ((BLOCKS - 1, channels, 128), F32)
    half_shape = ((4, BLOCKS * 8, 128), BF16)
    results = call(
        functools.partial(backward_second_kernel, chunked=chunked),
        [(grid, BF16)] * 2 + ([half_shape] * 2 if chunked else [block_shape, ((8, 128), F32)]),
        "v" * 13,
        [shift_scr] + sums + ([block_shape] if chunked else []),
        far[1], far[0], near, select, cots, w_act, act[1], slope[1], phases[1], *first,
        flops=10**9,
    )
    pre_b, grads = results[:2], results[2:]
    feature_shape = ((channels, cells_in), BF16)
    if chunked:
        keep, give = grads
        got = scene_xor(give, 1)
        stage = ((2 * BLOCKS * 8, 128), BF16)
        own, by_y, by_z, by_zy = call(spread_kernel, [stage] * 4, "vvv", [], place, keep, got)
        by_zy, by_z, by_y = scene_xor(by_zy, 6), scene_xor(by_z, 4), scene_xor(by_y, 2)
    (feature_first,) = call(
        feature_first_kernel, [feature_shape], "vv", [shift_scr], pre_b[0], w_feature, flops=10**9
    )
    chunk = (BLOCKS * 8, 128)
    if chunked:
        feature_first, own = lax.optimization_barrier((feature_first, own))
        kept, stay, cross = call(
            join_kernel, [(chunk, F32), (chunk, BF16), (chunk, BF16)], "vvvv", [], own, by_zy, by_z, by_y
        )
        by_zx, by_z, by_x = device_xor(cross, 8, 1), device_xor(cross, 8, 0), device_xor(stay, 0, 1)
    feature_last, feature_grads = call(
        feature_second_kernel,
        [feature_shape, (features.shape, BF16)],
        "vvv",
        [shift_scr, pltpu.SemaphoreType.DMA],
        pre_b[1], w_feature, feature_first,
        flops=10**9,
        out_spaces="vh",
    )
    if not chunked:
        feature_grads = feature_grads.at[1].set(feature_last)
        grad_weights, grad_bias = reduce_anywhere(
            grads[0], grads[1][0], tile_owner, bias_rows, weight_scale, bias_scale
        )
        return (feature_grads[None], grad_weights, grad_bias)
    grad_weights, grad_bias, feature_grads = call(
        functools.partial(finish_kernel, weight_scale=weight_scale, bias_scale=bias_scale),
        [((8, 25 * channels), F32), ((1, channels), F32), (features.shape, BF16)],
        "vvvvva",
        [
            ((8, 25 * channels), F32),
            ((1, channels), F32),
            ((128, 128), F32),
            ((128, 128), F32),
            ((9 * channels, 128), F32),
            pltpu.SemaphoreType.DMA((4,)),
        ],
        kept, by_zx, by_z, by_x, feature_last, feature_grads,
        out_spaces="hhh",
        aliases={5: 2},
    )
    return (feature_grads[None], grad_weights, grad_bias)


def solution(mesh):
    return jax.shard_map(
        local,
        mesh=mesh,
        in_specs=(
            P("scene", "tile", None, None),
            P(),
            P(),
            P(),
            P("scene", "tile", None),
            P(),
            P(),
            P(),
        ),
        out_specs=(P("scene", "tile", None, None), P("scene", None), P(("scene", "tile"), None)),
        check_vma=False,
    )
```

time: 35.8 us -> 33.7 us (0.941)
  Pallas kernels: 13.1 us -> 11.4 us
  waiting for transfers between devices: 8.01 us -> 9.46 us
  starting transfers between devices: 13 us -> 12 us
  local copies, waits for them, and re-layouts: 0.77 us -> 0.02 us
    pallas_call x9 -> x10, Pallas kernels: 13.1 us -> 11.4 us  [call(): pl.pallas_call(kernel, out_shape=[jax.ShapeDtypeStruct(shape, kind) for s...]
    ppermute x5, waiting for transfers between devices: 4.21 us -> 5.6 us  [device_pairs(): return lax.ppermute(x, ('scene', 'tile'), flat)]
    ppermute x5, starting transfers between devices: 8.33 us -> 7.51 us  [device_pairs(): return lax.ppermute(x, ('scene', 'tile'), flat)]
    unnamed x15 -> x8, local copies, waits for them, and re-layouts: 0.77 us -> 0.02 us
    ppermute x6 -> x5, starting transfers between devices: 4.68 us -> 4.47 us  [scene_xor(): lax.ppermute(x, 'scene', [(i, i ^ distance) for i in range(lax.axis_size(...]
    ppermute x6 -> x5, waiting for transfers between devices: 3.8 us -> 3.86 us  [scene_xor(): lax.ppermute(x, 'scene', [(i, i ^ distance) for i in range(lax.axis_size(...]
  transfers between devices with their start and end apart: 11 -> 10, of which waited for: 6 -> 8; matrix products, arithmetic and copies ran while one was open for 0% -> 0% of each run, Pallas kernels for 18% -> 17%
where the time goes in v3:
time: 33.7 us; the launch traced here: 33.5 us
  starting transfers between devices  12 us (36%)
  Pallas kernels  11.4 us (34%)
  waiting for transfers between devices  9.46 us (28%)
  between operations  0.72 us (2%)
    pallas_call x10, Pallas kernels, call(): pl.pallas_call(kernel, out_shape=[jax.ShapeDtypeStruct(shape, kind) for s...  11.4 us
    ppermute x5, starting transfers between devices, device_pairs(): return lax.ppermute(x, ('scene', 'tile'), flat)  7.51 us
    ppermute x5, waiting for transfers between devices, device_pairs(): return lax.ppermute(x, ('scene', 'tile'), flat)  5.6 us
    ppermute x5, starting transfers between devices, scene_xor(): lax.ppermute(x, 'scene', [(i, i ^ distance) for i in range(lax.axis_size(...  4.47 us
    ppermute x5, waiting for transfers between devices, scene_xor(): lax.ppermute(x, 'scene', [(i, i ^ distance) for i in range(lax.axis_size(...  3.86 us
  transfers between devices with their start and end apart: 10, of which 8 were waited for; matrix products, arithmetic and copies ran while one was open for 0% of the time, Pallas kernels for 17%

profile of v3, /device:TPU:0, one launch (start us, length us, event | category | flops | bytes accessed | tf_op | source)
XLA Modules:
  0.0 33.5 jit_solution(8427234483976009028)
XLA Ops:
  0.6 0.0 copy-start
  0.6 3.0 %shard_map.103 = (bf16[256,1024]{1,0:T(8,128)(2,1)S(1)}, f32[64,1024]{1,0:T(8,128)S(1)}, bf16[64,1024]{1,0:T(8,128)(2,1)S(1)}, bf16[528,128]{1,0:T(8,128)(2,1)S(...) custom-call(s32[16]{0:T(128)} %owner_hbm.3, bf16[2,64,4096]{2,1,0:T(8,128)(2,1)} %bitcast.4, ...), custom_call_target="tpu_custom_call" | custom-call | flops 1000000000 | bytes 1048576 | tf_op jit(solution)/shard_map/pallas_call | solution.py:451
  3.6 0.0 copy-start.3
  3.6 2.4 %collective-permute-start.1 = (bf16[528,128]{1,0:T(8,128)(2,1)S(1)}, bf16[528,128]{1,0:T(8,128)(2,1)S(1)}, u32[]{:S(2)}, u32[]{:S(2)}) collective-permute-start(bf16[528,128]{1,0:T(8,128)(2,1)S(1)} %get-tuple-element.51.sent_ref.refs_6_), channel_id=1, source_target_pairs={{0,3},{1,2},{2,1},{3,0},{4,7},{5,6},{6,5},{7,4},{8,11},{9,10},{10,... | collective-permute-start | bytes 405512 | tf_op jit(solution)/shard_map/ppermute | solution.py:466
  6.1 0.0 copy-done
  6.1 0.0 copy-done.3
  6.1 1.5 %shard_map.104 = (bf16[256,1024]{1,0:T(8,128)(2,1)S(1)}, f32[64,1024]{1,0:T(8,128)S(1)}, bf16[64,1024]{1,0:T(8,128)(2,1)S(1)}, bf16[528,128]{1,0:T(8,128)(2,1)S(1)}, bf16[2,528,128]{2,1,0:T(8,128)(2,1)S(1)}) custom-call(bf16[2,64,4096]{2,1,0:T(8,128)(2,1)S(1)} %bitcast.5, bf16[2,1024]{1,0:T(2,128)(2,1)S(1)} %bitcast.7, ...), custom_call_target="tpu_custom_call" | custom-call | flops 10000000000 | bytes 1048576 | tf_op jit(solution)/shard_map/pallas_call | solution.py:451
  7.6 0.7 %collective-permute-start.2 = (bf16[2,528,128]{2,1,0:T(8,128)(2,1)S(1)}, bf16[2,528,128]{2,1,0:T(8,128)(2,1)S(1)}, u32[]{:S(2)}, u32[]{:S(2)}) collective-permute-start(bf16[2,528,128]{2,1,0:T(8,128)(2,1)S(1)} %get-tuple-element.53), channel_id=1, source_target_pairs={{0,2},{2,0},{4,6},{6,4},{8,10},{10,8},{12,14},{14,12},{16,18},{18,... | collective-permute-start | bytes 811016 | tf_op jit(solution)/shard_map/ppermute | solution.py:470
  8.3 0.6 %collective-permute-start = (bf16[528,128]{1,0:T(8,128)(2,1)S(1)}, bf16[528,128]{1,0:T(8,128)(2,1)S(1)}, u32[]{:S(2)}, u32[]{:S(2)}) collective-permute-start(bf16[528,128]{1,0:T(8,128)(2,1)S(1)} %get-tuple-element.52.refs_7_), channel_id=1, source_target_pairs={{0,3},{1,2},{2,1},{3,0},{4,7},{5,6},{6,5},{7,4},{8,11},{9,10},{10,... | collective-permute-start | bytes 405512 | tf_op jit(solution)/shard_map/ppermute | solution.py:466
  8.9 1.0 %shard_map.105 = (f32[64,1024]{1,0:T(8,128)S(1)}, f32[64,1024]{1,0:T(8,128)S(1)}, bf16[64,1024]{1,0:T(8,128)(2,1)S(1)}, bf16[64,1024]{1,0:T(8,128)(2,1)S(1)}, bf...) custom-call(s32[4,8]{1,0:T(4,128)} %bitcast.9, ...), custom_call_target="tpu_custom_call" | custom-call | flops 10000000000 | bytes 1048576 | tf_op jit(solution)/shard_map/pallas_call | solution.py:451
  9.9 0.1 collective-permute-done.1.far0_ref
  10.0 0.0 collective-permute-done.2.near_ref
  10.0 1.2 %shard_map.106 = (bf16[64,1024]{1,0:T(8,128)(2,1)S(1)}, f32[64,128]{1,0:T(8,128)S(1)}, f32[576,128]{1,0:T(8,128)S(1)}, f32[576,256]{1,0:T(8,128)S(1)}) custom-call(bf16[528,128]{1,0:T(8,128)(2,1)S(1)} %collective-permute-done.1.far0_ref, bf16[2,528,128]{2,1,0:T(8,128)(2,1)S(1)} %collective-permute-done.2.near_ref, ...), custom_call_target="tpu_custom_call" | custom-call | flops 1000000000 | bytes 1048576 | tf_op jit(solution)/shard_map/pallas_call | solution.py:451
  11.3 2.6 %collective-permute-done.far1_ref = bf16[528,128]{1,0:T(8,128)(2,1)S(1)} collective-permute-done((bf16[528,128]{1,0:T(8,128)(2,1)S(1)}, bf16[528,128]{1,0:T(8,128)(2,1)S(1)}, u32[]{:S(2)}, u32[]{:S(2)}) %collective-permute-start) | collective-permute-done | bytes 135200 | tf_op jit(solution)/shard_map/ppermute | solution.py:466
  13.9 1.3 %shard_map.107 = (bf16[64,1024]{1,0:T(8,128)(2,1)S(1)}, bf16[64,1024]{1,0:T(8,128)(2,1)S(1)}, bf16[4,112,128]{2,1,0:T(8,128)(2,1)S(1)}, bf16[4,112,128]{2,1,0:T(8,128)(2,1)S(1)}) custom-call(bf16[528,128]{1,0:T(8,128)(2,1)S(1)} %collective-permute-done.far1_ref, bf16[528,128]{1,0:T(8,128)(2,1)S(1)} %collective-permute-done.1.far0_ref, ...), custom_call_target="tpu_custom_call" | custom-call | flops 1000000000 | bytes 1048576 | tf_op jit(solution)/shard_map/pallas_call | solution.py:451
  15.3 0.2 collective-permute-start.3
  15.4 1.2 %collective-permute-done.3.got_ref = bf16[4,112,128]{2,1,0:T(8,128)(2,1)S(1)} collective-permute-done((bf16[4,112,128]{2,1,0:T(8,128)(2,1)S(1)}, bf16[4,112,128]{2,1,0:T(8,128)(2,1)S(1)}, u32[]{:S(2)}, u32[]{:S(2)}) %collective-permute-start.3) | collective-permute-done | bytes 114720 | tf_op jit(solution)/shard_map/ppermute | solution.py:470
  16.7 2.6 %collective-permute-start.4 = (bf16[224,128]{1,0:T(8,128)(2,1)S(1)}, bf16[224,128]{1,0:T(8,128)(2,1)S(1)}, u32[]{:S(2)}, u32[]{:S(2)}) collective-permute-start(bf16[224,128]{1,0:T(8,128)(2,1)S(1)} %get-tuple-element.80), channel_id=1, source_target_pairs={{0,12},{2,14},{4,8},{6,10},{8,4},{10,6},{12,0},{14,2},{16,28},{18,... | collective-permute-start | bytes 172040 | tf_op jit(solution)/shard_map/ppermute | solution.py:470
  19.3 0.5 %collective-permute-start.5 = (bf16[224,128]{1,0:T(8,128)(2,1)S(1)}, bf16[224,128]{1,0:T(8,128)(2,1)S(1)}, u32[]{:S(2)}, u32[]{:S(2)}) collective-permute-start(bf16[224,128]{1,0:T(8,128)(2,1)S(1)} %get-tuple-element.81), channel_id=1, source_target_pairs={{0,8},{2,10},{4,12},{6,14},{8,0},{10,2},{12,4},{14,6},{16,24},{18,... | collective-permute-start | bytes 172040 | tf_op jit(solution)/shard_map/ppermute | solution.py:470
  19.7 0.5 %collective-permute-start.6 = (bf16[224,128]{1,0:T(8,128)(2,1)S(1)}, bf16[224,128]{1,0:T(8,128)(2,1)S(1)}, u32[]{:S(2)}, u32[]{:S(2)}) collective-permute-start(bf16[224,128]{1,0:T(8,128)(2,1)S(1)} %get-tuple-element.82), channel_id=1, source_target_pairs={{0,4},{2,6},{4,0},{6,2},{8,12},{10,14},{12,8},{14,10},{16,20},{18,... | collective-permute-start | bytes 172040 | tf_op jit(solution)/shard_map/ppermute | solution.py:470
  20.2 1.0 %shard_map.108.first_ref = bf16[64,4096]{1,0:T(8,128)(2,1)S(1)} custom-call(bf16[64,1024]{1,0:T(8,128)(2,1)S(1)} %get-tuple-element.73.pre_b_ref, bf16[256,576]{1,0:T(8,128)(2,1)S(1)} %get-tuple-element.74.wf_ref), custom_call_target="tpu_custom_call" | custom-call | flops 1000000000 | bytes 1048576 | tf_op jit(solution)/shard_map/pallas_call | solution.py:451
  21.3 0.8 %collective-permute-done.4.a_ref = bf16[224,128]{1,0:T(8,128)(2,1)S(1)} collective-permute-done((bf16[224,128]{1,0:T(8,128)(2,1)S(1)}, bf16[224,128]{1,0:T(8,128)(2,1)S(1)}, u32[]{:S(2)}, u32[]{:S(2)}) %collective-permute-start.4) | collective-permute-done | bytes 57376 | tf_op jit(solution)/shard_map/ppermute | solution.py:470
  22.0 1.4 %collective-permute-done.5.b_ref = bf16[224,128]{1,0:T(8,128)(2,1)S(1)} collective-permute-done((bf16[224,128]{1,0:T(8,128)(2,1)S(1)}, bf16[224,128]{1,0:T(8,128)(2,1)S(1)}, u32[]{:S(2)}, u32[]{:S(2)}) %collective-permute-start.5) | collective-permute-done | bytes 57376 | tf_op jit(solution)/shard_map/ppermute | solution.py:470
  23.5 0.5 %collective-permute-done.6.c_ref = bf16[224,128]{1,0:T(8,128)(2,1)S(1)} collective-permute-done((bf16[224,128]{1,0:T(8,128)(2,1)S(1)}, bf16[224,128]{1,0:T(8,128)(2,1)S(1)}, u32[]{:S(2)}, u32[]{:S(2)}) %collective-permute-start.6) | collective-permute-done | bytes 57376 | tf_op jit(solution)/shard_map/ppermute | solution.py:470
  24.0 3.5 %collective-permute-start.7 = (bf16[112,128]{1,0:T(8,128)(2,1)S(1)}, bf16[112,128]{1,0:T(8,128)(2,1)S(1)}, u32[]{:S(2)}, u32[]{:S(2)}) collective-permute-start(bf16[112,128]{1,0:T(8,128)(2,1)S(1)} %get-tuple-element.84), channel_id=1, source_target_pairs={{0,17},{1,16},{2,19},{3,18},{4,21},{5,20},{6,23},{7,22},{8,25},{9,... | collective-permute-start | bytes 86024 | tf_op jit(solution)/shard_map/ppermute | solution.py:466
  27.5 0.3 %collective-permute-start.8 = (bf16[112,128]{1,0:T(8,128)(2,1)S(1)}, bf16[112,128]{1,0:T(8,128)(2,1)S(1)}, u32[]{:S(2)}, u32[]{:S(2)}) collective-permute-start(bf16[112,128]{1,0:T(8,128)(2,1)S(1)} %get-tuple-element.84), channel_id=1, source_target_pairs={{0,16},{1,17},{2,18},{3,19},{4,20},{5,21},{6,22},{7,23},{8,24},{9,... | collective-permute-start | bytes 86024 | tf_op jit(solution)/shard_map/ppermute | solution.py:466
  27.8 0.6 %collective-permute-start.9 = (bf16[112,128]{1,0:T(8,128)(2,1)S(1)}, bf16[112,128]{1,0:T(8,128)(2,1)S(1)}, u32[]{:S(2)}, u32[]{:S(2)}) collective-permute-start(bf16[112,128]{1,0:T(8,128)(2,1)S(1)} %get-tuple-element.85), channel_id=1, source_target_pairs={{0,1},{1,0},{2,3},{3,2},{4,5},{5,4},{6,7},{7,6},{8,9},{9,8},{10,11... | collective-permute-start | bytes 86024 | tf_op jit(solution)/shard_map/ppermute | solution.py:466
  28.4 1.0 %shard_map.111 = (bf16[64,4096]{1,0:T(8,128)(2,1)S(1)}, bf16[2,64,4096]{2,1,0:T(8,128)(2,1)}) custom-call(bf16[64,1024]{1,0:T(8,128)(2,1)S(1)} %get-tuple-element.86.pre_b_ref, bf16[256,576]{1,0:T(8,128)(2,1)S(1)} %get-tuple-element.74.wf_ref, bf16[64,4096]{1,0:T(8,128)(2,1)S(1)} %shard_map.108.first_ref), custom_call_target="tpu_custom_call" | custom-call | flops 1000000000 | bytes 1048576 | tf_op jit(solution)/shard_map/pallas_call | solution.py:451
  29.5 0.4 %collective-permute-done.7.a_ref = bf16[112,128]{1,0:T(8,128)(2,1)S(1)} collective-permute-done((bf16[112,128]{1,0:T(8,128)(2,1)S(1)}, bf16[112,128]{1,0:T(8,128)(2,1)S(1)}, u32[]{:S(2)}, u32[]{:S(2)}) %collective-permute-start.7) | collective-permute-done | bytes 28704 | tf_op jit(solution)/shard_map/ppermute | solution.py:466
  29.8 2.4 %collective-permute-done.8.b_ref = bf16[112,128]{1,0:T(8,128)(2,1)S(1)} collective-permute-done((bf16[112,128]{1,0:T(8,128)(2,1)S(1)}, bf16[112,128]{1,0:T(8,128)(2,1)S(1)}, u32[]{:S(2)}, u32[]{:S(2)}) %collective-permute-start.8) | collective-permute-done | bytes 28704 | tf_op jit(solution)/shard_map/ppermute | solution.py:466
  32.3 0.0 collective-permute-done.9.c_ref
  32.3 1.3 %shard_map.112 = (f32[8,1600]{1,0:T(8,128)}, f32[1,64]{1,0:T(1,128)}, bf16[2,64,4096]{2,1,0:T(8,128)(2,1)}) custom-call(f32[112,128]{1,0:T(8,128)S(1)} %get-tuple-element.83.own_ref, bf16[112,128]{1,0:T(8,128)(2,1)S(1)} %collective-permute-done.7.a_ref, bf16[112,128]{1,0:T(8,128)(2,1)S(1)} %collective-permute-done.8.b_ref, ...), custom_call_target="tpu_custom_call", output_to_operand_aliasing={{2}: (5, {})} | custom-call | bytes 1048576 | tf_op jit(solution)/shard_map/pallas_call | solution.py:451
  (6 shorter events, 0.1 us)
Async XLA Ops:
  0.6 5.4 %copy-start = (bf16[1,2,64,4096]{3,2,1,0:T(8,128)(2,1)S(1)}, bf16[1,2,64,4096]{3,2,1,0:T(8,128)(2,1)}, u32[]{:S(2)}) copy-start(bf16[1,2,64,4096]{3,2,1,0:T(8,128)(2,1)} %param.8) | copy-start | bytes 3145732
  3.6 2.5 %copy-start.3 = (bf16[1,2,1024]{2,1,0:T(2,128)(2,1)S(1)}, bf16[1,2,1024]{2,1,0:T(2,128)(2,1)}, u32[]{:S(2)}) copy-start(bf16[1,2,1024]{2,1,0:T(2,128)(2,1)} %param.12) | copy-start | bytes 12292
  3.6 6.4 %collective-permute-start.1 = (bf16[528,128]{1,0:T(8,128)(2,1)S(1)}, bf16[528,128]{1,0:T(8,128)(2,1)S(1)}, u32[]{:S(2)}, u32[]{:S(2)}) collective-permute-start(bf16[528,128]{1,0:T(8,128)(2,1)S(1)} %get-tuple-element.51.sent_ref.refs_6_), channel_id=1, source_target_pairs={{0,3},{1,2},{2,1},{3,0},{4,7},{5,6},{6,5},{7,4},{8,11},{9,10},{10,... | collective-permute-start | bytes 405512 | tf_op jit(solution)/shard_map/ppermute | solution.py:466
  6.1 2.8 %copy-start.1 = (bf16[2,64,1024]{2,1,0:T(8,128)(2,1)S(1)}, bf16[2,64,1024]{2,1,0:T(8,128)(2,1)}, u32[]{:S(2)}) copy-start(bf16[2,64,1024]{2,1,0:T(8,128)(2,1)} %ws_ref.1) | copy-start | bytes 786436
  6.1 2.8 %copy-start.2 = (bf16[2,64,576]{2,1,0:T(8,128)(2,1)S(1)}, bf16[2,64,576]{2,1,0:T(8,128)(2,1)}, u32[]{:S(2)}) copy-start(bf16[2,64,576]{2,1,0:T(8,128)(2,1)} %wd_ref.1) | copy-start | bytes 442372
  7.6 2.5 %collective-permute-start.2 = (bf16[2,528,128]{2,1,0:T(8,128)(2,1)S(1)}, bf16[2,528,128]{2,1,0:T(8,128)(2,1)S(1)}, u32[]{:S(2)}, u32[]{:S(2)}) collective-permute-start(bf16[2,528,128]{2,1,0:T(8,128)(2,1)S(1)} %get-tuple-element.53), channel_id=1, source_target_pairs={{0,2},{2,0},{4,6},{6,4},{8,10},{10,8},{12,14},{14,12},{16,18},{18,... | collective-permute-start | bytes 811016 | tf_op jit(solution)/shard_map/ppermute | solution.py:470
  8.3 5.6 %collective-permute-start = (bf16[528,128]{1,0:T(8,128)(2,1)S(1)}, bf16[528,128]{1,0:T(8,128)(2,1)S(1)}, u32[]{:S(2)}, u32[]{:S(2)}) collective-permute-start(bf16[528,128]{1,0:T(8,128)(2,1)S(1)} %get-tuple-element.52.refs_7_), channel_id=1, source_target_pairs={{0,3},{1,2},{2,1},{3,0},{4,7},{5,6},{6,5},{7,4},{8,11},{9,10},{10,... | collective-permute-start | bytes 405512 | tf_op jit(solution)/shard_map/ppermute | solution.py:466
  15.3 1.4 %collective-permute-start.3 = (bf16[4,112,128]{2,1,0:T(8,128)(2,1)S(1)}, bf16[4,112,128]{2,1,0:T(8,128)(2,1)S(1)}, u32[]{:S(2)}, u32[]{:S(2)}) collective-permute-start(bf16[4,112,128]{2,1,0:T(8,128)(2,1)S(1)} %get-tuple-element.77), channel_id=1, source_target_pairs={{0,2},{2,0},{4,6},{6,4},{8,10},{10,8},{12,14},{14,12},{16,18},{18,... | collective-permute-start | bytes 344072 | tf_op jit(solution)/shard_map/ppermute | solution.py:470
  16.7 5.4 %collective-permute-start.4 = (bf16[224,128]{1,0:T(8,128)(2,1)S(1)}, bf16[224,128]{1,0:T(8,128)(2,1)S(1)}, u32[]{:S(2)}, u32[]{:S(2)}) collective-permute-start(bf16[224,128]{1,0:T(8,128)(2,1)S(1)} %get-tuple-element.80), channel_id=1, source_target_pairs={{0,12},{2,14},{4,8},{6,10},{8,4},{10,6},{12,0},{14,2},{16,28},{18,... | collective-permute-start | bytes 172040 | tf_op jit(solution)/shard_map/ppermute | solution.py:470
  19.3 4.2 %collective-permute-start.5 = (bf16[224,128]{1,0:T(8,128)(2,1)S(1)}, bf16[224,128]{1,0:T(8,128)(2,1)S(1)}, u32[]{:S(2)}, u32[]{:S(2)}) collective-permute-start(bf16[224,128]{1,0:T(8,128)(2,1)S(1)} %get-tuple-element.81), channel_id=1, source_target_pairs={{0,8},{2,10},{4,12},{6,14},{8,0},{10,2},{12,4},{14,6},{16,24},{18,... | collective-permute-start | bytes 172040 | tf_op jit(solution)/shard_map/ppermute | solution.py:470
  19.7 4.2 %collective-permute-start.6 = (bf16[224,128]{1,0:T(8,128)(2,1)S(1)}, bf16[224,128]{1,0:T(8,128)(2,1)S(1)}, u32[]{:S(2)}, u32[]{:S(2)}) collective-permute-start(bf16[224,128]{1,0:T(8,128)(2,1)S(1)} %get-tuple-element.82), channel_id=1, source_target_pairs={{0,4},{2,6},{4,0},{6,2},{8,12},{10,14},{12,8},{14,10},{16,20},{18,... | collective-permute-start | bytes 172040 | tf_op jit(solution)/shard_map/ppermute | solution.py:470
  24.0 5.9 %collective-permute-start.7 = (bf16[112,128]{1,0:T(8,128)(2,1)S(1)}, bf16[112,128]{1,0:T(8,128)(2,1)S(1)}, u32[]{:S(2)}, u32[]{:S(2)}) collective-permute-start(bf16[112,128]{1,0:T(8,128)(2,1)S(1)} %get-tuple-element.84), channel_id=1, source_target_pairs={{0,17},{1,16},{2,19},{3,18},{4,21},{5,20},{6,23},{7,22},{8,25},{9,... | collective-permute-start | bytes 86024 | tf_op jit(solution)/shard_map/ppermute | solution.py:466
  27.5 4.8 %collective-permute-start.8 = (bf16[112,128]{1,0:T(8,128)(2,1)S(1)}, bf16[112,128]{1,0:T(8,128)(2,1)S(1)}, u32[]{:S(2)}, u32[]{:S(2)}) collective-permute-start(bf16[112,128]{1,0:T(8,128)(2,1)S(1)} %get-tuple-element.84), channel_id=1, source_target_pairs={{0,16},{1,17},{2,18},{3,19},{4,20},{5,21},{6,22},{7,23},{8,24},{9,... | collective-permute-start | bytes 86024 | tf_op jit(solution)/shard_map/ppermute | solution.py:466
  27.8 4.4 %collective-permute-start.9 = (bf16[112,128]{1,0:T(8,128)(2,1)S(1)}, bf16[112,128]{1,0:T(8,128)(2,1)S(1)}, u32[]{:S(2)}, u32[]{:S(2)}) collective-permute-start(bf16[112,128]{1,0:T(8,128)(2,1)S(1)} %get-tuple-element.85), channel_id=1, source_target_pairs={{0,1},{1,0},{2,3},{3,2},{4,5},{5,4},{6,7},{7,6},{8,9},{9,8},{10,11... | collective-permute-start | bytes 86024 | tf_op jit(solution)/shard_map/ppermute | solution.py:466

commit v4 on v3

--- a/solution.py
+++ b/solution.py
@@ -63,12 +63,17 @@
     return jnp.where(source == wanted, 1.0, 0.0).astype(BF16)
 
 
+def halves(values, core):
+    even = jnp.concatenate([values[16 * m : 16 * m + 8] for m in range(CH // 16)], axis=0)
+    odd = jnp.concatenate([values[16 * m + 8 : 16 * m + 16] for m in range(CH // 16)], axis=0)
+    return jnp.where(core == 0, odd, even), jnp.where(core == 0, even, odd)
+
+
 TAP_LINES = {0: (1, -1), 1: (0, 0), 2: (1, 0), 3: (0, 1)}
 
 
 def tap_matrices(weight, taps, scratch):
-    wide = weight.astype(F32)
-    scratch[0 : CH * taps, 0:CH] = wide.T
+    scratch[0 : CH * taps, 0:CH] = weight.astype(F32).T
     return [scratch[pl.ds(tap, CH, stride=taps), 0:CH] for tap in range(taps)]
 
 
@@ -108,8 +113,8 @@
 
 def first_kernel(
     owner_hbm, x_hbm, ws_hbm, wd_hbm, bias_hbm, cot_hbm,
-    ph_ref, pre_ref, act_ref, send_ref, strided_ref, dilated_ref, bias_ref,
-    x_ref, ws_ref, wd_ref, cot_ref, table_ref, owner_ref, wscr, im_scr, sems,
+    ph_ref, pre_ref, act_ref, send_ref, strided_ref, dilated_ref, bias_ref, cot_ref,
+    x_ref, ws_ref, wd_ref, table_ref, owner_ref, wscr, im_scr, sems,
 ):
     scene = lax.axis_index("scene")
     branch = scene % 2
@@ -183,8 +188,12 @@
     for phase in range(4):
         row = [blocks.get((phase, s), zero) for s in range(9)]
         wf_ref[phase * CH : (phase + 1) * CH, :] = jnp.concatenate(row, axis=1).astype(BF16)
-    mats = tap_matrices(wd_ref[branch], 9, wscr)
-    wt_ref[...] = jnp.concatenate(mats[::-1], axis=1).astype(BF16)
+    give, keep = halves(wd_ref[branch].astype(F32), branch)
+    mats = tap_matrices(jnp.concatenate([give, keep], axis=0), 9, wscr)[::-1]
+    half = CH // 2
+    wt_ref[...] = jnp.concatenate(
+        [mat[:, h * half : (h + 1) * half] for h in range(2) for mat in mats], axis=1
+    ).astype(BF16)
     slopes = []
     for pre_ref in pre_refs:
         pre = pre_ref[...]
@@ -230,18 +239,22 @@
     place_ref[...] = place
 
 
-def strided_product(pre_b, ph_ref, shift_scr):
-    side = math.isqrt(pre_b.shape[1])
-    near = shifted_masks(side, 1)
-    for s, (dr, dc) in enumerate(SHIFTS):
-        shift_scr[s * CH : (s + 1) * CH, :] = shifted(pre_b, dr, dc, side, 1, near)
-    return dot_nt(shift_scr[...], ph_ref[...])
-
-
-def backward_patch(position, candidates, select_ref, cot_ref, wt_ref, act_ref, slope_ref, shift_scr):
-    side = math.isqrt(act_ref.shape[1])
+HALF = 9 * CH // 2
+
+
+def shift_rows(pieces, reach, side, target):
+    masks = shifted_masks(side, reach)
+    rows = CH // 2
+    for h, piece in enumerate(pieces):
+        for s, (dr, dc) in enumerate(SHIFTS):
+            at = h * HALF + s * rows
+            target[at : at + rows, :] = shifted(piece, dr, dc, side, reach, masks)
+
+
+def backward_patch(position, candidates, select_ref, cot_ref, wt_ref, slope_ref, shift_scr):
+    side = math.isqrt(slope_ref.shape[1])
     lanes = side * side // 128
-    far = shifted_masks(side, 2)
+    core = lax.axis_index("scene") % 2
     partner = None
     for k, payload in enumerate(candidates):
         term = payload * select_ref[position * 4 + k : position * 4 + k + 1, :].astype(BF16)
@@ -249,88 +262,103 @@
     live = select_ref[8 + position : 9 + position, :]
     signal = (cot_ref[position * 16 : position * 16 + 16, :] + partner[lanes * CH :, :].astype(F32)) * live
     out_grad = jnp.concatenate(
-        [
-            (signal[j : j + 1, :] * partner[j * CH : (j + 1) * CH, :].astype(F32)).astype(BF16)
-            for j in range(lanes)
-        ],
-        axis=1,
-    )
-    for tap, (dr, dc) in enumerate(SHIFTS):
-        shift_scr[tap * CH : (tap + 1) * CH, :] = shifted(out_grad, dr, dc, side, 2, far)
-    act_grad = dot(wt_ref[...], shift_scr[...])
-    act = act_ref[...]
-    dilated = dot_nt(shift_scr[...], jnp.concatenate([act, act], axis=0))
-    pre_grad = act_grad * slope_ref[...]
-    bias = jnp.sum(pre_grad, axis=1, keepdims=True)
-    return pre_grad.astype(BF16), bias, dilated
+        [signal[j : j + 1, :] * partner[j * CH : (j + 1) * CH, :].astype(F32) for j in range(lanes)], axis=1
+    )
+    shift_rows([piece.astype(BF16) for piece in halves(out_grad, core)], 2, side, shift_scr)
+    return dot(wt_ref[...], shift_scr[...]) * slope_ref[...]
 
 
 def backward_first_kernel(
     far0_ref, near_ref, select_ref, cot_ref, wt_ref, act_ref, slope_ref, ph_ref,
     pre_b_ref, bias_ref, dilated_ref, strided_ref, shift_scr,
 ):
-    pre_b, bias, dilated = backward_patch(
-        0, (near_ref[0], near_ref[1], far0_ref[...]), select_ref, cot_ref, wt_ref, act_ref, slope_ref, shift_scr
-    )
-    pre_b_ref[...] = pre_b
-    bias_ref[...] = jnp.broadcast_to(bias, bias_ref.shape)
-    dilated_ref[...] = dilated
-    strided_ref[...] = strided_product(pre_b, ph_ref, shift_scr)
+    side = math.isqrt(slope_ref.shape[1])
+    core = lax.axis_index("scene") % 2
+    candidates = (near_ref[0], near_ref[1], far0_ref[...])
+    pre_grad = backward_patch(0, candidates, select_ref, cot_ref, wt_ref, slope_ref, shift_scr)
+    act = act_ref[...]
+    dilated_ref[...] = dot_nt(shift_scr[...], jnp.concatenate([act, act], axis=0))
+    bias_ref[...] = jnp.broadcast_to(jnp.sum(pre_grad, axis=1, keepdims=True), bias_ref.shape)
+    pre_b_ref[...] = pre_grad.astype(BF16)
+    shift_rows([piece.astype(BF16) for piece in halves(pre_grad, core)], 1, side, shift_scr)
+    strided_ref[...] = dot_nt(shift_scr[...], ph_ref[...])
+
+
+def tap_blocks(strided, dilated):
+    rows = CH // 2
+    lower = lax.broadcasted_iota(jnp.int32, (rows, 2 * CH), 1) < CH
+
+    def strided_piece(pr, shift):
+        return strided[shift * rows : (shift + 1) * rows, pr * 2 * CH : (pr + 1) * 2 * CH]
+
+    blocks = []
+    for rt in range(4):
+        pr, dr = TAP_LINES[rt]
+        blocks.append(strided_piece(pr, shift_index(-dr, 0)))
+        blocks.append(
+            jnp.where(lower, strided_piece(pr, shift_index(-dr, -1)), strided_piece(pr, shift_index(-dr, 1)))
+        )
+    for j in range(5):
+        low = dilated[(8 - 2 * j) * rows : (9 - 2 * j) * rows, :]
+        high = dilated[(7 - 2 * j) * rows : (8 - 2 * j) * rows, :] if j < 4 else jnp.zeros_like(low)
+        blocks.append(jnp.where(lower, low, high))
+    return blocks
+
+
+def write_blocks(blocks, bias_wide, ref, chunked):
+    if not chunked:
+        for i, block in enumerate(blocks):
+            ref[i] = block
+        return
+    here = lax.axis_index("scene") // 2 % 4
+    for m in range(4):
+        pieces = [block[8 * m : 8 * m + 8] for block in blocks] + [bias_wide]
+        ref[here ^ m] = jnp.concatenate(pieces, axis=0).astype(BF16)
 
 
 def backward_second_kernel(
     far1_ref, far0_ref, near_ref, select_ref, cot_ref, wt_ref, act_ref, slope_ref, ph_ref,
-    other_ref, bias_ref, dilated_ref, strided_ref, *refs, chunked,
+    other_ref, other_bias_ref, other_dilated_ref, other_strided_ref,
+    pre_b0_ref, pre_b1_ref, bias_ref, give_ref, out_shifts_ref, kept_ref, shift_scr, *, chunked,
 ):
-    pre_b0_ref, pre_b1_ref = refs[:2]
-    if chunked:
-        keep_ref, give_ref, shift_scr, dil_scr, grad_acc, grad_scr = refs[2:]
-    else:
-        grad_scr, bias_out_ref, shift_scr, dil_scr, grad_acc = refs[2:]
-    pre_b, bias, dilated = backward_patch(
-        1, (near_ref[0], near_ref[1], far0_ref[...], far1_ref[...]),
-        select_ref, cot_ref, wt_ref, act_ref, slope_ref, shift_scr,
-    )
+    side = math.isqrt(slope_ref.shape[1])
+    core = lax.axis_index("scene") % 2
+    candidates = (near_ref[0], near_ref[1], far0_ref[...], far1_ref[...])
+    pre_grad = backward_patch(1, candidates, select_ref, cot_ref, wt_ref, slope_ref, out_shifts_ref)
+    act = act_ref[...]
+    dilated = dot_nt(out_shifts_ref[0:HALF, :], jnp.concatenate([act, act], axis=0))
+    give, keep = (piece.astype(BF16) for piece in halves(pre_grad, core))
+    shift_rows([give], 1, side, shift_scr)
+    strided = dot_nt(shift_scr[...], ph_ref[...])
+    kept_ref[...] = keep
+    bias_wide = (jnp.sum(pre_grad, axis=1, keepdims=True) + other_bias_ref[...]).T[0:8, :]
+    bias_wide = jnp.concatenate([bias_wide, jnp.zeros_like(bias_wide)], axis=1)
+    bias_ref[...] = bias_wide
+    blocks = tap_blocks(strided + other_strided_ref[0:HALF, :], dilated + other_dilated_ref[0:HALF, :])
+    write_blocks(blocks, bias_wide, give_ref, chunked)
+    pre_b = pre_grad.astype(BF16)
     swapped = select_ref[10:11, 0:1].astype(BF16)
     straight = 1.0 - swapped
     pre_b0_ref[...] = other_ref[...] * straight + pre_b * swapped
     pre_b1_ref[...] = other_ref[...] * swapped + pre_b * straight
-    dil_scr[...] = dilated + dilated_ref[...]
-    grad_acc[...] = strided_product(pre_b, ph_ref, shift_scr) + strided_ref[...]
-    lower = lax.broadcasted_iota(jnp.int32, (CH, 2 * CH), 1) < CH
-
-    def strided_piece(pr, shift):
-        return grad_acc[shift * CH : (shift + 1) * CH, pr * 2 * CH : (pr + 1) * 2 * CH]
-
-    for rt in range(4):
-        pr, dr = TAP_LINES[rt]
-        for k in range(2):
-            low_dc, high_dc = (0, 0) if k == 0 else (1, -1)
-            low = strided_piece(pr, shift_index(-dr, -low_dc))
-            high = strided_piece(pr, shift_index(-dr, -high_dc))
-            grad_scr[rt * 2 + k] = low if k == 0 else jnp.where(lower, low, high)
-    for j in range(5):
-        low = dil_scr[(8 - 2 * j) * CH : (9 - 2 * j) * CH, :]
-        high = dil_scr[(7 - 2 * j) * CH : (8 - 2 * j) * CH, :] if j < 4 else jnp.zeros_like(low)
-        grad_scr[8 + j] = jnp.where(lower, low, high)
-    bias_wide = (bias + bias_ref[...]).T[0:8, :]
-    bias_wide = jnp.concatenate([bias_wide, jnp.zeros_like(bias_wide)], axis=1)
-    if not chunked:
-        bias_out_ref[...] = bias_wide
-        return
-    scene = lax.axis_index("scene")
-    here, branch = scene // 2 % 4, scene % 2
-    for ref, core in ((keep_ref, branch), (give_ref, 1 - branch)):
-        for d in range(4):
-            row = pl.multiple_of(((here ^ d) * 2 + core) * 8, 8)
-            pieces = [grad_scr[block, pl.ds(row, 8), :] for block in range(BLOCKS - 1)]
-            ref[d] = jnp.concatenate(pieces + [bias_wide], axis=0).astype(BF16)
-
-
-def spread_kernel(place_ref, keep_ref, got_ref, *out_refs):
+
+
+def backward_kept_kernel(
+    out_shifts_ref, kept_pre_ref, act_ref, ph_ref, other_dilated_ref, other_strided_ref, keep_ref, shift_scr, *, chunked
+):
+    side = math.isqrt(act_ref.shape[1])
+    act = act_ref[...]
+    dilated = dot_nt(out_shifts_ref[HALF:, :], jnp.concatenate([act, act], axis=0))
+    shift_rows([kept_pre_ref[...]], 1, side, shift_scr)
+    strided = dot_nt(shift_scr[...], ph_ref[...])
+    blocks = tap_blocks(strided + other_strided_ref[HALF:, :], dilated + other_dilated_ref[HALF:, :])
+    write_blocks(blocks, jnp.zeros((8, 2 * CH), F32), keep_ref, chunked)
+
+
+def spread_kernel(place_ref, bias_ref, keep_ref, got_ref, *out_refs):
     rows = keep_ref.shape[1]
     top = lax.broadcasted_iota(jnp.int32, (16, 128), 0) < 8
-    mine = keep_ref[0, rows - 16 :, :].astype(F32)[8:9, :]
+    mine = bias_ref[0:1, :]
     theirs = got_ref[0, rows - 16 :, :].astype(F32)[8:9, :]
     for d, out_ref in enumerate(out_refs):
         for half, ref in enumerate((keep_ref, got_ref)):
@@ -477,6 +505,13 @@
     )
 
 
+def join_halves(give, keep):
+    parts = [half.reshape(BLOCKS - 1, -1, 8, half.shape[-1]) for half in (give, keep)]
+    first = lax.axis_index("scene") % 2 == 0
+    pair = jnp.stack([jnp.where(first, parts[1], parts[0]), jnp.where(first, parts[0], parts[1])], axis=2)
+    return pair.reshape(BLOCKS - 1, -1, pair.shape[-1])
+
+
 def reduce_anywhere(blocks, bias_row, tile_owner, bias_rows, weight_scale, bias_scale):
     channels = blocks.shape[1]
     scene = lax.axis_index("scene")
@@ -531,8 +566,9 @@
         ((channels, 16 * channels), BF16),
         ((channels, 9 * channels), BF16),
         ((channels, 128), F32),
+        (own_cot.shape, BF16),
     ]
-    *part, w_strided, w_dilated, bias_col = call(
+    *part, w_strided, w_dilated, bias_col, cot = call(
         first_kernel,
         first_outs,
         "hhhhhh",
@@ -540,7 +576,6 @@
             ((channels, cells_in), BF16),
             (strided_weights.shape[1:], BF16),
             (dilated_weights.shape[1:], BF16),
-            (own_cot.shape, BF16),
             (tile_bias.shape, F32),
             pltpu.SMEM(tile_owner.shape, jnp.int32),
             wscr,
@@ -556,7 +591,7 @@
         patch_outs + [((2,) + payload, BF16)],
         "vvvvvv",
         [im_scr],
-        features, own_cot, w_strided, w_dilated, bias_col, part[3],
+        features, cot, w_strided, w_dilated, bias_col, part[3],
         flops=10**10,
     )
     far.append(device_xor(late[3], 1, 1))
@@ -596,23 +631,30 @@
         far[0], near, select, cots, w_act, act[0], slope[0], phases[0],
         flops=10**9,
     )
-    block_shape = ((BLOCKS - 1, channels, 128), F32)
-    half_shape = ((4, BLOCKS * 8, 128), BF16)
-    results = call(
+    half_shift = ((9 * channels // 2, cells), BF16)
+    grads_shape = ((4, BLOCKS * 8, 128), BF16) if chunked else ((BLOCKS - 1, channels // 2, 128), F32)
+    *pre_b, bias, give, out_shifts, kept_rows = call(
         functools.partial(backward_second_kernel, chunked=chunked),
-        [(grid, BF16)] * 2 + ([half_shape] * 2 if chunked else [block_shape, ((8, 128), F32)]),
+        [(grid, BF16)] * 2 + [((8, 128), F32), grads_shape, shift_scr, ((channels // 2, cells), BF16)],
         "v" * 13,
-        [shift_scr] + sums + ([block_shape] if chunked else []),
+        [half_shift],
         far[1], far[0], near, select, cots, w_act, act[1], slope[1], phases[1], *first,
         flops=10**9,
     )
-    pre_b, grads = results[:2], results[2:]
+    if chunked:
+        got = scene_xor(give, 1)
+    (keep,) = call(
+        functools.partial(backward_kept_kernel, chunked=chunked),
+        [grads_shape],
+        "v" * 6,
+        [half_shift],
+        out_shifts, kept_rows, act[1], phases[1], *first[2:],
+        flops=10**9,
+    )
     feature_shape = ((channels, cells_in), BF16)
     if chunked:
-        keep, give = grads
-        got = scene_xor(give, 1)
         stage = ((2 * BLOCKS * 8, 128), BF16)
-        own, by_y, by_z, by_zy = call(spread_kernel, [stage] * 4, "vvv", [], place, keep, got)
+        own, by_y, by_z, by_zy = call(spread_kernel, [stage] * 4, "vvvv", [], place, bias, keep, got)
         by_zy, by_z, by_y = scene_xor(by_zy, 6), scene_xor(by_z, 4), scene_xor(by_y, 2)
     (feature_first,) = call(
         feature_first_kernel, [feature_shape], "vv", [shift_scr], pre_b[0], w_feature, flops=10**9
@@ -636,7 +678,7 @@
     if not chunked:
         feature_grads = feature_grads.at[1].set(feature_last)
         grad_weights, grad_bias = reduce_anywhere(
-            grads[0], grads[1][0], tile_owner, bias_rows, weight_scale, bias_scale
+            join_halves(give, keep), bias[0], tile_owner, bias_rows, weight_scale, bias_scale
         )
         return (feature_grads[None], grad_weights, grad_bias)
     grad_weights, grad_bias, feature_grads = call(

time: 33.7 us -> 33.4 us (level)
  starting transfers between devices: 12 us -> 11.4 us
  Pallas kernels: 11.4 us -> 11.8 us
    ppermute x5, starting transfers between devices: 7.51 us -> 6.96 us  [device_pairs(): return lax.ppermute(x, ('scene', 'tile'), flat)]
    ppermute x5, waiting for transfers between devices: 3.86 us -> 3.33 us  [scene_xor(): lax.ppermute(x, 'scene', [(i, i ^ distance) for i in range(lax.axis_size(...]
    pallas_call x10 -> x11, Pallas kernels: 11.4 us -> 11.8 us  [call(): pl.pallas_call(kernel, out_shape=[jax.ShapeDtypeStruct(shape, kind) for s...]
  transfers between devices with their start and end apart: 10 -> 10, of which waited for: 8 -> 8; matrix products, arithmetic and copies ran while one was open for 0% -> 0% of each run, Pallas kernels for 17% -> 20%
where the time goes in v4:
time: 33.4 us; the launch traced here: 33.2 us
  Pallas kernels  11.8 us (35%)
  starting transfers between devices  11.4 us (34%)
  waiting for transfers between devices  9.23 us (28%)
  between operations  0.71 us (2%)
    pallas_call x11, Pallas kernels, call(): pl.pallas_call(kernel, out_shape=[jax.ShapeDtypeStruct(shape, kind) for s...  11.8 us
    ppermute x5, starting transfers between devices, device_pairs(): return lax.ppermute(x, ('scene', 'tile'), flat)  6.96 us
    ppermute x5, waiting for transfers between devices, device_pairs(): return lax.ppermute(x, ('scene', 'tile'), flat)  5.9 us
    ppermute x5, starting transfers between devices, scene_xor(): lax.ppermute(x, 'scene', [(i, i ^ distance) for i in range(lax.axis_size(...  4.48 us
    ppermute x5, waiting for transfers between devices, scene_xor(): lax.ppermute(x, 'scene', [(i, i ^ distance) for i in range(lax.axis_size(...  3.33 us
  transfers between devices with their start and end apart: 10, of which 8 were waited for; matrix products, arithmetic and copies ran while one was open for 0% of the time, Pallas kernels for 20%

profile of v4, /device:TPU:0, one launch (start us, length us, event | category | flops | bytes accessed | tf_op | source)
XLA Modules:
  0.0 33.2 jit_solution(4712740328217549601)
XLA Ops:
  0.6 0.0 copy-start
  0.6 3.0 %shard_map.103 = (bf16[256,1024]{1,0:T(8,128)(2,1)S(1)}, f32[64,1024]{1,0:T(8,128)S(1)}, bf16[64,1024]{1,0:T(8,128)(2,1)S(1)}, bf16[528,128]{1,0:T(8,128)(2,1)S(...) custom-call(s32[16]{0:T(128)} %owner_hbm.3, ...), custom_call_target="tpu_custom_call" | custom-call | flops 1000000000 | bytes 1048576 | tf_op jit(solution)/shard_map/pallas_call | solution.py:479
  3.6 2.4 %collective-permute-start.1 = (bf16[528,128]{1,0:T(8,128)(2,1)S(1)}, bf16[528,128]{1,0:T(8,128)(2,1)S(1)}, u32[]{:S(2)}, u32[]{:S(2)}) collective-permute-start(bf16[528,128]{1,0:T(8,128)(2,1)S(1)} %get-tuple-element.55.sent_ref.refs_6_), channel_id=1, source_target_pairs={{0,3},{1,2},{2,1},{3,0},{4,7},{5,6},{6,5},{7,4},{8,11},{9,10},{10,... | collective-permute-start | bytes 405512 | tf_op jit(solution)/shard_map/ppermute | solution.py:494
  6.1 0.0 copy-done
  6.1 1.5 %shard_map.104 = (bf16[256,1024]{1,0:T(8,128)(2,1)S(1)}, f32[64,1024]{1,0:T(8,128)S(1)}, bf16[64,1024]{1,0:T(8,128)(2,1)S(1)}, bf16[528,128]{1,0:T(8,128)(2,1)S(1)}, bf16[2,528,128]{2,1,0:T(8,128)(2,1)S(1)}) custom-call(bf16[2,64,4096]{2,1,0:T(8,128)(2,1)S(1)} %bitcast.5, bf16[2,1024]{1,0:T(2,128)(2,1)S(1)} %get-tuple-element.51.cot_ref, ...), custom_call_target="tpu_custom_call" | custom-call | flops 10000000000 | bytes 1048576 | tf_op jit(solution)/shard_map/pallas_call | solution.py:479
  7.6 0.7 %collective-permute-start.2 = (bf16[2,528,128]{2,1,0:T(8,128)(2,1)S(1)}, bf16[2,528,128]{2,1,0:T(8,128)(2,1)S(1)}, u32[]{:S(2)}, u32[]{:S(2)}) collective-permute-start(bf16[2,528,128]{2,1,0:T(8,128)(2,1)S(1)} %get-tuple-element.57), channel_id=1, source_target_pairs={{0,2},{2,0},{4,6},{6,4},{8,10},{10,8},{12,14},{14,12},{16,18},{18,... | collective-permute-start | bytes 811016 | tf_op jit(solution)/shard_map/ppermute | solution.py:498
  8.3 0.1 collective-permute-start
  8.4 0.0 copy-done.1
  8.4 1.2 %shard_map.105 = (f32[64,1024]{1,0:T(8,128)S(1)}, f32[64,1024]{1,0:T(8,128)S(1)}, bf16[64,1024]{1,0:T(8,128)(2,1)S(1)}, bf16[64,1024]{1,0:T(8,128)(2,1)S(1)}, bf...) custom-call(s32[4,8]{1,0:T(4,128)} %bitcast.8, ...), custom_call_target="tpu_custom_call" | custom-call | flops 10000000000 | bytes 1048576 | tf_op jit(solution)/shard_map/pallas_call | solution.py:479
  9.6 0.4 %collective-permute-done.1.far0_ref = bf16[528,128]{1,0:T(8,128)(2,1)S(1)} collective-permute-done((bf16[528,128]{1,0:T(8,128)(2,1)S(1)}, bf16[528,128]{1,0:T(8,128)(2,1)S(1)}, u32[]{:S(2)}, u32[]{:S(2)}) %collective-permute-start.1) | collective-permute-done | bytes 135200 | tf_op jit(solution)/shard_map/ppermute | solution.py:494
  10.1 0.0 collective-permute-done.2.near_ref
  10.1 1.2 %shard_map.106 = (bf16[64,1024]{1,0:T(8,128)(2,1)S(1)}, f32[64,128]{1,0:T(8,128)S(1)}, f32[576,128]{1,0:T(8,128)S(1)}, f32[576,256]{1,0:T(8,128)S(1)}) custom-call(bf16[528,128]{1,0:T(8,128)(2,1)S(1)} %collective-permute-done.1.far0_ref, bf16[2,528,128]{2,1,0:T(8,128)(2,1)S(1)} %collective-permute-done.2.near_ref, ...), custom_call_target="tpu_custom_call" | custom-call | flops 1000000000 | bytes 1048576 | tf_op jit(solution)/shard_map/pallas_call | solution.py:479
  11.3 2.6 %collective-permute-done.far1_ref = bf16[528,128]{1,0:T(8,128)(2,1)S(1)} collective-permute-done((bf16[528,128]{1,0:T(8,128)(2,1)S(1)}, bf16[528,128]{1,0:T(8,128)(2,1)S(1)}, u32[]{:S(2)}, u32[]{:S(2)}) %collective-permute-start) | collective-permute-done | bytes 135200 | tf_op jit(solution)/shard_map/ppermute | solution.py:494
  13.9 1.0 %shard_map.107 = (bf16[64,1024]{1,0:T(8,128)(2,1)S(1)}, bf16[64,1024]{1,0:T(8,128)(2,1)S(1)}, f32[8,128]{1,0:T(8,128)S(1)}, bf16[4,112,128]{2,1,0:T(8,128)(2,1)S...) custom-call(bf16[528,128]{1,0:T(8,128)(2,1)S(1)} %collective-permute-done.far1_ref, ...), custom_call_target="tpu_custom_call" | custom-call | flops 1000000000 | bytes 1048576 | tf_op jit(solution)/shard_map/pallas_call | solution.py:479
  14.9 0.2 collective-permute-start.3
  15.1 0.5 %shard_map.109.keep_ref = bf16[4,112,128]{2,1,0:T(8,128)(2,1)S(1)} custom-call(bf16[576,1024]{1,0:T(8,128)(2,1)S(1)} %get-tuple-element.81.out_shifts_ref, bf16[32,1024]{1,0:T(8,128)(2,1)S(1)} %get-tuple-element.82.kept_pre_ref, bf16[64,1024]{1,0:T(8,128)(2,1)S(1)} %get-tuple-element.67.act_ref, bf16[256,1024]{1,0:T(8,128)(2,1)S(1)} %get-tuple-element.69.ph_ref, ...), custom_call_target="tpu_custom_call" | custom-call | flops 1000000000 | bytes 1048576 | tf_op jit(solution)/shard_map/pallas_call | solution.py:479
  15.6 0.7 %collective-permute-done.3.got_ref = bf16[4,112,128]{2,1,0:T(8,128)(2,1)S(1)} collective-permute-done((bf16[4,112,128]{2,1,0:T(8,128)(2,1)S(1)}, bf16[4,112,128]{2,1,0:T(8,128)(2,1)S(1)}, u32[]{:S(2)}, u32[]{:S(2)}) %collective-permute-start.3) | collective-permute-done | bytes 114720 | tf_op jit(solution)/shard_map/ppermute | solution.py:498
  16.3 2.6 %collective-permute-start.4 = (bf16[224,128]{1,0:T(8,128)(2,1)S(1)}, bf16[224,128]{1,0:T(8,128)(2,1)S(1)}, u32[]{:S(2)}, u32[]{:S(2)}) collective-permute-start(bf16[224,128]{1,0:T(8,128)(2,1)S(1)} %get-tuple-element.86), channel_id=1, source_target_pairs={{0,12},{2,14},{4,8},{6,10},{8,4},{10,6},{12,0},{14,2},{16,28},{18,... | collective-permute-start | bytes 172040 | tf_op jit(solution)/shard_map/ppermute | solution.py:498
  18.9 0.4 %collective-permute-start.5 = (bf16[224,128]{1,0:T(8,128)(2,1)S(1)}, bf16[224,128]{1,0:T(8,128)(2,1)S(1)}, u32[]{:S(2)}, u32[]{:S(2)}) collective-permute-start(bf16[224,128]{1,0:T(8,128)(2,1)S(1)} %get-tuple-element.87), channel_id=1, source_target_pairs={{0,8},{2,10},{4,12},{6,14},{8,0},{10,2},{12,4},{14,6},{16,24},{18,... | collective-permute-start | bytes 172040 | tf_op jit(solution)/shard_map/ppermute | solution.py:498
  19.4 0.5 %collective-permute-start.6 = (bf16[224,128]{1,0:T(8,128)(2,1)S(1)}, bf16[224,128]{1,0:T(8,128)(2,1)S(1)}, u32[]{:S(2)}, u32[]{:S(2)}) collective-permute-start(bf16[224,128]{1,0:T(8,128)(2,1)S(1)} %get-tuple-element.88), channel_id=1, source_target_pairs={{0,4},{2,6},{4,0},{6,2},{8,12},{10,14},{12,8},{14,10},{16,20},{18,... | collective-permute-start | bytes 172040 | tf_op jit(solution)/shard_map/ppermute | solution.py:498
  19.9 1.0 %shard_map.108.first_ref = bf16[64,4096]{1,0:T(8,128)(2,1)S(1)} custom-call(bf16[64,1024]{1,0:T(8,128)(2,1)S(1)} %get-tuple-element.77.pre_b_ref, bf16[256,576]{1,0:T(8,128)(2,1)S(1)} %get-tuple-element.78.wf_ref), custom_call_target="tpu_custom_call" | custom-call | flops 1000000000 | bytes 1048576 | tf_op jit(solution)/shard_map/pallas_call | solution.py:479
  20.9 0.8 %collective-permute-done.4.a_ref = bf16[224,128]{1,0:T(8,128)(2,1)S(1)} collective-permute-done((bf16[224,128]{1,0:T(8,128)(2,1)S(1)}, bf16[224,128]{1,0:T(8,128)(2,1)S(1)}, u32[]{:S(2)}, u32[]{:S(2)}) %collective-permute-start.4) | collective-permute-done | bytes 57376 | tf_op jit(solution)/shard_map/ppermute | solution.py:498
  21.7 1.4 %collective-permute-done.5.b_ref = bf16[224,128]{1,0:T(8,128)(2,1)S(1)} collective-permute-done((bf16[224,128]{1,0:T(8,128)(2,1)S(1)}, bf16[224,128]{1,0:T(8,128)(2,1)S(1)}, u32[]{:S(2)}, u32[]{:S(2)}) %collective-permute-start.5) | collective-permute-done | bytes 57376 | tf_op jit(solution)/shard_map/ppermute | solution.py:498
  23.1 0.4 %collective-permute-done.6.c_ref = bf16[224,128]{1,0:T(8,128)(2,1)S(1)} collective-permute-done((bf16[224,128]{1,0:T(8,128)(2,1)S(1)}, bf16[224,128]{1,0:T(8,128)(2,1)S(1)}, u32[]{:S(2)}, u32[]{:S(2)}) %collective-permute-start.6) | collective-permute-done | bytes 57376 | tf_op jit(solution)/shard_map/ppermute | solution.py:498
  23.6 3.6 %collective-permute-start.7 = (bf16[112,128]{1,0:T(8,128)(2,1)S(1)}, bf16[112,128]{1,0:T(8,128)(2,1)S(1)}, u32[]{:S(2)}, u32[]{:S(2)}) collective-permute-start(bf16[112,128]{1,0:T(8,128)(2,1)S(1)} %get-tuple-element.90), channel_id=1, source_target_pairs={{0,17},{1,16},{2,19},{3,18},{4,21},{5,20},{6,23},{7,22},{8,25},{9,... | collective-permute-start | bytes 86024 | tf_op jit(solution)/shard_map/ppermute | solution.py:494
  27.2 0.3 collective-permute-start.8
  27.5 0.6 %collective-permute-start.9 = (bf16[112,128]{1,0:T(8,128)(2,1)S(1)}, bf16[112,128]{1,0:T(8,128)(2,1)S(1)}, u32[]{:S(2)}, u32[]{:S(2)}) collective-permute-start(bf16[112,128]{1,0:T(8,128)(2,1)S(1)} %get-tuple-element.91), channel_id=1, source_target_pairs={{0,1},{1,0},{2,3},{3,2},{4,5},{5,4},{6,7},{7,6},{8,9},{9,8},{10,11... | collective-permute-start | bytes 86024 | tf_op jit(solution)/shard_map/ppermute | solution.py:494
  28.1 1.0 %shard_map.112 = (bf16[64,4096]{1,0:T(8,128)(2,1)S(1)}, bf16[2,64,4096]{2,1,0:T(8,128)(2,1)}) custom-call(bf16[64,1024]{1,0:T(8,128)(2,1)S(1)} %get-tuple-element.92.pre_b_ref, bf16[256,576]{1,0:T(8,128)(2,1)S(1)} %get-tuple-element.78.wf_ref, bf16[64,4096]{1,0:T(8,128)(2,1)S(1)} %shard_map.108.first_ref), custom_call_target="tpu_custom_call" | custom-call | flops 1000000000 | bytes 1048576 | tf_op jit(solution)/shard_map/pallas_call | solution.py:479
  29.1 0.4 %collective-permute-done.7.a_ref = bf16[112,128]{1,0:T(8,128)(2,1)S(1)} collective-permute-done((bf16[112,128]{1,0:T(8,128)(2,1)S(1)}, bf16[112,128]{1,0:T(8,128)(2,1)S(1)}, u32[]{:S(2)}, u32[]{:S(2)}) %collective-permute-start.7) | collective-permute-done | bytes 28704 | tf_op jit(solution)/shard_map/ppermute | solution.py:494
  29.5 2.5 %collective-permute-done.8.b_ref = bf16[112,128]{1,0:T(8,128)(2,1)S(1)} collective-permute-done((bf16[112,128]{1,0:T(8,128)(2,1)S(1)}, bf16[112,128]{1,0:T(8,128)(2,1)S(1)}, u32[]{:S(2)}, u32[]{:S(2)}) %collective-permute-start.8) | collective-permute-done | bytes 28704 | tf_op jit(solution)/shard_map/ppermute | solution.py:494
  31.9 0.0 collective-permute-done.9.c_ref
  31.9 1.3 %shard_map.113 = (f32[8,1600]{1,0:T(8,128)}, f32[1,64]{1,0:T(1,128)}, bf16[2,64,4096]{2,1,0:T(8,128)(2,1)}) custom-call(f32[112,128]{1,0:T(8,128)S(1)} %get-tuple-element.89.own_ref, bf16[112,128]{1,0:T(8,128)(2,1)S(1)} %collective-permute-done.7.a_ref, bf16[112,128]{1,0:T(8,128)(2,1)S(1)} %collective-permute-done.8.b_ref, ...), custom_call_target="tpu_custom_call", output_to_operand_aliasing={{2}: (5, {})} | custom-call | bytes 1048576 | tf_op jit(solution)/shard_map/pallas_call | solution.py:479
  (5 shorter events, 0.1 us)
Async XLA Ops:
  0.6 5.4 %copy-start = (bf16[1,2,64,4096]{3,2,1,0:T(8,128)(2,1)S(1)}, bf16[1,2,64,4096]{3,2,1,0:T(8,128)(2,1)}, u32[]{:S(2)}) copy-start(bf16[1,2,64,4096]{3,2,1,0:T(8,128)(2,1)} %param.8) | copy-start | bytes 3145732
  3.6 6.4 %collective-permute-start.1 = (bf16[528,128]{1,0:T(8,128)(2,1)S(1)}, bf16[528,128]{1,0:T(8,128)(2,1)S(1)}, u32[]{:S(2)}, u32[]{:S(2)}) collective-permute-start(bf16[528,128]{1,0:T(8,128)(2,1)S(1)} %get-tuple-element.55.sent_ref.refs_6_), channel_id=1, source_target_pairs={{0,3},{1,2},{2,1},{3,0},{4,7},{5,6},{6,5},{7,4},{8,11},{9,10},{10,... | collective-permute-start | bytes 405512 | tf_op jit(solution)/shard_map/ppermute | solution.py:494
  6.1 2.3 %copy-start.1 = (bf16[2,64,1024]{2,1,0:T(8,128)(2,1)S(1)}, bf16[2,64,1024]{2,1,0:T(8,128)(2,1)}, u32[]{:S(2)}) copy-start(bf16[2,64,1024]{2,1,0:T(8,128)(2,1)} %ws_ref.1) | copy-start | bytes 786436
  6.1 2.3 %copy-start.2 = (bf16[2,64,576]{2,1,0:T(8,128)(2,1)S(1)}, bf16[2,64,576]{2,1,0:T(8,128)(2,1)}, u32[]{:S(2)}) copy-start(bf16[2,64,576]{2,1,0:T(8,128)(2,1)} %wd_ref.1) | copy-start | bytes 442372
  7.6 2.5 %collective-permute-start.2 = (bf16[2,528,128]{2,1,0:T(8,128)(2,1)S(1)}, bf16[2,528,128]{2,1,0:T(8,128)(2,1)S(1)}, u32[]{:S(2)}, u32[]{:S(2)}) collective-permute-start(bf16[2,528,128]{2,1,0:T(8,128)(2,1)S(1)} %get-tuple-element.57), channel_id=1, source_target_pairs={{0,2},{2,0},{4,6},{6,4},{8,10},{10,8},{12,14},{14,12},{16,18},{18,... | collective-permute-start | bytes 811016 | tf_op jit(solution)/shard_map/ppermute | solution.py:498
  8.3 5.6 %collective-permute-start = (bf16[528,128]{1,0:T(8,128)(2,1)S(1)}, bf16[528,128]{1,0:T(8,128)(2,1)S(1)}, u32[]{:S(2)}, u32[]{:S(2)}) collective-permute-start(bf16[528,128]{1,0:T(8,128)(2,1)S(1)} %get-tuple-element.56.refs_7_), channel_id=1, source_target_pairs={{0,3},{1,2},{2,1},{3,0},{4,7},{5,6},{6,5},{7,4},{8,11},{9,10},{10,... | collective-permute-start | bytes 405512 | tf_op jit(solution)/shard_map/ppermute | solution.py:494
  14.9 1.4 %collective-permute-start.3 = (bf16[4,112,128]{2,1,0:T(8,128)(2,1)S(1)}, bf16[4,112,128]{2,1,0:T(8,128)(2,1)S(1)}, u32[]{:S(2)}, u32[]{:S(2)}) collective-permute-start(bf16[4,112,128]{2,1,0:T(8,128)(2,1)S(1)} %get-tuple-element.83), channel_id=1, source_target_pairs={{0,2},{2,0},{4,6},{6,4},{8,10},{10,8},{12,14},{14,12},{16,18},{18,... | collective-permute-start | bytes 344072 | tf_op jit(solution)/shard_map/ppermute | solution.py:498
  16.3 5.4 %collective-permute-start.4 = (bf16[224,128]{1,0:T(8,128)(2,1)S(1)}, bf16[224,128]{1,0:T(8,128)(2,1)S(1)}, u32[]{:S(2)}, u32[]{:S(2)}) collective-permute-start(bf16[224,128]{1,0:T(8,128)(2,1)S(1)} %get-tuple-element.86), channel_id=1, source_target_pairs={{0,12},{2,14},{4,8},{6,10},{8,4},{10,6},{12,0},{14,2},{16,28},{18,... | collective-permute-start | bytes 172040 | tf_op jit(solution)/shard_map/ppermute | solution.py:498
  18.9 4.2 %collective-permute-start.5 = (bf16[224,128]{1,0:T(8,128)(2,1)S(1)}, bf16[224,128]{1,0:T(8,128)(2,1)S(1)}, u32[]{:S(2)}, u32[]{:S(2)}) collective-permute-start(bf16[224,128]{1,0:T(8,128)(2,1)S(1)} %get-tuple-element.87), channel_id=1, source_target_pairs={{0,8},{2,10},{4,12},{6,14},{8,0},{10,2},{12,4},{14,6},{16,24},{18,... | collective-permute-start | bytes 172040 | tf_op jit(solution)/shard_map/ppermute | solution.py:498
  19.4 4.2 %collective-permute-start.6 = (bf16[224,128]{1,0:T(8,128)(2,1)S(1)}, bf16[224,128]{1,0:T(8,128)(2,1)S(1)}, u32[]{:S(2)}, u32[]{:S(2)}) collective-permute-start(bf16[224,128]{1,0:T(8,128)(2,1)S(1)} %get-tuple-element.88), channel_id=1, source_target_pairs={{0,4},{2,6},{4,0},{6,2},{8,12},{10,14},{12,8},{14,10},{16,20},{18,... | collective-permute-start | bytes 172040 | tf_op jit(solution)/shard_map/ppermute | solution.py:498
  23.6 5.9 %collective-permute-start.7 = (bf16[112,128]{1,0:T(8,128)(2,1)S(1)}, bf16[112,128]{1,0:T(8,128)(2,1)S(1)}, u32[]{:S(2)}, u32[]{:S(2)}) collective-permute-start(bf16[112,128]{1,0:T(8,128)(2,1)S(1)} %get-tuple-element.90), channel_id=1, source_target_pairs={{0,17},{1,16},{2,19},{3,18},{4,21},{5,20},{6,23},{7,22},{8,25},{9,... | collective-permute-start | bytes 86024 | tf_op jit(solution)/shard_map/ppermute | solution.py:494
  27.2 4.8 %collective-permute-start.8 = (bf16[112,128]{1,0:T(8,128)(2,1)S(1)}, bf16[112,128]{1,0:T(8,128)(2,1)S(1)}, u32[]{:S(2)}, u32[]{:S(2)}) collective-permute-start(bf16[112,128]{1,0:T(8,128)(2,1)S(1)} %get-tuple-element.90), channel_id=1, source_target_pairs={{0,16},{1,17},{2,18},{3,19},{4,20},{5,21},{6,22},{7,23},{8,24},{9,... | collective-permute-start | bytes 86024 | tf_op jit(solution)/shard_map/ppermute | solution.py:494
  27.5 4.4 %collective-permute-start.9 = (bf16[112,128]{1,0:T(8,128)(2,1)S(1)}, bf16[112,128]{1,0:T(8,128)(2,1)S(1)}, u32[]{:S(2)}, u32[]{:S(2)}) collective-permute-start(bf16[112,128]{1,0:T(8,128)(2,1)S(1)} %get-tuple-element.91), channel_id=1, source_target_pairs={{0,1},{1,0},{2,3},{3,2},{4,5},{5,4},{6,7},{7,6},{8,9},{9,8},{10,11... | collective-permute-start | bytes 86024 | tf_op jit(solution)/shard_map/ppermute | solution.py:494

commit v5 on v4

--- a/solution.py
+++ b/solution.py
@@ -49,14 +49,14 @@
     if dr == 0 and dc == 0:
         return x
     cells = side * side
-    return pltpu.roll(x, (-(dr * side + dc) * reach) % cells, 1) * masks[dr, dc]
-
-
-def phase_matrix(side, transposed):
+    return pltpu.roll(x, (-(dr * side + dc) * reach) % cells, 1) * masks[dr, dc].astype(x.dtype)
+
+
+def merge_matrix(side):
     size = 16 * side
     dims = (size, size)
-    source = lax.broadcasted_iota(jnp.int32, dims, 1 if transposed else 0)
-    target = lax.broadcasted_iota(jnp.int32, dims, 0 if transposed else 1)
+    source = lax.broadcasted_iota(jnp.int32, dims, 1)
+    target = lax.broadcasted_iota(jnp.int32, dims, 0)
     phase, cell = target // (4 * side), target % (4 * side)
     row, col = cell // side, cell % side
     wanted = (2 * row + phase // 2) * (2 * side) + 2 * col + phase % 2
@@ -69,7 +69,17 @@
     return jnp.where(core == 0, odd, even), jnp.where(core == 0, even, odd)
 
 
+def half_run_matrix(side, odd):
+    dims = (8 * side, 8 * side)
+    source, target = (lax.broadcasted_iota(jnp.int32, dims, k) for k in range(2))
+    phase, cell = target // (2 * side) ^ odd, target % (2 * side)
+    row, col = cell // side, cell % side
+    wanted = (2 * row + phase // 2) * (2 * side) + 2 * col + phase % 2
+    return jnp.where(source == wanted, 1.0, 0.0).astype(BF16)
+
+
 TAP_LINES = {0: (1, -1), 1: (0, 0), 2: (1, 0), 3: (0, 1)}
+ROW_ORDER = (1, 3, 2, 0)
 
 
 def tap_matrices(weight, taps, scratch):
@@ -80,30 +90,46 @@
 def forward_patch(x_ref, cot, w_strided, w_dilated, bias_col, ph_ref, pre_ref, act_ref, send_ref, im_scr):
     side = math.isqrt(x_ref.shape[1]) // 2
     run, lanes = 16 * side, side * side // 128
-    split = phase_matrix(side, False)
     near, far = shifted_masks(side, 1), shifted_masks(side, 2)
-    runs = x_ref.shape[1] // run
-    stacked = jnp.concatenate([x_ref[:, q * run : (q + 1) * run] for q in range(runs)], axis=0)
-    parts = dot(stacked, split).astype(BF16)
-    for q in range(runs):
-        for phase in range(4):
-            ph_ref[phase * CH : (phase + 1) * CH, q * 4 * side : (q + 1) * 4 * side] = parts[
-                q * CH : (q + 1) * CH, phase * 4 * side : (phase + 1) * 4 * side
-            ]
-    for rt in range(4):
+    runs, wide = x_ref.shape[1] // run, 4 * side
+    even, odd = (
+        dot(
+            jnp.concatenate(
+                [x_ref[:, q * run + h * run // 2 : q * run + (h + 1) * run // 2] for q in range(runs)], axis=0
+            ),
+            half_run_matrix(side, h),
+        )
+        for h in range(2)
+    )
+    lower = lax.broadcasted_iota(jnp.int32, (runs * CH, wide), 1) < wide // 2
+    for pr in range(2):
+        one, two = even[:, pr * wide : (pr + 1) * wide], odd[:, pr * wide : (pr + 1) * wide]
+        first = jnp.where(lower, one, two).astype(BF16)
+        second = pltpu.roll(jnp.where(lower, two, one).astype(BF16), wide // 2, 1)
+        for pc, lines in ((0, first), (1, second)):
+            for q in range(runs):
+                at = (pr * 2 + pc) * CH
+                ph_ref[at : at + CH, q * wide : (q + 1) * wide] = lines[q * CH : (q + 1) * CH]
+    sums = []
+    for pr in range(2):
         for ct in range(4):
-            (pr, dr), (pc, dc) = TAP_LINES[rt], TAP_LINES[ct]
-            phase, tap = pr * 2 + pc, rt * 4 + ct
-            im_scr[tap * CH : (tap + 1) * CH, :] = shifted(
-                ph_ref[phase * CH : (phase + 1) * CH, :], dr, dc, side, 1, near
-            )
-    pre = dot(w_strided, im_scr[...]) + bias_col
+            pc, dc = TAP_LINES[ct]
+            at, phase = (pr * 4 + ct) * CH, pr * 2 + pc
+            im_scr[at : at + CH, :] = shifted(ph_ref[phase * CH : (phase + 1) * CH, :], 0, dc, side, 1, near)
+        both = dot(w_strided[pr * 2 * CH : (pr + 1) * 2 * CH], im_scr[pr * 4 * CH : (pr + 1) * 4 * CH, :])
+        dr = TAP_LINES[ROW_ORDER[2 * pr + 1]][1]
+        sums.append(both[:CH] + shifted(both[CH:], dr, 0, side, 1, near))
+    pre = sums[0] + sums[1] + bias_col
     pre_ref[...] = pre
     act = (pre * (1.0 / (1.0 + jnp.exp(-pre)))).astype(BF16)
     act_ref[...] = act
-    for tap, (dr, dc) in enumerate(SHIFTS):
-        im_scr[tap * CH : (tap + 1) * CH, :] = shifted(act, dr, dc, side, 2, far)
-    out = dot(w_dilated, im_scr[0 : DIL_TAPS * CH, :]).astype(BF16)
+    for k in range(3):
+        im_scr[k * CH : (k + 1) * CH, :] = shifted(act, 0, k - 1, side, 2, far)
+    rows = dot(w_dilated, im_scr[0 : 3 * CH, :])
+    out = rows[CH : 2 * CH]
+    for k in (0, 2):
+        out = out + shifted(rows[k * CH : (k + 1) * CH], k - 1, 0, side, 2, far)
+    out = out.astype(BF16)
     for lane in range(lanes):
         send_ref[lane * CH : (lane + 1) * CH, :] = out[:, lane * 128 : (lane + 1) * 128]
     rows = [cot[:, lane * 128 : (lane + 1) * 128] for lane in range(lanes)]
@@ -136,9 +162,13 @@
     for copy in copies:
         copy.wait()
     mats = tap_matrices(ws_ref[...], 16, wscr)
-    strided_ref[...] = jnp.concatenate(mats, axis=0).T.astype(BF16)
+    for k, rt in enumerate(ROW_ORDER):
+        line = jnp.concatenate(mats[rt * 4 : rt * 4 + 4], axis=0)
+        strided_ref[k * CH : (k + 1) * CH, :] = line.T.astype(BF16)
     mats = tap_matrices(wd_ref[...], 9, wscr)
-    dilated_ref[...] = jnp.concatenate(mats, axis=0).T.astype(BF16)
+    for k in range(3):
+        line = jnp.concatenate(mats[3 * k : 3 * k + 3], axis=0)
+        dilated_ref[k * CH : (k + 1) * CH, :] = line.T.astype(BF16)
     bias_row = table_ref[pl.ds(owner_ref[scene], 1), :]
     bias_ref[...] = jnp.broadcast_to(jnp.broadcast_to(bias_row, (8, CH)).T[:, 0:1], (CH, 128))
     forward_patch(
@@ -251,14 +281,18 @@
             target[at : at + rows, :] = shifted(piece, dr, dc, side, reach, masks)
 
 
-def backward_patch(position, candidates, select_ref, cot_ref, wt_ref, slope_ref, shift_scr):
+def pick(position, candidates, select_ref, first=0):
+    partner = None
+    for k, payload in enumerate(candidates, first):
+        term = payload * select_ref[position * 4 + k : position * 4 + k + 1, :].astype(BF16)
+        partner = term if partner is None else partner + term
+    return partner
+
+
+def backward_patch(position, partner, select_ref, cot_ref, wt_ref, slope_ref, shift_scr):
     side = math.isqrt(slope_ref.shape[1])
     lanes = side * side // 128
     core = lax.axis_index("scene") % 2
-    partner = None
-    for k, payload in enumerate(candidates):
-        term = payload * select_ref[position * 4 + k : position * 4 + k + 1, :].astype(BF16)
-        partner = term if partner is None else partner + term
     live = select_ref[8 + position : 9 + position, :]
     signal = (cot_ref[position * 16 : position * 16 + 16, :] + partner[lanes * CH :, :].astype(F32)) * live
     out_grad = jnp.concatenate(
@@ -270,12 +304,13 @@
 
 def backward_first_kernel(
     far0_ref, near_ref, select_ref, cot_ref, wt_ref, act_ref, slope_ref, ph_ref,
-    pre_b_ref, bias_ref, dilated_ref, strided_ref, shift_scr,
+    pick_ref, pre_b_ref, bias_ref, dilated_ref, strided_ref, shift_scr,
 ):
     side = math.isqrt(slope_ref.shape[1])
     core = lax.axis_index("scene") % 2
     candidates = (near_ref[0], near_ref[1], far0_ref[...])
-    pre_grad = backward_patch(0, candidates, select_ref, cot_ref, wt_ref, slope_ref, shift_scr)
+    pick_ref[...] = pick(1, candidates, select_ref)
+    pre_grad = backward_patch(0, pick(0, candidates, select_ref), select_ref, cot_ref, wt_ref, slope_ref, shift_scr)
     act = act_ref[...]
     dilated_ref[...] = dot_nt(shift_scr[...], jnp.concatenate([act, act], axis=0))
     bias_ref[...] = jnp.broadcast_to(jnp.sum(pre_grad, axis=1, keepdims=True), bias_ref.shape)
@@ -317,42 +352,44 @@
 
 
 def backward_second_kernel(
-    far1_ref, far0_ref, near_ref, select_ref, cot_ref, wt_ref, act_ref, slope_ref, ph_ref,
-    other_ref, other_bias_ref, other_dilated_ref, other_strided_ref,
-    pre_b0_ref, pre_b1_ref, bias_ref, give_ref, out_shifts_ref, kept_ref, shift_scr, *, chunked,
+    far1_ref, pick_ref, select_ref, cot_ref, wt_ref, act_ref, slope_ref, ph_ref,
+    other_bias_ref, other_dilated_ref, other_strided_ref,
+    pre_b_ref, bias_ref, give_ref, out_shifts_ref, shift_scr, *, chunked,
 ):
     side = math.isqrt(slope_ref.shape[1])
     core = lax.axis_index("scene") % 2
-    candidates = (near_ref[0], near_ref[1], far0_ref[...], far1_ref[...])
-    pre_grad = backward_patch(1, candidates, select_ref, cot_ref, wt_ref, slope_ref, out_shifts_ref)
+    partner = pick_ref[...] + pick(1, (far1_ref[...],), select_ref, 3)
+    pre_grad = backward_patch(1, partner, select_ref, cot_ref, wt_ref, slope_ref, out_shifts_ref)
     act = act_ref[...]
     dilated = dot_nt(out_shifts_ref[0:HALF, :], jnp.concatenate([act, act], axis=0))
-    give, keep = (piece.astype(BF16) for piece in halves(pre_grad, core))
-    shift_rows([give], 1, side, shift_scr)
+    give, _ = halves(pre_grad, core)
+    shift_rows([give.astype(BF16)], 1, side, shift_scr)
     strided = dot_nt(shift_scr[...], ph_ref[...])
-    kept_ref[...] = keep
+    pre_b_ref[...] = pre_grad.astype(BF16)
     bias_wide = (jnp.sum(pre_grad, axis=1, keepdims=True) + other_bias_ref[...]).T[0:8, :]
     bias_wide = jnp.concatenate([bias_wide, jnp.zeros_like(bias_wide)], axis=1)
     bias_ref[...] = bias_wide
     blocks = tap_blocks(strided + other_strided_ref[0:HALF, :], dilated + other_dilated_ref[0:HALF, :])
     write_blocks(blocks, bias_wide, give_ref, chunked)
-    pre_b = pre_grad.astype(BF16)
-    swapped = select_ref[10:11, 0:1].astype(BF16)
-    straight = 1.0 - swapped
-    pre_b0_ref[...] = other_ref[...] * straight + pre_b * swapped
-    pre_b1_ref[...] = other_ref[...] * swapped + pre_b * straight
 
 
 def backward_kept_kernel(
-    out_shifts_ref, kept_pre_ref, act_ref, ph_ref, other_dilated_ref, other_strided_ref, keep_ref, shift_scr, *, chunked
+    select_ref, out_shifts_ref, pre_b_ref, other_ref, act_ref, ph_ref, other_dilated_ref, other_strided_ref,
+    keep_ref, pre_b0_ref, pre_b1_ref, shift_scr, *, chunked,
 ):
     side = math.isqrt(act_ref.shape[1])
     act = act_ref[...]
     dilated = dot_nt(out_shifts_ref[HALF:, :], jnp.concatenate([act, act], axis=0))
-    shift_rows([kept_pre_ref[...]], 1, side, shift_scr)
+    pre_b, other = pre_b_ref[...], other_ref[...]
+    _, keep = halves(pre_b.astype(F32), lax.axis_index("scene") % 2)
+    shift_rows([keep.astype(BF16)], 1, side, shift_scr)
     strided = dot_nt(shift_scr[...], ph_ref[...])
     blocks = tap_blocks(strided + other_strided_ref[HALF:, :], dilated + other_dilated_ref[HALF:, :])
     write_blocks(blocks, jnp.zeros((8, 2 * CH), F32), keep_ref, chunked)
+    swapped = select_ref[10:11, 0:1].astype(BF16)
+    straight = 1.0 - swapped
+    pre_b0_ref[...] = other * straight + pre_b * swapped
+    pre_b1_ref[...] = other * swapped + pre_b * straight
 
 
 def spread_kernel(place_ref, bias_ref, keep_ref, got_ref, *out_refs):
@@ -436,7 +473,7 @@
 def feature_patch(pre_b_ref, wf_ref, out_ref, shift_scr):
     side = math.isqrt(pre_b_ref.shape[1])
     near = shifted_masks(side, 1)
-    merge = phase_matrix(side, True)
+    merge = merge_matrix(side)
     run, wide = 16 * side, 4 * side
     pre_b = pre_b_ref[...]
     for s, (dr, dc) in enumerate(SHIFTS):
@@ -560,11 +597,11 @@
     payload = (cells * channels // 128 + 16, 128)
     chunked = scenes == 16 and tiles == 2 and patches == 2 and bias_rows == 1
     wscr = ((16 * channels, 2 * channels), F32)
-    im_scr = ((16 * channels, cells), BF16)
+    im_scr = ((8 * channels, cells), BF16)
     patch_outs = [((4 * channels, cells), BF16), (grid, F32), (grid, BF16), (payload, BF16)]
     first_outs = patch_outs + [
-        ((channels, 16 * channels), BF16),
-        ((channels, 9 * channels), BF16),
+        ((4 * channels, 4 * channels), BF16),
+        ((3 * channels, 3 * channels), BF16),
         ((channels, 128), F32),
         (own_cot.shape, BF16),
     ]
@@ -623,9 +660,9 @@
     slope, act, phases = both[0:2], both[2:4], both[4:6]
     shift_scr = ((9 * channels, cells), BF16)
     sums = [((9 * channels, 128), F32), ((9 * channels, 4 * channels), F32)]
-    first = call(
+    picked, *first = call(
         backward_first_kernel,
-        [(grid, BF16), ((channels, 128), F32)] + sums,
+        [(payload, BF16), (grid, BF16), ((channels, 128), F32)] + sums,
         "v" * 8,
         [shift_scr],
         far[0], near, select, cots, w_act, act[0], slope[0], phases[0],
@@ -633,22 +670,22 @@
     )
     half_shift = ((9 * channels // 2, cells), BF16)
     grads_shape = ((4, BLOCKS * 8, 128), BF16) if chunked else ((BLOCKS - 1, channels // 2, 128), F32)
-    *pre_b, bias, give, out_shifts, kept_rows = call(
+    last, bias, give, out_shifts = call(
         functools.partial(backward_second_kernel, chunked=chunked),
-        [(grid, BF16)] * 2 + [((8, 128), F32), grads_shape, shift_scr, ((channels // 2, cells), BF16)],
-        "v" * 13,
+        [(grid, BF16), ((8, 128), F32), grads_shape, shift_scr],
+        "v" * 11,
         [half_shift],
-        far[1], far[0], near, select, cots, w_act, act[1], slope[1], phases[1], *first,
+        far[1], picked, select, cots, w_act, act[1], slope[1], phases[1], *first[1:],
         flops=10**9,
     )
     if chunked:
         got = scene_xor(give, 1)
-    (keep,) = call(
+    keep, *pre_b = call(
         functools.partial(backward_kept_kernel, chunked=chunked),
-        [grads_shape],
-        "v" * 6,
+        [grads_shape] + [(grid, BF16)] * 2,
+        "v" * 8,
         [half_shift],
-        out_shifts, kept_rows, act[1], phases[1], *first[2:],
+        select, out_shifts, last, first[0], act[1], phases[1], *first[2:],
         flops=10**9,
     )
     feature_shape = ((channels, cells_in), BF16)

time: 33.4 us -> 33.2 us (level)
  no operation moved by 1% of the time
where the time goes in v5:
time: 33.2 us; the launch traced here: 33.1 us
  Pallas kernels  11.7 us (35%)
  starting transfers between devices  11.4 us (34%)
  waiting for transfers between devices  9.28 us (28%)
  between operations  0.7 us (2%)
    pallas_call x11, Pallas kernels, call(): pl.pallas_call(kernel, out_shape=[jax.ShapeDtypeStruct(shape, kind) for s...  11.7 us
    ppermute x5, starting transfers between devices, device_pairs(): return lax.ppermute(x, ('scene', 'tile'), flat)  6.95 us
    ppermute x5, waiting for transfers between devices, device_pairs(): return lax.ppermute(x, ('scene', 'tile'), flat)  5.96 us
    ppermute x5, starting transfers between devices, scene_xor(): lax.ppermute(x, 'scene', [(i, i ^ distance) for i in range(lax.axis_size(...  4.47 us
    ppermute x5, waiting for transfers between devices, scene_xor(): lax.ppermute(x, 'scene', [(i, i ^ distance) for i in range(lax.axis_size(...  3.31 us
  transfers between devices with their start and end apart: 10, of which 8 were waited for; matrix products, arithmetic and copies ran while one was open for 0% of the time, Pallas kernels for 20%

profile of v5, /device:TPU:0, one launch (start us, length us, event | category | flops | bytes accessed | tf_op | source)
XLA Modules:
  0.0 33.1 jit_solution(16937094266923121766)
XLA Ops:
  0.6 0.0 copy-start
  0.6 2.9 %shard_map.103 = (bf16[256,1024]{1,0:T(8,128)(2,1)S(1)}, f32[64,1024]{1,0:T(8,128)S(1)}, bf16[64,1024]{1,0:T(8,128)(2,1)S(1)}, bf16[528,128]{1,0:T(8,128)(2,1)S(...) custom-call(s32[16]{0:T(128)} %owner_hbm.3, ...), custom_call_target="tpu_custom_call" | custom-call | flops 1000000000 | bytes 1048576 | tf_op jit(solution)/shard_map/pallas_call | solution.py:516
  3.5 2.4 %collective-permute-start.1 = (bf16[528,128]{1,0:T(8,128)(2,1)S(1)}, bf16[528,128]{1,0:T(8,128)(2,1)S(1)}, u32[]{:S(2)}, u32[]{:S(2)}) collective-permute-start(bf16[528,128]{1,0:T(8,128)(2,1)S(1)} %get-tuple-element.58.sent_ref.refs_6_), channel_id=1, source_target_pairs={{0,3},{1,2},{2,1},{3,0},{4,7},{5,6},{6,5},{7,4},{8,11},{9,10},{10,... | collective-permute-start | bytes 405512 | tf_op jit(solution)/shard_map/ppermute | solution.py:531
  6.0 0.0 copy-done
  6.0 1.4 %shard_map.104 = (bf16[256,1024]{1,0:T(8,128)(2,1)S(1)}, f32[64,1024]{1,0:T(8,128)S(1)}, bf16[64,1024]{1,0:T(8,128)(2,1)S(1)}, bf16[528,128]{1,0:T(8,128)(2,1)S(1)}, bf16[2,528,128]{2,1,0:T(8,128)(2,1)S(1)}) custom-call(bf16[2,64,4096]{2,1,0:T(8,128)(2,1)S(1)} %bitcast.5, bf16[2,1024]{1,0:T(2,128)(2,1)S(1)} %get-tuple-element.54.cot_ref, ...), custom_call_target="tpu_custom_call" | custom-call | flops 10000000000 | bytes 1048576 | tf_op jit(solution)/shard_map/pallas_call | solution.py:516
  7.4 0.7 %collective-permute-start.2 = (bf16[2,528,128]{2,1,0:T(8,128)(2,1)S(1)}, bf16[2,528,128]{2,1,0:T(8,128)(2,1)S(1)}, u32[]{:S(2)}, u32[]{:S(2)}) collective-permute-start(bf16[2,528,128]{2,1,0:T(8,128)(2,1)S(1)} %get-tuple-element.66), channel_id=1, source_target_pairs={{0,2},{2,0},{4,6},{6,4},{8,10},{10,8},{12,14},{14,12},{16,18},{18,... | collective-permute-start | bytes 811016 | tf_op jit(solution)/shard_map/ppermute | solution.py:535
  8.1 0.1 collective-permute-start
  8.2 0.0 copy-done.1
  8.2 1.2 %shard_map.105 = (f32[64,1024]{1,0:T(8,128)S(1)}, f32[64,1024]{1,0:T(8,128)S(1)}, bf16[64,1024]{1,0:T(8,128)(2,1)S(1)}, bf16[64,1024]{1,0:T(8,128)(2,1)S(1)}, bf...) custom-call(s32[4,8]{1,0:T(4,128)} %bitcast.8, ...), custom_call_target="tpu_custom_call" | custom-call | flops 10000000000 | bytes 1048576 | tf_op jit(solution)/shard_map/pallas_call | solution.py:516
  9.4 0.5 %collective-permute-done.1.far0_ref = bf16[528,128]{1,0:T(8,128)(2,1)S(1)} collective-permute-done((bf16[528,128]{1,0:T(8,128)(2,1)S(1)}, bf16[528,128]{1,0:T(8,128)(2,1)S(1)}, u32[]{:S(2)}, u32[]{:S(2)}) %collective-permute-start.1) | collective-permute-done | bytes 135200 | tf_op jit(solution)/shard_map/ppermute | solution.py:531
  10.0 0.0 collective-permute-done.2.near_ref
  10.0 1.3 %shard_map.106 = (bf16[528,128]{1,0:T(8,128)(2,1)S(1)}, bf16[64,1024]{1,0:T(8,128)(2,1)S(1)}, f32[64,128]{1,0:T(8,128)S(1)}, f32[576,128]{1,0:T(8,128)S(1)}, f32[576,256]{1,0:T(8,128)S(1)}) custom-call(bf16[528,128]{1,0:T(8,128)(2,1)S(1)} %collective-permute-done.1.far0_ref, bf16[2,528,128]{2,1,0:T(8,128)(2,1)S(1)} %collective-permute-done.2.near_ref, ...), custom_call_target="tpu_custom_call" | custom-call | flops 1000000000 | bytes 1048576 | tf_op jit(solution)/shard_map/pallas_call | solution.py:516
  11.2 2.5 %collective-permute-done.far1_ref = bf16[528,128]{1,0:T(8,128)(2,1)S(1)} collective-permute-done((bf16[528,128]{1,0:T(8,128)(2,1)S(1)}, bf16[528,128]{1,0:T(8,128)(2,1)S(1)}, u32[]{:S(2)}, u32[]{:S(2)}) %collective-permute-start) | collective-permute-done | bytes 135200 | tf_op jit(solution)/shard_map/ppermute | solution.py:531
  13.7 0.9 %shard_map.107 = (bf16[64,1024]{1,0:T(8,128)(2,1)S(1)}, f32[8,128]{1,0:T(8,128)S(1)}, bf16[4,112,128]{2,1,0:T(8,128)(2,1)S(1)}, bf16[576,1024]{1,0:T(8,128)(2,1)S(1)}) custom-call(bf16[528,128]{1,0:T(8,128)(2,1)S(1)} %collective-permute-done.far1_ref, bf16[528,128]{1,0:T(8,128)(2,1)S(1)} %get-tuple-element.72.pick_ref, ...), custom_call_target="tpu_custom_call" | custom-call | flops 1000000000 | bytes 1048576 | tf_op jit(solution)/shard_map/pallas_call | solution.py:516
  14.7 0.2 collective-permute-start.3
  14.9 0.5 %shard_map.108 = (bf16[4,112,128]{2,1,0:T(8,128)(2,1)S(1)}, bf16[64,1024]{1,0:T(8,128)(2,1)S(1)}, bf16[64,1024]{1,0:T(8,128)(2,1)S(1)}) custom-call(f32[16,128]{1,0:T(8,128)S(1)} %get-tuple-element.65.select_ref, bf16[576,1024]{1,0:T(8,128)(2,1)S(1)} %get-tuple-element.79.out_shifts_ref, bf16[64,1024]{1,0:T(8,128)(2,1)S(1)} %get-tuple-element.80.pre_b_ref, ...), custom_call_target="tpu_custom_call" | custom-call | flops 1000000000 | bytes 1048576 | tf_op jit(solution)/shard_map/pallas_call | solution.py:516
  15.4 0.7 %collective-permute-done.3.got_ref = bf16[4,112,128]{2,1,0:T(8,128)(2,1)S(1)} collective-permute-done((bf16[4,112,128]{2,1,0:T(8,128)(2,1)S(1)}, bf16[4,112,128]{2,1,0:T(8,128)(2,1)S(1)}, u32[]{:S(2)}, u32[]{:S(2)}) %collective-permute-start.3) | collective-permute-done | bytes 114720 | tf_op jit(solution)/shard_map/ppermute | solution.py:535
  16.1 2.6 %collective-permute-start.4 = (bf16[224,128]{1,0:T(8,128)(2,1)S(1)}, bf16[224,128]{1,0:T(8,128)(2,1)S(1)}, u32[]{:S(2)}, u32[]{:S(2)}) collective-permute-start(bf16[224,128]{1,0:T(8,128)(2,1)S(1)} %get-tuple-element.90), channel_id=1, source_target_pairs={{0,12},{2,14},{4,8},{6,10},{8,4},{10,6},{12,0},{14,2},{16,28},{18,... | collective-permute-start | bytes 172040 | tf_op jit(solution)/shard_map/ppermute | solution.py:535
  18.7 0.5 %collective-permute-start.5 = (bf16[224,128]{1,0:T(8,128)(2,1)S(1)}, bf16[224,128]{1,0:T(8,128)(2,1)S(1)}, u32[]{:S(2)}, u32[]{:S(2)}) collective-permute-start(bf16[224,128]{1,0:T(8,128)(2,1)S(1)} %get-tuple-element.91), channel_id=1, source_target_pairs={{0,8},{2,10},{4,12},{6,14},{8,0},{10,2},{12,4},{14,6},{16,24},{18,... | collective-permute-start | bytes 172040 | tf_op jit(solution)/shard_map/ppermute | solution.py:535
  19.2 0.5 %collective-permute-start.6 = (bf16[224,128]{1,0:T(8,128)(2,1)S(1)}, bf16[224,128]{1,0:T(8,128)(2,1)S(1)}, u32[]{:S(2)}, u32[]{:S(2)}) collective-permute-start(bf16[224,128]{1,0:T(8,128)(2,1)S(1)} %get-tuple-element.92), channel_id=1, source_target_pairs={{0,4},{2,6},{4,0},{6,2},{8,12},{10,14},{12,8},{14,10},{16,20},{18,... | collective-permute-start | bytes 172040 | tf_op jit(solution)/shard_map/ppermute | solution.py:535
  19.7 1.0 %shard_map.109.first_ref = bf16[64,4096]{1,0:T(8,128)(2,1)S(1)} custom-call(bf16[64,1024]{1,0:T(8,128)(2,1)S(1)} %get-tuple-element.82.pre_b_ref, bf16[256,576]{1,0:T(8,128)(2,1)S(1)} %get-tuple-element.83.wf_ref), custom_call_target="tpu_custom_call" | custom-call | flops 1000000000 | bytes 1048576 | tf_op jit(solution)/shard_map/pallas_call | solution.py:516
  20.7 0.7 %collective-permute-done.4.a_ref = bf16[224,128]{1,0:T(8,128)(2,1)S(1)} collective-permute-done((bf16[224,128]{1,0:T(8,128)(2,1)S(1)}, bf16[224,128]{1,0:T(8,128)(2,1)S(1)}, u32[]{:S(2)}, u32[]{:S(2)}) %collective-permute-start.4) | collective-permute-done | bytes 57376 | tf_op jit(solution)/shard_map/ppermute | solution.py:535
  21.5 1.4 %collective-permute-done.5.b_ref = bf16[224,128]{1,0:T(8,128)(2,1)S(1)} collective-permute-done((bf16[224,128]{1,0:T(8,128)(2,1)S(1)}, bf16[224,128]{1,0:T(8,128)(2,1)S(1)}, u32[]{:S(2)}, u32[]{:S(2)}) %collective-permute-start.5) | collective-permute-done | bytes 57376 | tf_op jit(solution)/shard_map/ppermute | solution.py:535
  22.9 0.5 %collective-permute-done.6.c_ref = bf16[224,128]{1,0:T(8,128)(2,1)S(1)} collective-permute-done((bf16[224,128]{1,0:T(8,128)(2,1)S(1)}, bf16[224,128]{1,0:T(8,128)(2,1)S(1)}, u32[]{:S(2)}, u32[]{:S(2)}) %collective-permute-start.6) | collective-permute-done | bytes 57376 | tf_op jit(solution)/shard_map/ppermute | solution.py:535
  23.4 3.7 %collective-permute-start.7 = (bf16[112,128]{1,0:T(8,128)(2,1)S(1)}, bf16[112,128]{1,0:T(8,128)(2,1)S(1)}, u32[]{:S(2)}, u32[]{:S(2)}) collective-permute-start(bf16[112,128]{1,0:T(8,128)(2,1)S(1)} %get-tuple-element.94), channel_id=1, source_target_pairs={{0,17},{1,16},{2,19},{3,18},{4,21},{5,20},{6,23},{7,22},{8,25},{9,... | collective-permute-start | bytes 86024 | tf_op jit(solution)/shard_map/ppermute | solution.py:531
  27.0 0.3 %collective-permute-start.8 = (bf16[112,128]{1,0:T(8,128)(2,1)S(1)}, bf16[112,128]{1,0:T(8,128)(2,1)S(1)}, u32[]{:S(2)}, u32[]{:S(2)}) collective-permute-start(bf16[112,128]{1,0:T(8,128)(2,1)S(1)} %get-tuple-element.94), channel_id=1, source_target_pairs={{0,16},{1,17},{2,18},{3,19},{4,20},{5,21},{6,22},{7,23},{8,24},{9,... | collective-permute-start | bytes 86024 | tf_op jit(solution)/shard_map/ppermute | solution.py:531
  27.4 0.5 %collective-permute-start.9 = (bf16[112,128]{1,0:T(8,128)(2,1)S(1)}, bf16[112,128]{1,0:T(8,128)(2,1)S(1)}, u32[]{:S(2)}, u32[]{:S(2)}) collective-permute-start(bf16[112,128]{1,0:T(8,128)(2,1)S(1)} %get-tuple-element.95), channel_id=1, source_target_pairs={{0,1},{1,0},{2,3},{3,2},{4,5},{5,4},{6,7},{7,6},{8,9},{9,8},{10,11... | collective-permute-start | bytes 86024 | tf_op jit(solution)/shard_map/ppermute | solution.py:531
  27.8 1.0 %shard_map.112 = (bf16[64,4096]{1,0:T(8,128)(2,1)S(1)}, bf16[2,64,4096]{2,1,0:T(8,128)(2,1)}) custom-call(bf16[64,1024]{1,0:T(8,128)(2,1)S(1)} %get-tuple-element.96.pre_b_ref, bf16[256,576]{1,0:T(8,128)(2,1)S(1)} %get-tuple-element.83.wf_ref, bf16[64,4096]{1,0:T(8,128)(2,1)S(1)} %shard_map.109.first_ref), custom_call_target="tpu_custom_call" | custom-call | flops 1000000000 | bytes 1048576 | tf_op jit(solution)/shard_map/pallas_call | solution.py:516
  28.9 0.4 %collective-permute-done.7.a_ref = bf16[112,128]{1,0:T(8,128)(2,1)S(1)} collective-permute-done((bf16[112,128]{1,0:T(8,128)(2,1)S(1)}, bf16[112,128]{1,0:T(8,128)(2,1)S(1)}, u32[]{:S(2)}, u32[]{:S(2)}) %collective-permute-start.7) | collective-permute-done | bytes 28704 | tf_op jit(solution)/shard_map/ppermute | solution.py:531
  29.3 2.5 %collective-permute-done.8.b_ref = bf16[112,128]{1,0:T(8,128)(2,1)S(1)} collective-permute-done((bf16[112,128]{1,0:T(8,128)(2,1)S(1)}, bf16[112,128]{1,0:T(8,128)(2,1)S(1)}, u32[]{:S(2)}, u32[]{:S(2)}) %collective-permute-start.8) | collective-permute-done | bytes 28704 | tf_op jit(solution)/shard_map/ppermute | solution.py:531
  31.8 0.0 collective-permute-done.9.c_ref
  31.8 1.3 %shard_map.113 = (f32[8,1600]{1,0:T(8,128)}, f32[1,64]{1,0:T(1,128)}, bf16[2,64,4096]{2,1,0:T(8,128)(2,1)}) custom-call(f32[112,128]{1,0:T(8,128)S(1)} %get-tuple-element.93.own_ref, bf16[112,128]{1,0:T(8,128)(2,1)S(1)} %collective-permute-done.7.a_ref, bf16[112,128]{1,0:T(8,128)(2,1)S(1)} %collective-permute-done.8.b_ref, ...), custom_call_target="tpu_custom_call", output_to_operand_aliasing={{2}: (5, {})} | custom-call | bytes 1048576 | tf_op jit(solution)/shard_map/pallas_call | solution.py:516
  (5 shorter events, 0.1 us)
Async XLA Ops:
  0.6 5.4 %copy-start = (bf16[1,2,64,4096]{3,2,1,0:T(8,128)(2,1)S(1)}, bf16[1,2,64,4096]{3,2,1,0:T(8,128)(2,1)}, u32[]{:S(2)}) copy-start(bf16[1,2,64,4096]{3,2,1,0:T(8,128)(2,1)} %param.8) | copy-start | bytes 3145732
  3.5 6.4 %collective-permute-start.1 = (bf16[528,128]{1,0:T(8,128)(2,1)S(1)}, bf16[528,128]{1,0:T(8,128)(2,1)S(1)}, u32[]{:S(2)}, u32[]{:S(2)}) collective-permute-start(bf16[528,128]{1,0:T(8,128)(2,1)S(1)} %get-tuple-element.58.sent_ref.refs_6_), channel_id=1, source_target_pairs={{0,3},{1,2},{2,1},{3,0},{4,7},{5,6},{6,5},{7,4},{8,11},{9,10},{10,... | collective-permute-start | bytes 405512 | tf_op jit(solution)/shard_map/ppermute | solution.py:531
  6.0 2.2 %copy-start.1 = (bf16[2,64,1024]{2,1,0:T(8,128)(2,1)S(1)}, bf16[2,64,1024]{2,1,0:T(8,128)(2,1)}, u32[]{:S(2)}) copy-start(bf16[2,64,1024]{2,1,0:T(8,128)(2,1)} %ws_ref.1) | copy-start | bytes 786436
  6.0 2.2 %copy-start.2 = (bf16[2,64,576]{2,1,0:T(8,128)(2,1)S(1)}, bf16[2,64,576]{2,1,0:T(8,128)(2,1)}, u32[]{:S(2)}) copy-start(bf16[2,64,576]{2,1,0:T(8,128)(2,1)} %wd_ref.1) | copy-start | bytes 442372
  7.4 2.6 %collective-permute-start.2 = (bf16[2,528,128]{2,1,0:T(8,128)(2,1)S(1)}, bf16[2,528,128]{2,1,0:T(8,128)(2,1)S(1)}, u32[]{:S(2)}, u32[]{:S(2)}) collective-permute-start(bf16[2,528,128]{2,1,0:T(8,128)(2,1)S(1)} %get-tuple-element.66), channel_id=1, source_target_pairs={{0,2},{2,0},{4,6},{6,4},{8,10},{10,8},{12,14},{14,12},{16,18},{18,... | collective-permute-start | bytes 811016 | tf_op jit(solution)/shard_map/ppermute | solution.py:535
  8.1 5.6 %collective-permute-start = (bf16[528,128]{1,0:T(8,128)(2,1)S(1)}, bf16[528,128]{1,0:T(8,128)(2,1)S(1)}, u32[]{:S(2)}, u32[]{:S(2)}) collective-permute-start(bf16[528,128]{1,0:T(8,128)(2,1)S(1)} %get-tuple-element.64.refs_7_), channel_id=1, source_target_pairs={{0,3},{1,2},{2,1},{3,0},{4,7},{5,6},{6,5},{7,4},{8,11},{9,10},{10,... | collective-permute-start | bytes 405512 | tf_op jit(solution)/shard_map/ppermute | solution.py:531
  14.7 1.4 %collective-permute-start.3 = (bf16[4,112,128]{2,1,0:T(8,128)(2,1)S(1)}, bf16[4,112,128]{2,1,0:T(8,128)(2,1)S(1)}, u32[]{:S(2)}, u32[]{:S(2)}) collective-permute-start(bf16[4,112,128]{2,1,0:T(8,128)(2,1)S(1)} %get-tuple-element.87), channel_id=1, source_target_pairs={{0,2},{2,0},{4,6},{6,4},{8,10},{10,8},{12,14},{14,12},{16,18},{18,... | collective-permute-start | bytes 344072 | tf_op jit(solution)/shard_map/ppermute | solution.py:535
  16.1 5.3 %collective-permute-start.4 = (bf16[224,128]{1,0:T(8,128)(2,1)S(1)}, bf16[224,128]{1,0:T(8,128)(2,1)S(1)}, u32[]{:S(2)}, u32[]{:S(2)}) collective-permute-start(bf16[224,128]{1,0:T(8,128)(2,1)S(1)} %get-tuple-element.90), channel_id=1, source_target_pairs={{0,12},{2,14},{4,8},{6,10},{8,4},{10,6},{12,0},{14,2},{16,28},{18,... | collective-permute-start | bytes 172040 | tf_op jit(solution)/shard_map/ppermute | solution.py:535
  18.7 4.2 %collective-permute-start.5 = (bf16[224,128]{1,0:T(8,128)(2,1)S(1)}, bf16[224,128]{1,0:T(8,128)(2,1)S(1)}, u32[]{:S(2)}, u32[]{:S(2)}) collective-permute-start(bf16[224,128]{1,0:T(8,128)(2,1)S(1)} %get-tuple-element.91), channel_id=1, source_target_pairs={{0,8},{2,10},{4,12},{6,14},{8,0},{10,2},{12,4},{14,6},{16,24},{18,... | collective-permute-start | bytes 172040 | tf_op jit(solution)/shard_map/ppermute | solution.py:535
  19.2 4.2 %collective-permute-start.6 = (bf16[224,128]{1,0:T(8,128)(2,1)S(1)}, bf16[224,128]{1,0:T(8,128)(2,1)S(1)}, u32[]{:S(2)}, u32[]{:S(2)}) collective-permute-start(bf16[224,128]{1,0:T(8,128)(2,1)S(1)} %get-tuple-element.92), channel_id=1, source_target_pairs={{0,4},{2,6},{4,0},{6,2},{8,12},{10,14},{12,8},{14,10},{16,20},{18,... | collective-permute-start | bytes 172040 | tf_op jit(solution)/shard_map/ppermute | solution.py:535
  23.4 5.9 %collective-permute-start.7 = (bf16[112,128]{1,0:T(8,128)(2,1)S(1)}, bf16[112,128]{1,0:T(8,128)(2,1)S(1)}, u32[]{:S(2)}, u32[]{:S(2)}) collective-permute-start(bf16[112,128]{1,0:T(8,128)(2,1)S(1)} %get-tuple-element.94), channel_id=1, source_target_pairs={{0,17},{1,16},{2,19},{3,18},{4,21},{5,20},{6,23},{7,22},{8,25},{9,... | collective-permute-start | bytes 86024 | tf_op jit(solution)/shard_map/ppermute | solution.py:531
  27.0 4.8 %collective-permute-start.8 = (bf16[112,128]{1,0:T(8,128)(2,1)S(1)}, bf16[112,128]{1,0:T(8,128)(2,1)S(1)}, u32[]{:S(2)}, u32[]{:S(2)}) collective-permute-start(bf16[112,128]{1,0:T(8,128)(2,1)S(1)} %get-tuple-element.94), channel_id=1, source_target_pairs={{0,16},{1,17},{2,18},{3,19},{4,20},{5,21},{6,22},{7,23},{8,24},{9,... | collective-permute-start | bytes 86024 | tf_op jit(solution)/shard_map/ppermute | solution.py:531
  27.4 4.4 %collective-permute-start.9 = (bf16[112,128]{1,0:T(8,128)(2,1)S(1)}, bf16[112,128]{1,0:T(8,128)(2,1)S(1)}, u32[]{:S(2)}, u32[]{:S(2)}) collective-permute-start(bf16[112,128]{1,0:T(8,128)(2,1)S(1)} %get-tuple-element.95), channel_id=1, source_target_pairs={{0,1},{1,0},{2,3},{3,2},{4,5},{5,4},{6,7},{7,6},{8,9},{9,8},{10,11... | collective-permute-start | bytes 86024 | tf_op jit(solution)/shard_map/ppermute | solution.py:531

commit v6 on v5

--- a/solution.py
+++ b/solution.py
@@ -422,17 +422,15 @@
 
 
 def finish_kernel(
-    own_ref, a_ref, b_ref, c_ref, late_ref, features_in_hbm, weights_hbm, bias_hbm, features_hbm,
+    own_ref, a_ref, b_ref, c_ref, weights_hbm, bias_hbm,
     weights_ref, bias_ref, tap_scr, turn_scr, dilated_scr, sems, *, weight_scale, bias_scale,
 ):
     tile = lax.axis_index("tile")
-    late = pltpu.make_async_copy(late_ref, features_hbm.at[1], sems.at[0])
-    late.start()
     total = (own_ref[...] + a_ref[...].astype(F32)) + (b_ref[...].astype(F32) + c_ref[...].astype(F32))
     bias = total[(BLOCKS - 1) * 8 :, :] * bias_scale
     index = lax.broadcasted_iota(jnp.int32, bias.shape, 0)
     bias_ref[...] = jnp.sum(jnp.where(index == tile, bias, 0.0), axis=0, keepdims=True)[:, 0:CH]
-    bias_out = pltpu.make_async_copy(bias_ref, bias_hbm, sems.at[1])
+    bias_out = pltpu.make_async_copy(bias_ref, bias_hbm, sems.at[0])
     bias_out.start()
     total = total * weight_scale
     other = pltpu.roll(total, CH, 1)
@@ -451,7 +449,7 @@
     for block in range(8):
         weights_ref[:, block * 128 : (block + 1) * 128] = lines[block]
     strided_part, dilated_part = pl.ds(0, 16 * CH), pl.ds(16 * CH, DIL_TAPS * CH)
-    strided_out = pltpu.make_async_copy(weights_ref.at[:, strided_part], weights_hbm.at[:, strided_part], sems.at[2])
+    strided_out = pltpu.make_async_copy(weights_ref.at[:, strided_part], weights_hbm.at[:, strided_part], sems.at[1])
     strided_out.start()
     turn_scr[0:40, :] = total[64:104, :]
     turned = turn_scr[...].T
@@ -464,9 +462,9 @@
     for j in range(1, 5):
         result = jnp.where(tap // 2 == j, spread[8 * j : 8 * j + 8, :], result)
     weights_ref[:, 16 * CH :] = result
-    dilated_out = pltpu.make_async_copy(weights_ref.at[:, dilated_part], weights_hbm.at[:, dilated_part], sems.at[3])
+    dilated_out = pltpu.make_async_copy(weights_ref.at[:, dilated_part], weights_hbm.at[:, dilated_part], sems.at[2])
     dilated_out.start()
-    for copy in (late, bias_out, strided_out, dilated_out):
+    for copy in (bias_out, strided_out, dilated_out):
         copy.wait()
 
 
@@ -494,14 +492,14 @@
         out_ref[:, q * run : (q + 1) * run] = merged[q * CH : (q + 1) * CH, :]
 
 
-def feature_first_kernel(pre_b_ref, wf_ref, out_ref, shift_scr):
-    feature_patch(pre_b_ref, wf_ref, out_ref, shift_scr)
-
-
-def feature_second_kernel(pre_b_ref, wf_ref, first_ref, out_ref, features_hbm, shift_scr, sem):
-    copy = pltpu.make_async_copy(first_ref, features_hbm.at[0], sem)
+def feature_kernel(pre_b0_ref, pre_b1_ref, wf_ref, out_ref, shift_scr):
+    for p, pre_b_ref in enumerate((pre_b0_ref, pre_b1_ref)):
+        feature_patch(pre_b_ref, wf_ref, out_ref.at[p], shift_scr)
+
+
+def store_kernel(features_ref, out_hbm, sem):
+    copy = pltpu.make_async_copy(features_ref, out_hbm, sem)
     copy.start()
-    feature_patch(pre_b_ref, wf_ref, out_ref, shift_scr)
     copy.wait()
 
 
@@ -688,51 +686,50 @@
         select, out_shifts, last, first[0], act[1], phases[1], *first[2:],
         flops=10**9,
     )
-    feature_shape = ((channels, cells_in), BF16)
+    wide_scr = ((9 * channels, cells), BF16)
     if chunked:
         stage = ((2 * BLOCKS * 8, 128), BF16)
         own, by_y, by_z, by_zy = call(spread_kernel, [stage] * 4, "vvvv", [], place, bias, keep, got)
         by_zy, by_z, by_y = scene_xor(by_zy, 6), scene_xor(by_z, 4), scene_xor(by_y, 2)
-    (feature_first,) = call(
-        feature_first_kernel, [feature_shape], "vv", [shift_scr], pre_b[0], w_feature, flops=10**9
+    (feature_grads,) = call(
+        feature_kernel, [(features.shape, BF16)], "vvv", [wide_scr], *pre_b, w_feature, flops=10**9
     )
     chunk = (BLOCKS * 8, 128)
     if chunked:
-        feature_first, own = lax.optimization_barrier((feature_first, own))
+        feature_grads, own = lax.optimization_barrier((feature_grads, own))
         kept, stay, cross = call(
             join_kernel, [(chunk, F32), (chunk, BF16), (chunk, BF16)], "vvvv", [], own, by_zy, by_z, by_y
         )
         by_zx, by_z, by_x = device_xor(cross, 8, 1), device_xor(cross, 8, 0), device_xor(stay, 0, 1)
-    feature_last, feature_grads = call(
-        feature_second_kernel,
-        [feature_shape, (features.shape, BF16)],
-        "vvv",
-        [shift_scr, pltpu.SemaphoreType.DMA],
-        pre_b[1], w_feature, feature_first,
+    (feature_grads,) = call(
+        store_kernel,
+        [(features.shape, BF16)],
+        "v",
+        [pltpu.SemaphoreType.DMA],
+        feature_grads,
         flops=10**9,
-        out_spaces="vh",
+        out_spaces="h",
     )
     if not chunked:
-        feature_grads = feature_grads.at[1].set(feature_last)
         grad_weights, grad_bias = reduce_anywhere(
             join_halves(give, keep), bias[0], tile_owner, bias_rows, weight_scale, bias_scale
         )
         return (feature_grads[None], grad_weights, grad_bias)
-    grad_weights, grad_bias, feature_grads = call(
+    feature_grads, kept = lax.optimization_barrier((feature_grads, kept))
+    grad_weights, grad_bias = call(
         functools.partial(finish_kernel, weight_scale=weight_scale, bias_scale=bias_scale),
-        [((8, 25 * channels), F32), ((1, channels), F32), (features.shape, BF16)],
-        "vvvvva",
+        [((8, 25 * channels), F32), ((1, channels), F32)],
+        "vvvv",
         [
             ((8, 25 * channels), F32),
             ((1, channels), F32),
             ((128, 128), F32),
             ((128, 128), F32),
             ((9 * channels, 128), F32),
-            pltpu.SemaphoreType.DMA((4,)),
+            pltpu.SemaphoreType.DMA((3,)),
         ],
-        kept, by_zx, by_z, by_x, feature_last, feature_grads,
-        out_spaces="hhh",
-        aliases={5: 2},
+        kept, by_zx, by_z, by_x,
+        out_spaces="hh",
     )
     return (feature_grads[None], grad_weights, grad_bias)
 

time: 33.2 us -> 33.1 us (level)
  waiting for transfers between devices: 9.28 us -> 8.6 us
  Pallas kernels: 11.7 us -> 12.2 us
    ppermute x5, waiting for transfers between devices: 3.31 us -> 2.59 us  [scene_xor(): lax.ppermute(x, 'scene', [(i, i ^ distance) for i in range(lax.axis_size(...]
    pallas_call x11, Pallas kernels: 11.7 us -> 12.2 us  [call(): pl.pallas_call(kernel, out_shape=[jax.ShapeDtypeStruct(shape, kind) for s...]
  transfers between devices with their start and end apart: 10 -> 10, of which waited for: 8 -> 7; matrix products, arithmetic and copies ran while one was open for 0% -> 0% of each run, Pallas kernels for 20% -> 22%
where the time goes in v6:
time: 33.1 us; the launch traced here: 33 us
  Pallas kernels  12.2 us (37%)
  starting transfers between devices  11.4 us (34%)
  waiting for transfers between devices  8.6 us (26%)
  between operations  0.7 us (2%)
    pallas_call x11, Pallas kernels, call(): pl.pallas_call(kernel, out_shape=[jax.ShapeDtypeStruct(shape, kind) for s...  12.2 us
    ppermute x5, starting transfers between devices, device_pairs(): return lax.ppermute(x, ('scene', 'tile'), flat)  6.96 us
    ppermute x5, waiting for transfers between devices, device_pairs(): return lax.ppermute(x, ('scene', 'tile'), flat)  6.02 us
    ppermute x5, starting transfers between devices, scene_xor(): lax.ppermute(x, 'scene', [(i, i ^ distance) for i in range(lax.axis_size(...  4.47 us
    ppermute x5, waiting for transfers between devices, scene_xor(): lax.ppermute(x, 'scene', [(i, i ^ distance) for i in range(lax.axis_size(...  2.59 us
  transfers between devices with their start and end apart: 10, of which 7 were waited for; matrix products, arithmetic and copies ran while one was open for 0% of the time, Pallas kernels for 22%

profile of v6, /device:TPU:0, one launch (start us, length us, event | category | flops | bytes accessed | tf_op | source)
XLA Modules:
  0.0 33.0 jit_solution(12969172445659036552)
XLA Ops:
  0.6 0.0 copy-start
  0.6 2.9 %shard_map.103 = (bf16[256,1024]{1,0:T(8,128)(2,1)S(1)}, f32[64,1024]{1,0:T(8,128)S(1)}, bf16[64,1024]{1,0:T(8,128)(2,1)S(1)}, bf16[528,128]{1,0:T(8,128)(2,1)S(...) custom-call(s32[16]{0:T(128)} %owner_hbm.3, ...), custom_call_target="tpu_custom_call" | custom-call | flops 1000000000 | bytes 1048576 | tf_op jit(solution)/shard_map/pallas_call | solution.py:514
  3.5 2.5 %collective-permute-start.1 = (bf16[528,128]{1,0:T(8,128)(2,1)S(1)}, bf16[528,128]{1,0:T(8,128)(2,1)S(1)}, u32[]{:S(2)}, u32[]{:S(2)}) collective-permute-start(bf16[528,128]{1,0:T(8,128)(2,1)S(1)} %get-tuple-element.57.sent_ref.refs_6_), channel_id=1, source_target_pairs={{0,3},{1,2},{2,1},{3,0},{4,7},{5,6},{6,5},{7,4},{8,11},{9,10},{10,... | collective-permute-start | bytes 405512 | tf_op jit(solution)/shard_map/ppermute | solution.py:529
  6.0 0.0 copy-done
  6.0 1.4 %shard_map.104 = (bf16[256,1024]{1,0:T(8,128)(2,1)S(1)}, f32[64,1024]{1,0:T(8,128)S(1)}, bf16[64,1024]{1,0:T(8,128)(2,1)S(1)}, bf16[528,128]{1,0:T(8,128)(2,1)S(1)}, bf16[2,528,128]{2,1,0:T(8,128)(2,1)S(1)}) custom-call(bf16[2,64,4096]{2,1,0:T(8,128)(2,1)S(1)} %bitcast.5, bf16[2,1024]{1,0:T(2,128)(2,1)S(1)} %get-tuple-element.53.cot_ref, ...), custom_call_target="tpu_custom_call" | custom-call | flops 10000000000 | bytes 1048576 | tf_op jit(solution)/shard_map/pallas_call | solution.py:514
  7.4 0.7 %collective-permute-start.2 = (bf16[2,528,128]{2,1,0:T(8,128)(2,1)S(1)}, bf16[2,528,128]{2,1,0:T(8,128)(2,1)S(1)}, u32[]{:S(2)}, u32[]{:S(2)}) collective-permute-start(bf16[2,528,128]{2,1,0:T(8,128)(2,1)S(1)} %get-tuple-element.65), channel_id=1, source_target_pairs={{0,2},{2,0},{4,6},{6,4},{8,10},{10,8},{12,14},{14,12},{16,18},{18,... | collective-permute-start | bytes 811016 | tf_op jit(solution)/shard_map/ppermute | solution.py:533
  8.1 0.1 collective-permute-start
  8.2 0.0 copy-done.1
  8.2 1.2 %shard_map.105 = (f32[64,1024]{1,0:T(8,128)S(1)}, f32[64,1024]{1,0:T(8,128)S(1)}, bf16[64,1024]{1,0:T(8,128)(2,1)S(1)}, bf16[64,1024]{1,0:T(8,128)(2,1)S(1)}, bf...) custom-call(s32[4,8]{1,0:T(4,128)} %bitcast.7, ...), custom_call_target="tpu_custom_call" | custom-call | flops 10000000000 | bytes 1048576 | tf_op jit(solution)/shard_map/pallas_call | solution.py:514
  9.4 0.5 %collective-permute-done.1.far0_ref = bf16[528,128]{1,0:T(8,128)(2,1)S(1)} collective-permute-done((bf16[528,128]{1,0:T(8,128)(2,1)S(1)}, bf16[528,128]{1,0:T(8,128)(2,1)S(1)}, u32[]{:S(2)}, u32[]{:S(2)}) %collective-permute-start.1) | collective-permute-done | bytes 135200 | tf_op jit(solution)/shard_map/ppermute | solution.py:529
  10.0 0.0 collective-permute-done.2.near_ref
  10.0 1.3 %shard_map.106 = (bf16[528,128]{1,0:T(8,128)(2,1)S(1)}, bf16[64,1024]{1,0:T(8,128)(2,1)S(1)}, f32[64,128]{1,0:T(8,128)S(1)}, f32[576,128]{1,0:T(8,128)S(1)}, f32[576,256]{1,0:T(8,128)S(1)}) custom-call(bf16[528,128]{1,0:T(8,128)(2,1)S(1)} %collective-permute-done.1.far0_ref, bf16[2,528,128]{2,1,0:T(8,128)(2,1)S(1)} %collective-permute-done.2.near_ref, ...), custom_call_target="tpu_custom_call" | custom-call | flops 1000000000 | bytes 1048576 | tf_op jit(solution)/shard_map/pallas_call | solution.py:514
  11.2 2.5 %collective-permute-done.far1_ref = bf16[528,128]{1,0:T(8,128)(2,1)S(1)} collective-permute-done((bf16[528,128]{1,0:T(8,128)(2,1)S(1)}, bf16[528,128]{1,0:T(8,128)(2,1)S(1)}, u32[]{:S(2)}, u32[]{:S(2)}) %collective-permute-start) | collective-permute-done | bytes 135200 | tf_op jit(solution)/shard_map/ppermute | solution.py:529
  13.7 0.9 %shard_map.107 = (bf16[64,1024]{1,0:T(8,128)(2,1)S(1)}, f32[8,128]{1,0:T(8,128)S(1)}, bf16[4,112,128]{2,1,0:T(8,128)(2,1)S(1)}, bf16[576,1024]{1,0:T(8,128)(2,1)S(1)}) custom-call(bf16[528,128]{1,0:T(8,128)(2,1)S(1)} %collective-permute-done.far1_ref, bf16[528,128]{1,0:T(8,128)(2,1)S(1)} %get-tuple-element.71.pick_ref, ...), custom_call_target="tpu_custom_call" | custom-call | flops 1000000000 | bytes 1048576 | tf_op jit(solution)/shard_map/pallas_call | solution.py:514
  14.7 0.2 collective-permute-start.3
  14.9 0.5 %shard_map.108 = (bf16[4,112,128]{2,1,0:T(8,128)(2,1)S(1)}, bf16[64,1024]{1,0:T(8,128)(2,1)S(1)}, bf16[64,1024]{1,0:T(8,128)(2,1)S(1)}) custom-call(f32[16,128]{1,0:T(8,128)S(1)} %get-tuple-element.64.select_ref, bf16[576,1024]{1,0:T(8,128)(2,1)S(1)} %get-tuple-element.78.out_shifts_ref, bf16[64,1024]{1,0:T(8,128)(2,1)S(1)} %get-tuple-element.79.pre_b_ref, ...), custom_call_target="tpu_custom_call" | custom-call | flops 1000000000 | bytes 1048576 | tf_op jit(solution)/shard_map/pallas_call | solution.py:514
  15.4 0.7 %collective-permute-done.3.got_ref = bf16[4,112,128]{2,1,0:T(8,128)(2,1)S(1)} collective-permute-done((bf16[4,112,128]{2,1,0:T(8,128)(2,1)S(1)}, bf16[4,112,128]{2,1,0:T(8,128)(2,1)S(1)}, u32[]{:S(2)}, u32[]{:S(2)}) %collective-permute-start.3) | collective-permute-done | bytes 114720 | tf_op jit(solution)/shard_map/ppermute | solution.py:533
  16.1 2.6 %collective-permute-start.4 = (bf16[224,128]{1,0:T(8,128)(2,1)S(1)}, bf16[224,128]{1,0:T(8,128)(2,1)S(1)}, u32[]{:S(2)}, u32[]{:S(2)}) collective-permute-start(bf16[224,128]{1,0:T(8,128)(2,1)S(1)} %get-tuple-element.91), channel_id=1, source_target_pairs={{0,12},{2,14},{4,8},{6,10},{8,4},{10,6},{12,0},{14,2},{16,28},{18,... | collective-permute-start | bytes 172040 | tf_op jit(solution)/shard_map/ppermute | solution.py:533
  18.7 0.4 %collective-permute-start.5 = (bf16[224,128]{1,0:T(8,128)(2,1)S(1)}, bf16[224,128]{1,0:T(8,128)(2,1)S(1)}, u32[]{:S(2)}, u32[]{:S(2)}) collective-permute-start(bf16[224,128]{1,0:T(8,128)(2,1)S(1)} %get-tuple-element.92), channel_id=1, source_target_pairs={{0,8},{2,10},{4,12},{6,14},{8,0},{10,2},{12,4},{14,6},{16,24},{18,... | collective-permute-start | bytes 172040 | tf_op jit(solution)/shard_map/ppermute | solution.py:533
  19.2 0.5 %collective-permute-start.6 = (bf16[224,128]{1,0:T(8,128)(2,1)S(1)}, bf16[224,128]{1,0:T(8,128)(2,1)S(1)}, u32[]{:S(2)}, u32[]{:S(2)}) collective-permute-start(bf16[224,128]{1,0:T(8,128)(2,1)S(1)} %get-tuple-element.93), channel_id=1, source_target_pairs={{0,4},{2,6},{4,0},{6,2},{8,12},{10,14},{12,8},{14,10},{16,20},{18,... | collective-permute-start | bytes 172040 | tf_op jit(solution)/shard_map/ppermute | solution.py:533
  19.7 1.8 %shard_map.109.features_ref = bf16[2,64,4096]{2,1,0:T(8,128)(2,1)S(1)} custom-call(bf16[64,1024]{1,0:T(8,128)(2,1)S(1)} %get-tuple-element.81.pre_b0_ref, bf16[64,1024]{1,0:T(8,128)(2,1)S(1)} %get-tuple-element.82.pre_b1_ref, bf16[256,576]{1,0:T(8,128)(2,1)S(1)} %get-tuple-element.83.wf_ref), custom_call_target="tpu_custom_call" | custom-call | flops 1000000000 | bytes 1048576 | tf_op jit(solution)/shard_map/pallas_call | solution.py:514
  21.4 0.0 collective-permute-done.4.a_ref
  21.5 1.4 %collective-permute-done.5.b_ref = bf16[224,128]{1,0:T(8,128)(2,1)S(1)} collective-permute-done((bf16[224,128]{1,0:T(8,128)(2,1)S(1)}, bf16[224,128]{1,0:T(8,128)(2,1)S(1)}, u32[]{:S(2)}, u32[]{:S(2)}) %collective-permute-start.5) | collective-permute-done | bytes 57376 | tf_op jit(solution)/shard_map/ppermute | solution.py:533
  22.9 0.4 %collective-permute-done.6.c_ref = bf16[224,128]{1,0:T(8,128)(2,1)S(1)} collective-permute-done((bf16[224,128]{1,0:T(8,128)(2,1)S(1)}, bf16[224,128]{1,0:T(8,128)(2,1)S(1)}, u32[]{:S(2)}, u32[]{:S(2)}) %collective-permute-start.6) | collective-permute-done | bytes 57376 | tf_op jit(solution)/shard_map/ppermute | solution.py:533
  23.4 3.6 %collective-permute-start.7 = (bf16[112,128]{1,0:T(8,128)(2,1)S(1)}, bf16[112,128]{1,0:T(8,128)(2,1)S(1)}, u32[]{:S(2)}, u32[]{:S(2)}) collective-permute-start(bf16[112,128]{1,0:T(8,128)(2,1)S(1)} %get-tuple-element.97), channel_id=1, source_target_pairs={{0,17},{1,16},{2,19},{3,18},{4,21},{5,20},{6,23},{7,22},{8,25},{9,... | collective-permute-start | bytes 86024 | tf_op jit(solution)/shard_map/ppermute | solution.py:529
  27.0 0.4 %collective-permute-start.8 = (bf16[112,128]{1,0:T(8,128)(2,1)S(1)}, bf16[112,128]{1,0:T(8,128)(2,1)S(1)}, u32[]{:S(2)}, u32[]{:S(2)}) collective-permute-start(bf16[112,128]{1,0:T(8,128)(2,1)S(1)} %get-tuple-element.97), channel_id=1, source_target_pairs={{0,16},{1,17},{2,18},{3,19},{4,20},{5,21},{6,22},{7,23},{8,24},{9,... | collective-permute-start | bytes 86024 | tf_op jit(solution)/shard_map/ppermute | solution.py:529
  27.4 0.5 %collective-permute-start.9 = (bf16[112,128]{1,0:T(8,128)(2,1)S(1)}, bf16[112,128]{1,0:T(8,128)(2,1)S(1)}, u32[]{:S(2)}, u32[]{:S(2)}) collective-permute-start(bf16[112,128]{1,0:T(8,128)(2,1)S(1)} %get-tuple-element.98), channel_id=1, source_target_pairs={{0,1},{1,0},{2,3},{3,2},{4,5},{5,4},{6,7},{7,6},{8,9},{9,8},{10,11... | collective-permute-start | bytes 86024 | tf_op jit(solution)/shard_map/ppermute | solution.py:529
  27.8 1.0 %shard_map.111 = bf16[2,64,4096]{2,1,0:T(8,128)(2,1)} custom-call(bf16[2,64,4096]{2,1,0:T(8,128)(2,1)S(1)} %shard_map.109.features_ref), custom_call_target="tpu_custom_call" | custom-call | flops 1000000000 | bytes 1048576 | tf_op jit(solution)/shard_map/pallas_call | solution.py:514
  28.8 0.4 %collective-permute-done.7.a_ref = bf16[112,128]{1,0:T(8,128)(2,1)S(1)} collective-permute-done((bf16[112,128]{1,0:T(8,128)(2,1)S(1)}, bf16[112,128]{1,0:T(8,128)(2,1)S(1)}, u32[]{:S(2)}, u32[]{:S(2)}) %collective-permute-start.7) | collective-permute-done | bytes 28704 | tf_op jit(solution)/shard_map/ppermute | solution.py:529
  29.3 2.5 %collective-permute-done.8.b_ref = bf16[112,128]{1,0:T(8,128)(2,1)S(1)} collective-permute-done((bf16[112,128]{1,0:T(8,128)(2,1)S(1)}, bf16[112,128]{1,0:T(8,128)(2,1)S(1)}, u32[]{:S(2)}, u32[]{:S(2)}) %collective-permute-start.8) | collective-permute-done | bytes 28704 | tf_op jit(solution)/shard_map/ppermute | solution.py:529
  31.8 0.0 collective-permute-done.9.c_ref
  31.8 1.2 %shard_map.113 = (f32[8,1600]{1,0:T(8,128)}, f32[1,64]{1,0:T(1,128)}) custom-call(f32[112,128]{1,0:T(8,128)S(1)} %get-tuple-element.96.own_ref, bf16[112,128]{1,0:T(8,128)(2,1)S(1)} %collective-permute-done.7.a_ref, bf16[112,128]{1,0:T(8,128)(2,1)S(1)} %collective-permute-done.8.b_ref, bf16[112,128]{1,0:T(8,128)(2,1)S(1)} %collective-permute-done.9.c_ref), custom_call_target="tpu_custom_call" | custom-call | bytes 1048576 | tf_op jit(solution)/shard_map/pallas_call | solution.py:514
  (5 shorter events, 0.1 us)
Async XLA Ops:
  0.6 5.4 %copy-start = (bf16[1,2,64,4096]{3,2,1,0:T(8,128)(2,1)S(1)}, bf16[1,2,64,4096]{3,2,1,0:T(8,128)(2,1)}, u32[]{:S(2)}) copy-start(bf16[1,2,64,4096]{3,2,1,0:T(8,128)(2,1)} %param.8) | copy-start | bytes 3145732
  3.5 6.4 %collective-permute-start.1 = (bf16[528,128]{1,0:T(8,128)(2,1)S(1)}, bf16[528,128]{1,0:T(8,128)(2,1)S(1)}, u32[]{:S(2)}, u32[]{:S(2)}) collective-permute-start(bf16[528,128]{1,0:T(8,128)(2,1)S(1)} %get-tuple-element.57.sent_ref.refs_6_), channel_id=1, source_target_pairs={{0,3},{1,2},{2,1},{3,0},{4,7},{5,6},{6,5},{7,4},{8,11},{9,10},{10,... | collective-permute-start | bytes 405512 | tf_op jit(solution)/shard_map/ppermute | solution.py:529
  6.0 2.2 %copy-start.1 = (bf16[2,64,1024]{2,1,0:T(8,128)(2,1)S(1)}, bf16[2,64,1024]{2,1,0:T(8,128)(2,1)}, u32[]{:S(2)}) copy-start(bf16[2,64,1024]{2,1,0:T(8,128)(2,1)} %ws_ref.1) | copy-start | bytes 786436
  6.0 2.2 %copy-start.2 = (bf16[2,64,576]{2,1,0:T(8,128)(2,1)S(1)}, bf16[2,64,576]{2,1,0:T(8,128)(2,1)}, u32[]{:S(2)}) copy-start(bf16[2,64,576]{2,1,0:T(8,128)(2,1)} %wd_ref.1) | copy-start | bytes 442372
  7.4 2.6 %collective-permute-start.2 = (bf16[2,528,128]{2,1,0:T(8,128)(2,1)S(1)}, bf16[2,528,128]{2,1,0:T(8,128)(2,1)S(1)}, u32[]{:S(2)}, u32[]{:S(2)}) collective-permute-start(bf16[2,528,128]{2,1,0:T(8,128)(2,1)S(1)} %get-tuple-element.65), channel_id=1, source_target_pairs={{0,2},{2,0},{4,6},{6,4},{8,10},{10,8},{12,14},{14,12},{16,18},{18,... | collective-permute-start | bytes 811016 | tf_op jit(solution)/shard_map/ppermute | solution.py:533
  8.1 5.6 %collective-permute-start = (bf16[528,128]{1,0:T(8,128)(2,1)S(1)}, bf16[528,128]{1,0:T(8,128)(2,1)S(1)}, u32[]{:S(2)}, u32[]{:S(2)}) collective-permute-start(bf16[528,128]{1,0:T(8,128)(2,1)S(1)} %get-tuple-element.63.refs_7_), channel_id=1, source_target_pairs={{0,3},{1,2},{2,1},{3,0},{4,7},{5,6},{6,5},{7,4},{8,11},{9,10},{10,... | collective-permute-start | bytes 405512 | tf_op jit(solution)/shard_map/ppermute | solution.py:529
  14.7 1.4 %collective-permute-start.3 = (bf16[4,112,128]{2,1,0:T(8,128)(2,1)S(1)}, bf16[4,112,128]{2,1,0:T(8,128)(2,1)S(1)}, u32[]{:S(2)}, u32[]{:S(2)}) collective-permute-start(bf16[4,112,128]{2,1,0:T(8,128)(2,1)S(1)} %get-tuple-element.87), channel_id=1, source_target_pairs={{0,2},{2,0},{4,6},{6,4},{8,10},{10,8},{12,14},{14,12},{16,18},{18,... | collective-permute-start | bytes 344072 | tf_op jit(solution)/shard_map/ppermute | solution.py:533
  16.1 5.4 %collective-permute-start.4 = (bf16[224,128]{1,0:T(8,128)(2,1)S(1)}, bf16[224,128]{1,0:T(8,128)(2,1)S(1)}, u32[]{:S(2)}, u32[]{:S(2)}) collective-permute-start(bf16[224,128]{1,0:T(8,128)(2,1)S(1)} %get-tuple-element.91), channel_id=1, source_target_pairs={{0,12},{2,14},{4,8},{6,10},{8,4},{10,6},{12,0},{14,2},{16,28},{18,... | collective-permute-start | bytes 172040 | tf_op jit(solution)/shard_map/ppermute | solution.py:533
  18.7 4.2 %collective-permute-start.5 = (bf16[224,128]{1,0:T(8,128)(2,1)S(1)}, bf16[224,128]{1,0:T(8,128)(2,1)S(1)}, u32[]{:S(2)}, u32[]{:S(2)}) collective-permute-start(bf16[224,128]{1,0:T(8,128)(2,1)S(1)} %get-tuple-element.92), channel_id=1, source_target_pairs={{0,8},{2,10},{4,12},{6,14},{8,0},{10,2},{12,4},{14,6},{16,24},{18,... | collective-permute-start | bytes 172040 | tf_op jit(solution)/shard_map/ppermute | solution.py:533
  19.2 4.2 %collective-permute-start.6 = (bf16[224,128]{1,0:T(8,128)(2,1)S(1)}, bf16[224,128]{1,0:T(8,128)(2,1)S(1)}, u32[]{:S(2)}, u32[]{:S(2)}) collective-permute-start(bf16[224,128]{1,0:T(8,128)(2,1)S(1)} %get-tuple-element.93), channel_id=1, source_target_pairs={{0,4},{2,6},{4,0},{6,2},{8,12},{10,14},{12,8},{14,10},{16,20},{18,... | collective-permute-start | bytes 172040 | tf_op jit(solution)/shard_map/ppermute | solution.py:533
  23.4 5.9 %collective-permute-start.7 = (bf16[112,128]{1,0:T(8,128)(2,1)S(1)}, bf16[112,128]{1,0:T(8,128)(2,1)S(1)}, u32[]{:S(2)}, u32[]{:S(2)}) collective-permute-start(bf16[112,128]{1,0:T(8,128)(2,1)S(1)} %get-tuple-element.97), channel_id=1, source_target_pairs={{0,17},{1,16},{2,19},{3,18},{4,21},{5,20},{6,23},{7,22},{8,25},{9,... | collective-permute-start | bytes 86024 | tf_op jit(solution)/shard_map/ppermute | solution.py:529
  27.0 4.8 %collective-permute-start.8 = (bf16[112,128]{1,0:T(8,128)(2,1)S(1)}, bf16[112,128]{1,0:T(8,128)(2,1)S(1)}, u32[]{:S(2)}, u32[]{:S(2)}) collective-permute-start(bf16[112,128]{1,0:T(8,128)(2,1)S(1)} %get-tuple-element.97), channel_id=1, source_target_pairs={{0,16},{1,17},{2,18},{3,19},{4,20},{5,21},{6,22},{7,23},{8,24},{9,... | collective-permute-start | bytes 86024 | tf_op jit(solution)/shard_map/ppermute | solution.py:529
  27.4 4.4 %collective-permute-start.9 = (bf16[112,128]{1,0:T(8,128)(2,1)S(1)}, bf16[112,128]{1,0:T(8,128)(2,1)S(1)}, u32[]{:S(2)}, u32[]{:S(2)}) collective-permute-start(bf16[112,128]{1,0:T(8,128)(2,1)S(1)} %get-tuple-element.98), channel_id=1, source_target_pairs={{0,1},{1,0},{2,3},{3,2},{4,5},{5,4},{6,7},{7,6},{8,9},{9,8},{10,11... | collective-permute-start | bytes 86024 | tf_op jit(solution)/shard_map/ppermute | solution.py:529

commit v7 on v6

--- a/solution.py
+++ b/solution.py
@@ -438,7 +438,7 @@
         for half, source in enumerate((total, other)):
             tap = block // 2 * 4 + ((1, 2), (3, 0))[block % 2][half]
             tap_scr[pl.ds(tap, 8, stride=16), :] = source[block * 8 : block * 8 + 8, :]
-    lines = tap_scr[...].T[0:CH, :].reshape(8, 8, 128)
+    lines = tap_scr[0:128, :].T[0:CH, :].reshape(8, 8, 128)
     sub = lax.broadcasted_iota(jnp.int32, lines.shape, 1)
     chunk = lax.broadcasted_iota(jnp.int32, lines.shape, 2) // 16
     for step in (1, 2, 4):
@@ -456,7 +456,7 @@
     for tap in range(DIL_TAPS):
         half = tap % 2
         dilated_scr[pl.ds(tap, CH, stride=DIL_TAPS), :] = turned[half * CH : (half + 1) * CH, :]
-    spread = dilated_scr[...].T
+    spread = dilated_scr[0 : DIL_TAPS * CH, :].T
     tap = lax.broadcasted_iota(jnp.int32, (8, DIL_TAPS * CH), 1) % DIL_TAPS
     result = spread[0:8, :]
     for j in range(1, 5):
@@ -594,7 +594,7 @@
     grid = (channels, cells)
     payload = (cells * channels // 128 + 16, 128)
     chunked = scenes == 16 and tiles == 2 and patches == 2 and bias_rows == 1
-    wscr = ((16 * channels, 2 * channels), F32)
+    wscr = ((16 * channels + 16, 2 * channels), F32)
     im_scr = ((8 * channels, cells), BF16)
     patch_outs = [((4 * channels, cells), BF16), (grid, F32), (grid, BF16), (payload, BF16)]
     first_outs = patch_outs + [
@@ -723,9 +723,9 @@
         [
             ((8, 25 * channels), F32),
             ((1, channels), F32),
+            ((144, 128), F32),
             ((128, 128), F32),
-            ((128, 128), F32),
-            ((9 * channels, 128), F32),
+            ((9 * channels + 16, 128), F32),
             pltpu.SemaphoreType.DMA((3,)),
         ],
         kept, by_zx, by_z, by_x,

time: 33.1 us -> 33.2 us (level)
  no operation moved by 1% of the time
where the time goes in v7:
time: 33.2 us; the launch traced here: 33 us
  Pallas kernels  12.2 us (37%)
  starting transfers between devices  11.4 us (34%)
  waiting for transfers between devices  8.61 us (26%)
  between operations  0.7 us (2%)
    pallas_call x11, Pallas kernels, call(): pl.pallas_call(kernel, out_shape=[jax.ShapeDtypeStruct(shape, kind) for s...  12.2 us
    ppermute x5, starting transfers between devices, device_pairs(): return lax.ppermute(x, ('scene', 'tile'), flat)  6.95 us
    ppermute x5, waiting for transfers between devices, device_pairs(): return lax.ppermute(x, ('scene', 'tile'), flat)  6.04 us
    ppermute x5, starting transfers between devices, scene_xor(): lax.ppermute(x, 'scene', [(i, i ^ distance) for i in range(lax.axis_size(...  4.47 us
    ppermute x5, waiting for transfers between devices, scene_xor(): lax.ppermute(x, 'scene', [(i, i ^ distance) for i in range(lax.axis_size(...  2.58 us
  transfers between devices with their start and end apart: 10, of which 7 were waited for; matrix products, arithmetic and copies ran while one was open for 0% of the time, Pallas kernels for 22%

profile of v7, /device:TPU:0, one launch (start us, length us, event | category | flops | bytes accessed | tf_op | source)
XLA Modules:
  0.0 33.0 jit_solution(1550425673652168837)
XLA Ops:
  0.6 0.0 copy-start
  0.6 2.9 %shard_map.103 = (bf16[256,1024]{1,0:T(8,128)(2,1)S(1)}, f32[64,1024]{1,0:T(8,128)S(1)}, bf16[64,1024]{1,0:T(8,128)(2,1)S(1)}, bf16[528,128]{1,0:T(8,128)(2,1)S(...) custom-call(s32[16]{0:T(128)} %owner_hbm.3, ...), custom_call_target="tpu_custom_call" | custom-call | flops 1000000000 | bytes 1048576 | tf_op jit(solution)/shard_map/pallas_call | solution.py:514
  3.5 2.4 %collective-permute-start.1 = (bf16[528,128]{1,0:T(8,128)(2,1)S(1)}, bf16[528,128]{1,0:T(8,128)(2,1)S(1)}, u32[]{:S(2)}, u32[]{:S(2)}) collective-permute-start(bf16[528,128]{1,0:T(8,128)(2,1)S(1)} %get-tuple-element.57.sent_ref.refs_6_), channel_id=1, source_target_pairs={{0,3},{1,2},{2,1},{3,0},{4,7},{5,6},{6,5},{7,4},{8,11},{9,10},{10,... | collective-permute-start | bytes 405512 | tf_op jit(solution)/shard_map/ppermute | solution.py:529
  6.0 0.0 copy-done
  6.0 1.4 %shard_map.104 = (bf16[256,1024]{1,0:T(8,128)(2,1)S(1)}, f32[64,1024]{1,0:T(8,128)S(1)}, bf16[64,1024]{1,0:T(8,128)(2,1)S(1)}, bf16[528,128]{1,0:T(8,128)(2,1)S(1)}, bf16[2,528,128]{2,1,0:T(8,128)(2,1)S(1)}) custom-call(bf16[2,64,4096]{2,1,0:T(8,128)(2,1)S(1)} %bitcast.5, bf16[2,1024]{1,0:T(2,128)(2,1)S(1)} %get-tuple-element.53.cot_ref, ...), custom_call_target="tpu_custom_call" | custom-call | flops 10000000000 | bytes 1048576 | tf_op jit(solution)/shard_map/pallas_call | solution.py:514
  7.4 0.7 %collective-permute-start.2 = (bf16[2,528,128]{2,1,0:T(8,128)(2,1)S(1)}, bf16[2,528,128]{2,1,0:T(8,128)(2,1)S(1)}, u32[]{:S(2)}, u32[]{:S(2)}) collective-permute-start(bf16[2,528,128]{2,1,0:T(8,128)(2,1)S(1)} %get-tuple-element.65), channel_id=1, source_target_pairs={{0,2},{2,0},{4,6},{6,4},{8,10},{10,8},{12,14},{14,12},{16,18},{18,... | collective-permute-start | bytes 811016 | tf_op jit(solution)/shard_map/ppermute | solution.py:533
  8.1 0.1 collective-permute-start
  8.2 0.0 copy-done.1
  8.2 1.2 %shard_map.105 = (f32[64,1024]{1,0:T(8,128)S(1)}, f32[64,1024]{1,0:T(8,128)S(1)}, bf16[64,1024]{1,0:T(8,128)(2,1)S(1)}, bf16[64,1024]{1,0:T(8,128)(2,1)S(1)}, bf...) custom-call(s32[4,8]{1,0:T(4,128)} %bitcast.7, ...), custom_call_target="tpu_custom_call" | custom-call | flops 10000000000 | bytes 1048576 | tf_op jit(solution)/shard_map/pallas_call | solution.py:514
  9.4 0.5 %collective-permute-done.1.far0_ref = bf16[528,128]{1,0:T(8,128)(2,1)S(1)} collective-permute-done((bf16[528,128]{1,0:T(8,128)(2,1)S(1)}, bf16[528,128]{1,0:T(8,128)(2,1)S(1)}, u32[]{:S(2)}, u32[]{:S(2)}) %collective-permute-start.1) | collective-permute-done | bytes 135200 | tf_op jit(solution)/shard_map/ppermute | solution.py:529
  10.0 0.0 collective-permute-done.2.near_ref
  10.0 1.3 %shard_map.106 = (bf16[528,128]{1,0:T(8,128)(2,1)S(1)}, bf16[64,1024]{1,0:T(8,128)(2,1)S(1)}, f32[64,128]{1,0:T(8,128)S(1)}, f32[576,128]{1,0:T(8,128)S(1)}, f32[576,256]{1,0:T(8,128)S(1)}) custom-call(bf16[528,128]{1,0:T(8,128)(2,1)S(1)} %collective-permute-done.1.far0_ref, bf16[2,528,128]{2,1,0:T(8,128)(2,1)S(1)} %collective-permute-done.2.near_ref, ...), custom_call_target="tpu_custom_call" | custom-call | flops 1000000000 | bytes 1048576 | tf_op jit(solution)/shard_map/pallas_call | solution.py:514
  11.2 2.5 %collective-permute-done.far1_ref = bf16[528,128]{1,0:T(8,128)(2,1)S(1)} collective-permute-done((bf16[528,128]{1,0:T(8,128)(2,1)S(1)}, bf16[528,128]{1,0:T(8,128)(2,1)S(1)}, u32[]{:S(2)}, u32[]{:S(2)}) %collective-permute-start) | collective-permute-done | bytes 135200 | tf_op jit(solution)/shard_map/ppermute | solution.py:529
  13.7 0.9 %shard_map.107 = (bf16[64,1024]{1,0:T(8,128)(2,1)S(1)}, f32[8,128]{1,0:T(8,128)S(1)}, bf16[4,112,128]{2,1,0:T(8,128)(2,1)S(1)}, bf16[576,1024]{1,0:T(8,128)(2,1)S(1)}) custom-call(bf16[528,128]{1,0:T(8,128)(2,1)S(1)} %collective-permute-done.far1_ref, bf16[528,128]{1,0:T(8,128)(2,1)S(1)} %get-tuple-element.71.pick_ref, ...), custom_call_target="tpu_custom_call" | custom-call | flops 1000000000 | bytes 1048576 | tf_op jit(solution)/shard_map/pallas_call | solution.py:514
  14.7 0.2 collective-permute-start.3
  14.9 0.5 %shard_map.108 = (bf16[4,112,128]{2,1,0:T(8,128)(2,1)S(1)}, bf16[64,1024]{1,0:T(8,128)(2,1)S(1)}, bf16[64,1024]{1,0:T(8,128)(2,1)S(1)}) custom-call(f32[16,128]{1,0:T(8,128)S(1)} %get-tuple-element.64.select_ref, bf16[576,1024]{1,0:T(8,128)(2,1)S(1)} %get-tuple-element.78.out_shifts_ref, bf16[64,1024]{1,0:T(8,128)(2,1)S(1)} %get-tuple-element.79.pre_b_ref, ...), custom_call_target="tpu_custom_call" | custom-call | flops 1000000000 | bytes 1048576 | tf_op jit(solution)/shard_map/pallas_call | solution.py:514
  15.4 0.7 %collective-permute-done.3.got_ref = bf16[4,112,128]{2,1,0:T(8,128)(2,1)S(1)} collective-permute-done((bf16[4,112,128]{2,1,0:T(8,128)(2,1)S(1)}, bf16[4,112,128]{2,1,0:T(8,128)(2,1)S(1)}, u32[]{:S(2)}, u32[]{:S(2)}) %collective-permute-start.3) | collective-permute-done | bytes 114720 | tf_op jit(solution)/shard_map/ppermute | solution.py:533
  16.1 2.6 %collective-permute-start.4 = (bf16[224,128]{1,0:T(8,128)(2,1)S(1)}, bf16[224,128]{1,0:T(8,128)(2,1)S(1)}, u32[]{:S(2)}, u32[]{:S(2)}) collective-permute-start(bf16[224,128]{1,0:T(8,128)(2,1)S(1)} %get-tuple-element.91), channel_id=1, source_target_pairs={{0,12},{2,14},{4,8},{6,10},{8,4},{10,6},{12,0},{14,2},{16,28},{18,... | collective-permute-start | bytes 172040 | tf_op jit(solution)/shard_map/ppermute | solution.py:533
  18.7 0.5 %collective-permute-start.5 = (bf16[224,128]{1,0:T(8,128)(2,1)S(1)}, bf16[224,128]{1,0:T(8,128)(2,1)S(1)}, u32[]{:S(2)}, u32[]{:S(2)}) collective-permute-start(bf16[224,128]{1,0:T(8,128)(2,1)S(1)} %get-tuple-element.92), channel_id=1, source_target_pairs={{0,8},{2,10},{4,12},{6,14},{8,0},{10,2},{12,4},{14,6},{16,24},{18,... | collective-permute-start | bytes 172040 | tf_op jit(solution)/shard_map/ppermute | solution.py:533
  19.2 0.5 %collective-permute-start.6 = (bf16[224,128]{1,0:T(8,128)(2,1)S(1)}, bf16[224,128]{1,0:T(8,128)(2,1)S(1)}, u32[]{:S(2)}, u32[]{:S(2)}) collective-permute-start(bf16[224,128]{1,0:T(8,128)(2,1)S(1)} %get-tuple-element.93), channel_id=1, source_target_pairs={{0,4},{2,6},{4,0},{6,2},{8,12},{10,14},{12,8},{14,10},{16,20},{18,... | collective-permute-start | bytes 172040 | tf_op jit(solution)/shard_map/ppermute | solution.py:533
  19.7 1.8 %shard_map.109.features_ref = bf16[2,64,4096]{2,1,0:T(8,128)(2,1)S(1)} custom-call(bf16[64,1024]{1,0:T(8,128)(2,1)S(1)} %get-tuple-element.81.pre_b0_ref, bf16[64,1024]{1,0:T(8,128)(2,1)S(1)} %get-tuple-element.82.pre_b1_ref, bf16[256,576]{1,0:T(8,128)(2,1)S(1)} %get-tuple-element.83.wf_ref), custom_call_target="tpu_custom_call" | custom-call | flops 1000000000 | bytes 1048576 | tf_op jit(solution)/shard_map/pallas_call | solution.py:514
  21.4 0.0 collective-permute-done.4.a_ref
  21.5 1.4 %collective-permute-done.5.b_ref = bf16[224,128]{1,0:T(8,128)(2,1)S(1)} collective-permute-done((bf16[224,128]{1,0:T(8,128)(2,1)S(1)}, bf16[224,128]{1,0:T(8,128)(2,1)S(1)}, u32[]{:S(2)}, u32[]{:S(2)}) %collective-permute-start.5) | collective-permute-done | bytes 57376 | tf_op jit(solution)/shard_map/ppermute | solution.py:533
  22.9 0.5 %collective-permute-done.6.c_ref = bf16[224,128]{1,0:T(8,128)(2,1)S(1)} collective-permute-done((bf16[224,128]{1,0:T(8,128)(2,1)S(1)}, bf16[224,128]{1,0:T(8,128)(2,1)S(1)}, u32[]{:S(2)}, u32[]{:S(2)}) %collective-permute-start.6) | collective-permute-done | bytes 57376 | tf_op jit(solution)/shard_map/ppermute | solution.py:533
  23.4 3.7 %collective-permute-start.7 = (bf16[112,128]{1,0:T(8,128)(2,1)S(1)}, bf16[112,128]{1,0:T(8,128)(2,1)S(1)}, u32[]{:S(2)}, u32[]{:S(2)}) collective-permute-start(bf16[112,128]{1,0:T(8,128)(2,1)S(1)} %get-tuple-element.97), channel_id=1, source_target_pairs={{0,17},{1,16},{2,19},{3,18},{4,21},{5,20},{6,23},{7,22},{8,25},{9,... | collective-permute-start | bytes 86024 | tf_op jit(solution)/shard_map/ppermute | solution.py:529
  27.0 0.3 collective-permute-start.8
  27.4 0.5 %collective-permute-start.9 = (bf16[112,128]{1,0:T(8,128)(2,1)S(1)}, bf16[112,128]{1,0:T(8,128)(2,1)S(1)}, u32[]{:S(2)}, u32[]{:S(2)}) collective-permute-start(bf16[112,128]{1,0:T(8,128)(2,1)S(1)} %get-tuple-element.98), channel_id=1, source_target_pairs={{0,1},{1,0},{2,3},{3,2},{4,5},{5,4},{6,7},{7,6},{8,9},{9,8},{10,11... | collective-permute-start | bytes 86024 | tf_op jit(solution)/shard_map/ppermute | solution.py:529
  27.8 1.0 %shard_map.111 = bf16[2,64,4096]{2,1,0:T(8,128)(2,1)} custom-call(bf16[2,64,4096]{2,1,0:T(8,128)(2,1)S(1)} %shard_map.109.features_ref), custom_call_target="tpu_custom_call" | custom-call | flops 1000000000 | bytes 1048576 | tf_op jit(solution)/shard_map/pallas_call | solution.py:514
  28.8 0.4 %collective-permute-done.7.a_ref = bf16[112,128]{1,0:T(8,128)(2,1)S(1)} collective-permute-done((bf16[112,128]{1,0:T(8,128)(2,1)S(1)}, bf16[112,128]{1,0:T(8,128)(2,1)S(1)}, u32[]{:S(2)}, u32[]{:S(2)}) %collective-permute-start.7) | collective-permute-done | bytes 28704 | tf_op jit(solution)/shard_map/ppermute | solution.py:529
  29.3 2.5 %collective-permute-done.8.b_ref = bf16[112,128]{1,0:T(8,128)(2,1)S(1)} collective-permute-done((bf16[112,128]{1,0:T(8,128)(2,1)S(1)}, bf16[112,128]{1,0:T(8,128)(2,1)S(1)}, u32[]{:S(2)}, u32[]{:S(2)}) %collective-permute-start.8) | collective-permute-done | bytes 28704 | tf_op jit(solution)/shard_map/ppermute | solution.py:529
  31.8 0.0 collective-permute-done.9.c_ref
  31.8 1.2 %shard_map.113 = (f32[8,1600]{1,0:T(8,128)}, f32[1,64]{1,0:T(1,128)}) custom-call(f32[112,128]{1,0:T(8,128)S(1)} %get-tuple-element.96.own_ref, bf16[112,128]{1,0:T(8,128)(2,1)S(1)} %collective-permute-done.7.a_ref, bf16[112,128]{1,0:T(8,128)(2,1)S(1)} %collective-permute-done.8.b_ref, bf16[112,128]{1,0:T(8,128)(2,1)S(1)} %collective-permute-done.9.c_ref), custom_call_target="tpu_custom_call" | custom-call | bytes 1048576 | tf_op jit(solution)/shard_map/pallas_call | solution.py:514
  (5 shorter events, 0.1 us)
Async XLA Ops:
  0.6 5.4 %copy-start = (bf16[1,2,64,4096]{3,2,1,0:T(8,128)(2,1)S(1)}, bf16[1,2,64,4096]{3,2,1,0:T(8,128)(2,1)}, u32[]{:S(2)}) copy-start(bf16[1,2,64,4096]{3,2,1,0:T(8,128)(2,1)} %param.8) | copy-start | bytes 3145732
  3.5 6.4 %collective-permute-start.1 = (bf16[528,128]{1,0:T(8,128)(2,1)S(1)}, bf16[528,128]{1,0:T(8,128)(2,1)S(1)}, u32[]{:S(2)}, u32[]{:S(2)}) collective-permute-start(bf16[528,128]{1,0:T(8,128)(2,1)S(1)} %get-tuple-element.57.sent_ref.refs_6_), channel_id=1, source_target_pairs={{0,3},{1,2},{2,1},{3,0},{4,7},{5,6},{6,5},{7,4},{8,11},{9,10},{10,... | collective-permute-start | bytes 405512 | tf_op jit(solution)/shard_map/ppermute | solution.py:529
  6.0 2.2 %copy-start.1 = (bf16[2,64,1024]{2,1,0:T(8,128)(2,1)S(1)}, bf16[2,64,1024]{2,1,0:T(8,128)(2,1)}, u32[]{:S(2)}) copy-start(bf16[2,64,1024]{2,1,0:T(8,128)(2,1)} %ws_ref.1) | copy-start | bytes 786436
  6.0 2.2 %copy-start.2 = (bf16[2,64,576]{2,1,0:T(8,128)(2,1)S(1)}, bf16[2,64,576]{2,1,0:T(8,128)(2,1)}, u32[]{:S(2)}) copy-start(bf16[2,64,576]{2,1,0:T(8,128)(2,1)} %wd_ref.1) | copy-start | bytes 442372
  7.4 2.6 %collective-permute-start.2 = (bf16[2,528,128]{2,1,0:T(8,128)(2,1)S(1)}, bf16[2,528,128]{2,1,0:T(8,128)(2,1)S(1)}, u32[]{:S(2)}, u32[]{:S(2)}) collective-permute-start(bf16[2,528,128]{2,1,0:T(8,128)(2,1)S(1)} %get-tuple-element.65), channel_id=1, source_target_pairs={{0,2},{2,0},{4,6},{6,4},{8,10},{10,8},{12,14},{14,12},{16,18},{18,... | collective-permute-start | bytes 811016 | tf_op jit(solution)/shard_map/ppermute | solution.py:533
  8.1 5.6 %collective-permute-start = (bf16[528,128]{1,0:T(8,128)(2,1)S(1)}, bf16[528,128]{1,0:T(8,128)(2,1)S(1)}, u32[]{:S(2)}, u32[]{:S(2)}) collective-permute-start(bf16[528,128]{1,0:T(8,128)(2,1)S(1)} %get-tuple-element.63.refs_7_), channel_id=1, source_target_pairs={{0,3},{1,2},{2,1},{3,0},{4,7},{5,6},{6,5},{7,4},{8,11},{9,10},{10,... | collective-permute-start | bytes 405512 | tf_op jit(solution)/shard_map/ppermute | solution.py:529
  14.7 1.4 %collective-permute-start.3 = (bf16[4,112,128]{2,1,0:T(8,128)(2,1)S(1)}, bf16[4,112,128]{2,1,0:T(8,128)(2,1)S(1)}, u32[]{:S(2)}, u32[]{:S(2)}) collective-permute-start(bf16[4,112,128]{2,1,0:T(8,128)(2,1)S(1)} %get-tuple-element.87), channel_id=1, source_target_pairs={{0,2},{2,0},{4,6},{6,4},{8,10},{10,8},{12,14},{14,12},{16,18},{18,... | collective-permute-start | bytes 344072 | tf_op jit(solution)/shard_map/ppermute | solution.py:533
  16.1 5.4 %collective-permute-start.4 = (bf16[224,128]{1,0:T(8,128)(2,1)S(1)}, bf16[224,128]{1,0:T(8,128)(2,1)S(1)}, u32[]{:S(2)}, u32[]{:S(2)}) collective-permute-start(bf16[224,128]{1,0:T(8,128)(2,1)S(1)} %get-tuple-element.91), channel_id=1, source_target_pairs={{0,12},{2,14},{4,8},{6,10},{8,4},{10,6},{12,0},{14,2},{16,28},{18,... | collective-permute-start | bytes 172040 | tf_op jit(solution)/shard_map/ppermute | solution.py:533
  18.7 4.2 %collective-permute-start.5 = (bf16[224,128]{1,0:T(8,128)(2,1)S(1)}, bf16[224,128]{1,0:T(8,128)(2,1)S(1)}, u32[]{:S(2)}, u32[]{:S(2)}) collective-permute-start(bf16[224,128]{1,0:T(8,128)(2,1)S(1)} %get-tuple-element.92), channel_id=1, source_target_pairs={{0,8},{2,10},{4,12},{6,14},{8,0},{10,2},{12,4},{14,6},{16,24},{18,... | collective-permute-start | bytes 172040 | tf_op jit(solution)/shard_map/ppermute | solution.py:533
  19.2 4.2 %collective-permute-start.6 = (bf16[224,128]{1,0:T(8,128)(2,1)S(1)}, bf16[224,128]{1,0:T(8,128)(2,1)S(1)}, u32[]{:S(2)}, u32[]{:S(2)}) collective-permute-start(bf16[224,128]{1,0:T(8,128)(2,1)S(1)} %get-tuple-element.93), channel_id=1, source_target_pairs={{0,4},{2,6},{4,0},{6,2},{8,12},{10,14},{12,8},{14,10},{16,20},{18,... | collective-permute-start | bytes 172040 | tf_op jit(solution)/shard_map/ppermute | solution.py:533
  23.4 5.9 %collective-permute-start.7 = (bf16[112,128]{1,0:T(8,128)(2,1)S(1)}, bf16[112,128]{1,0:T(8,128)(2,1)S(1)}, u32[]{:S(2)}, u32[]{:S(2)}) collective-permute-start(bf16[112,128]{1,0:T(8,128)(2,1)S(1)} %get-tuple-element.97), channel_id=1, source_target_pairs={{0,17},{1,16},{2,19},{3,18},{4,21},{5,20},{6,23},{7,22},{8,25},{9,... | collective-permute-start | bytes 86024 | tf_op jit(solution)/shard_map/ppermute | solution.py:529
  27.0 4.8 %collective-permute-start.8 = (bf16[112,128]{1,0:T(8,128)(2,1)S(1)}, bf16[112,128]{1,0:T(8,128)(2,1)S(1)}, u32[]{:S(2)}, u32[]{:S(2)}) collective-permute-start(bf16[112,128]{1,0:T(8,128)(2,1)S(1)} %get-tuple-element.97), channel_id=1, source_target_pairs={{0,16},{1,17},{2,18},{3,19},{4,20},{5,21},{6,22},{7,23},{8,24},{9,... | collective-permute-start | bytes 86024 | tf_op jit(solution)/shard_map/ppermute | solution.py:529
  27.4 4.4 %collective-permute-start.9 = (bf16[112,128]{1,0:T(8,128)(2,1)S(1)}, bf16[112,128]{1,0:T(8,128)(2,1)S(1)}, u32[]{:S(2)}, u32[]{:S(2)}) collective-permute-start(bf16[112,128]{1,0:T(8,128)(2,1)S(1)} %get-tuple-element.98), channel_id=1, source_target_pairs={{0,1},{1,0},{2,3},{3,2},{4,5},{5,4},{6,7},{7,6},{8,9},{9,8},{10,11... | collective-permute-start | bytes 86024 | tf_op jit(solution)/shard_map/ppermute | solution.py:529

commit v8 on v7

--- a/solution.py
+++ b/solution.py
@@ -139,7 +139,7 @@
 
 def first_kernel(
     owner_hbm, x_hbm, ws_hbm, wd_hbm, bias_hbm, cot_hbm,
-    ph_ref, pre_ref, act_ref, send_ref, strided_ref, dilated_ref, bias_ref, cot_ref,
+    ph_ref, pre_ref, act_ref, send_ref, strided_ref, dilated_ref, bias_ref, cot_ref, later_ref,
     x_ref, ws_ref, wd_ref, table_ref, owner_ref, wscr, im_scr, sems,
 ):
     scene = lax.axis_index("scene")
@@ -161,6 +161,8 @@
         copy.start()
     for copy in copies:
         copy.wait()
+    later = pltpu.make_async_copy(x_hbm.at[1], later_ref, sems.at[6])
+    later.start()
     mats = tap_matrices(ws_ref[...], 16, wscr)
     for k, rt in enumerate(ROW_ORDER):
         line = jnp.concatenate(mats[rt * 4 : rt * 4 + 4], axis=0)
@@ -175,6 +177,7 @@
         x_ref, cot_ref[...].astype(F32)[0:1, :], strided_ref[...], dilated_ref[...], bias_ref[:, 0:1],
         ph_ref, pre_ref, act_ref, send_ref, im_scr,
     )
+    later.wait()
 
 
 def later_kernel(
@@ -182,7 +185,7 @@
     ph_ref, pre_ref, act_ref, send_ref, both_ref, im_scr,
 ):
     forward_patch(
-        x_ref.at[1], cot_ref[...].astype(F32)[1:2, :], w_strided_ref[...], w_dilated_ref[...],
+        x_ref, cot_ref[...].astype(F32)[1:2, :], w_strided_ref[...], w_dilated_ref[...],
         bias_ref[:, 0:1], ph_ref, pre_ref, act_ref, send_ref, im_scr,
     )
     both_ref[0] = sent_ref[...]
@@ -602,8 +605,9 @@
         ((3 * channels, 3 * channels), BF16),
         ((channels, 128), F32),
         (own_cot.shape, BF16),
+        ((channels, cells_in), BF16),
     ]
-    *part, w_strided, w_dilated, bias_col, cot = call(
+    *part, w_strided, w_dilated, bias_col, cot, later = call(
         first_kernel,
         first_outs,
         "hhhhhh",
@@ -615,7 +619,7 @@
             pltpu.SMEM(tile_owner.shape, jnp.int32),
             wscr,
             im_scr,
-            pltpu.SemaphoreType.DMA((6,)),
+            pltpu.SemaphoreType.DMA((7,)),
         ],
         tile_owner, features, strided_weights, dilated_weights, tile_bias, own_cot,
         flops=10**9,
@@ -626,7 +630,7 @@
         patch_outs + [((2,) + payload, BF16)],
         "vvvvvv",
         [im_scr],
-        features, cot, w_strided, w_dilated, bias_col, part[3],
+        later, cot, w_strided, w_dilated, bias_col, part[3],
         flops=10**10,
     )
     far.append(device_xor(late[3], 1, 1))

time: 33.2 us -> 33.1 us (level)
  no operation moved by 1% of the time
where the time goes in v8:
time: 33.1 us; the launch traced here: 32.9 us
  Pallas kernels  12.1 us (37%)
  starting transfers between devices  11.4 us (34%)
  waiting for transfers between devices  8.67 us (26%)
  between operations  0.7 us (2%)
    pallas_call x11, Pallas kernels, call(): pl.pallas_call(kernel, out_shape=[jax.ShapeDtypeStruct(shape, kind) for s...  12.1 us
    ppermute x5, starting transfers between devices, device_pairs(): return lax.ppermute(x, ('scene', 'tile'), flat)  6.94 us
    ppermute x5, waiting for transfers between devices, device_pairs(): return lax.ppermute(x, ('scene', 'tile'), flat)  6.09 us
    ppermute x5, starting transfers between devices, scene_xor(): lax.ppermute(x, 'scene', [(i, i ^ distance) for i in range(lax.axis_size(...  4.48 us
    ppermute x5, waiting for transfers between devices, scene_xor(): lax.ppermute(x, 'scene', [(i, i ^ distance) for i in range(lax.axis_size(...  2.58 us
  transfers between devices with their start and end apart: 10, of which 7 were waited for; matrix products, arithmetic and copies ran while one was open for 0% of the time, Pallas kernels for 22%

profile of v8, /device:TPU:0, one launch (start us, length us, event | category | flops | bytes accessed | tf_op | source)
XLA Modules:
  0.0 32.9 jit_solution(2113274321797653443)
XLA Ops:
  0.6 2.8 %shard_map.103 = (bf16[256,1024]{1,0:T(8,128)(2,1)S(1)}, f32[64,1024]{1,0:T(8,128)S(1)}, bf16[64,1024]{1,0:T(8,128)(2,1)S(1)}, bf16[528,128]{1,0:T(8,128)(2,1)S(...) custom-call(s32[16]{0:T(128)} %owner_hbm.3, ...), custom_call_target="tpu_custom_call" | custom-call | flops 1000000000 | bytes 1048576 | tf_op jit(solution)/shard_map/pallas_call | solution.py:517
  3.5 2.4 %collective-permute-start.1 = (bf16[528,128]{1,0:T(8,128)(2,1)S(1)}, bf16[528,128]{1,0:T(8,128)(2,1)S(1)}, u32[]{:S(2)}, u32[]{:S(2)}) collective-permute-start(bf16[528,128]{1,0:T(8,128)(2,1)S(1)} %get-tuple-element.59.sent_ref.refs_6_), channel_id=1, source_target_pairs={{0,3},{1,2},{2,1},{3,0},{4,7},{5,6},{6,5},{7,4},{8,11},{9,10},{10,... | collective-permute-start | bytes 405512 | tf_op jit(solution)/shard_map/ppermute | solution.py:532
  5.9 0.0 copy-start
  5.9 1.4 %shard_map.104 = (bf16[256,1024]{1,0:T(8,128)(2,1)S(1)}, f32[64,1024]{1,0:T(8,128)S(1)}, bf16[64,1024]{1,0:T(8,128)(2,1)S(1)}, bf16[528,128]{1,0:T(8,128)(2,1)S(1)}, bf16[2,528,128]{2,1,0:T(8,128)(2,1)S(1)}) custom-call(bf16[64,4096]{1,0:T(8,128)(2,1)S(1)} %get-tuple-element.54.x_ref, bf16[2,1024]{1,0:T(2,128)(2,1)S(1)} %get-tuple-element.55.cot_ref, ...), custom_call_target="tpu_custom_call" | custom-call | flops 10000000000 | bytes 1048576 | tf_op jit(solution)/shard_map/pallas_call | solution.py:517
  7.3 0.7 %collective-permute-start.2 = (bf16[2,528,128]{2,1,0:T(8,128)(2,1)S(1)}, bf16[2,528,128]{2,1,0:T(8,128)(2,1)S(1)}, u32[]{:S(2)}, u32[]{:S(2)}) collective-permute-start(bf16[2,528,128]{2,1,0:T(8,128)(2,1)S(1)} %get-tuple-element.67), channel_id=1, source_target_pairs={{0,2},{2,0},{4,6},{6,4},{8,10},{10,8},{12,14},{14,12},{16,18},{18,... | collective-permute-start | bytes 811016 | tf_op jit(solution)/shard_map/ppermute | solution.py:536
  8.0 0.0 collective-permute-start
  8.1 0.0 copy-done
  8.1 0.0 copy-done.1
  8.1 1.2 %shard_map.105 = (f32[64,1024]{1,0:T(8,128)S(1)}, f32[64,1024]{1,0:T(8,128)S(1)}, bf16[64,1024]{1,0:T(8,128)(2,1)S(1)}, bf16[64,1024]{1,0:T(8,128)(2,1)S(1)}, bf...) custom-call(s32[4,8]{1,0:T(4,128)} %bitcast.6, ...), custom_call_target="tpu_custom_call" | custom-call | flops 10000000000 | bytes 1048576 | tf_op jit(solution)/shard_map/pallas_call | solution.py:517
  9.3 0.6 %collective-permute-done.1.far0_ref = bf16[528,128]{1,0:T(8,128)(2,1)S(1)} collective-permute-done((bf16[528,128]{1,0:T(8,128)(2,1)S(1)}, bf16[528,128]{1,0:T(8,128)(2,1)S(1)}, u32[]{:S(2)}, u32[]{:S(2)}) %collective-permute-start.1) | collective-permute-done | bytes 135200 | tf_op jit(solution)/shard_map/ppermute | solution.py:532
  9.9 0.0 collective-permute-done.2.near_ref
  9.9 1.3 %shard_map.106 = (bf16[528,128]{1,0:T(8,128)(2,1)S(1)}, bf16[64,1024]{1,0:T(8,128)(2,1)S(1)}, f32[64,128]{1,0:T(8,128)S(1)}, f32[576,128]{1,0:T(8,128)S(1)}, f32[576,256]{1,0:T(8,128)S(1)}) custom-call(bf16[528,128]{1,0:T(8,128)(2,1)S(1)} %collective-permute-done.1.far0_ref, bf16[2,528,128]{2,1,0:T(8,128)(2,1)S(1)} %collective-permute-done.2.near_ref, ...), custom_call_target="tpu_custom_call" | custom-call | flops 1000000000 | bytes 1048576 | tf_op jit(solution)/shard_map/pallas_call | solution.py:517
  11.1 2.5 %collective-permute-done.far1_ref = bf16[528,128]{1,0:T(8,128)(2,1)S(1)} collective-permute-done((bf16[528,128]{1,0:T(8,128)(2,1)S(1)}, bf16[528,128]{1,0:T(8,128)(2,1)S(1)}, u32[]{:S(2)}, u32[]{:S(2)}) %collective-permute-start) | collective-permute-done | bytes 135200 | tf_op jit(solution)/shard_map/ppermute | solution.py:532
  13.7 0.9 %shard_map.107 = (bf16[64,1024]{1,0:T(8,128)(2,1)S(1)}, f32[8,128]{1,0:T(8,128)S(1)}, bf16[4,112,128]{2,1,0:T(8,128)(2,1)S(1)}, bf16[576,1024]{1,0:T(8,128)(2,1)S(1)}) custom-call(bf16[528,128]{1,0:T(8,128)(2,1)S(1)} %collective-permute-done.far1_ref, bf16[528,128]{1,0:T(8,128)(2,1)S(1)} %get-tuple-element.73.pick_ref, ...), custom_call_target="tpu_custom_call" | custom-call | flops 1000000000 | bytes 1048576 | tf_op jit(solution)/shard_map/pallas_call | solution.py:517
  14.6 0.2 collective-permute-start.3
  14.8 0.5 %shard_map.108 = (bf16[4,112,128]{2,1,0:T(8,128)(2,1)S(1)}, bf16[64,1024]{1,0:T(8,128)(2,1)S(1)}, bf16[64,1024]{1,0:T(8,128)(2,1)S(1)}) custom-call(f32[16,128]{1,0:T(8,128)S(1)} %get-tuple-element.66.select_ref, bf16[576,1024]{1,0:T(8,128)(2,1)S(1)} %get-tuple-element.80.out_shifts_ref, bf16[64,1024]{1,0:T(8,128)(2,1)S(1)} %get-tuple-element.81.pre_b_ref, ...), custom_call_target="tpu_custom_call" | custom-call | flops 1000000000 | bytes 1048576 | tf_op jit(solution)/shard_map/pallas_call | solution.py:517
  15.3 0.7 %collective-permute-done.3.got_ref = bf16[4,112,128]{2,1,0:T(8,128)(2,1)S(1)} collective-permute-done((bf16[4,112,128]{2,1,0:T(8,128)(2,1)S(1)}, bf16[4,112,128]{2,1,0:T(8,128)(2,1)S(1)}, u32[]{:S(2)}, u32[]{:S(2)}) %collective-permute-start.3) | collective-permute-done | bytes 114720 | tf_op jit(solution)/shard_map/ppermute | solution.py:536
  16.0 2.6 %collective-permute-start.4 = (bf16[224,128]{1,0:T(8,128)(2,1)S(1)}, bf16[224,128]{1,0:T(8,128)(2,1)S(1)}, u32[]{:S(2)}, u32[]{:S(2)}) collective-permute-start(bf16[224,128]{1,0:T(8,128)(2,1)S(1)} %get-tuple-element.93), channel_id=1, source_target_pairs={{0,12},{2,14},{4,8},{6,10},{8,4},{10,6},{12,0},{14,2},{16,28},{18,... | collective-permute-start | bytes 172040 | tf_op jit(solution)/shard_map/ppermute | solution.py:536
  18.6 0.4 %collective-permute-start.5 = (bf16[224,128]{1,0:T(8,128)(2,1)S(1)}, bf16[224,128]{1,0:T(8,128)(2,1)S(1)}, u32[]{:S(2)}, u32[]{:S(2)}) collective-permute-start(bf16[224,128]{1,0:T(8,128)(2,1)S(1)} %get-tuple-element.94), channel_id=1, source_target_pairs={{0,8},{2,10},{4,12},{6,14},{8,0},{10,2},{12,4},{14,6},{16,24},{18,... | collective-permute-start | bytes 172040 | tf_op jit(solution)/shard_map/ppermute | solution.py:536
  19.1 0.5 %collective-permute-start.6 = (bf16[224,128]{1,0:T(8,128)(2,1)S(1)}, bf16[224,128]{1,0:T(8,128)(2,1)S(1)}, u32[]{:S(2)}, u32[]{:S(2)}) collective-permute-start(bf16[224,128]{1,0:T(8,128)(2,1)S(1)} %get-tuple-element.95), channel_id=1, source_target_pairs={{0,4},{2,6},{4,0},{6,2},{8,12},{10,14},{12,8},{14,10},{16,20},{18,... | collective-permute-start | bytes 172040 | tf_op jit(solution)/shard_map/ppermute | solution.py:536
  19.6 1.8 %shard_map.109.features_ref = bf16[2,64,4096]{2,1,0:T(8,128)(2,1)S(1)} custom-call(bf16[64,1024]{1,0:T(8,128)(2,1)S(1)} %get-tuple-element.83.pre_b0_ref, bf16[64,1024]{1,0:T(8,128)(2,1)S(1)} %get-tuple-element.84.pre_b1_ref, bf16[256,576]{1,0:T(8,128)(2,1)S(1)} %get-tuple-element.85.wf_ref), custom_call_target="tpu_custom_call" | custom-call | flops 1000000000 | bytes 1048576 | tf_op jit(solution)/shard_map/pallas_call | solution.py:517
  21.3 0.0 collective-permute-done.4.a_ref
  21.4 1.4 %collective-permute-done.5.b_ref = bf16[224,128]{1,0:T(8,128)(2,1)S(1)} collective-permute-done((bf16[224,128]{1,0:T(8,128)(2,1)S(1)}, bf16[224,128]{1,0:T(8,128)(2,1)S(1)}, u32[]{:S(2)}, u32[]{:S(2)}) %collective-permute-start.5) | collective-permute-done | bytes 57376 | tf_op jit(solution)/shard_map/ppermute | solution.py:536
  22.8 0.4 %collective-permute-done.6.c_ref = bf16[224,128]{1,0:T(8,128)(2,1)S(1)} collective-permute-done((bf16[224,128]{1,0:T(8,128)(2,1)S(1)}, bf16[224,128]{1,0:T(8,128)(2,1)S(1)}, u32[]{:S(2)}, u32[]{:S(2)}) %collective-permute-start.6) | collective-permute-done | bytes 57376 | tf_op jit(solution)/shard_map/ppermute | solution.py:536
  23.3 3.7 %collective-permute-start.7 = (bf16[112,128]{1,0:T(8,128)(2,1)S(1)}, bf16[112,128]{1,0:T(8,128)(2,1)S(1)}, u32[]{:S(2)}, u32[]{:S(2)}) collective-permute-start(bf16[112,128]{1,0:T(8,128)(2,1)S(1)} %get-tuple-element.99), channel_id=1, source_target_pairs={{0,17},{1,16},{2,19},{3,18},{4,21},{5,20},{6,23},{7,22},{8,25},{9,... | collective-permute-start | bytes 86024 | tf_op jit(solution)/shard_map/ppermute | solution.py:532
  27.0 0.3 collective-permute-start.8
  27.3 0.5 %collective-permute-start.9 = (bf16[112,128]{1,0:T(8,128)(2,1)S(1)}, bf16[112,128]{1,0:T(8,128)(2,1)S(1)}, u32[]{:S(2)}, u32[]{:S(2)}) collective-permute-start(bf16[112,128]{1,0:T(8,128)(2,1)S(1)} %get-tuple-element.100), channel_id=1, source_target_pairs={{0,1},{1,0},{2,3},{3,2},{4,5},{5,4},{6,7},{7,6},{8,9},{9,8},{10,11... | collective-permute-start | bytes 86024 | tf_op jit(solution)/shard_map/ppermute | solution.py:532
  27.7 1.0 %shard_map.111 = bf16[2,64,4096]{2,1,0:T(8,128)(2,1)} custom-call(bf16[2,64,4096]{2,1,0:T(8,128)(2,1)S(1)} %shard_map.109.features_ref), custom_call_target="tpu_custom_call" | custom-call | flops 1000000000 | bytes 1048576 | tf_op jit(solution)/shard_map/pallas_call | solution.py:517
  28.7 0.4 %collective-permute-done.7.a_ref = bf16[112,128]{1,0:T(8,128)(2,1)S(1)} collective-permute-done((bf16[112,128]{1,0:T(8,128)(2,1)S(1)}, bf16[112,128]{1,0:T(8,128)(2,1)S(1)}, u32[]{:S(2)}, u32[]{:S(2)}) %collective-permute-start.7) | collective-permute-done | bytes 28704 | tf_op jit(solution)/shard_map/ppermute | solution.py:532
  29.2 2.6 %collective-permute-done.8.b_ref = bf16[112,128]{1,0:T(8,128)(2,1)S(1)} collective-permute-done((bf16[112,128]{1,0:T(8,128)(2,1)S(1)}, bf16[112,128]{1,0:T(8,128)(2,1)S(1)}, u32[]{:S(2)}, u32[]{:S(2)}) %collective-permute-start.8) | collective-permute-done | bytes 28704 | tf_op jit(solution)/shard_map/ppermute | solution.py:532
  31.7 0.0 collective-permute-done.9.c_ref
  31.7 1.2 %shard_map.113 = (f32[8,1600]{1,0:T(8,128)}, f32[1,64]{1,0:T(1,128)}) custom-call(f32[112,128]{1,0:T(8,128)S(1)} %get-tuple-element.98.own_ref, bf16[112,128]{1,0:T(8,128)(2,1)S(1)} %collective-permute-done.7.a_ref, bf16[112,128]{1,0:T(8,128)(2,1)S(1)} %collective-permute-done.8.b_ref, bf16[112,128]{1,0:T(8,128)(2,1)S(1)} %collective-permute-done.9.c_ref), custom_call_target="tpu_custom_call" | custom-call | bytes 1048576 | tf_op jit(solution)/shard_map/pallas_call | solution.py:517
  (3 shorter events, 0.1 us)
Async XLA Ops:
  3.5 6.4 %collective-permute-start.1 = (bf16[528,128]{1,0:T(8,128)(2,1)S(1)}, bf16[528,128]{1,0:T(8,128)(2,1)S(1)}, u32[]{:S(2)}, u32[]{:S(2)}) collective-permute-start(bf16[528,128]{1,0:T(8,128)(2,1)S(1)} %get-tuple-element.59.sent_ref.refs_6_), channel_id=1, source_target_pairs={{0,3},{1,2},{2,1},{3,0},{4,7},{5,6},{6,5},{7,4},{8,11},{9,10},{10,... | collective-permute-start | bytes 405512 | tf_op jit(solution)/shard_map/ppermute | solution.py:532
  5.9 2.2 %copy-start = (bf16[2,64,1024]{2,1,0:T(8,128)(2,1)S(1)}, bf16[2,64,1024]{2,1,0:T(8,128)(2,1)}, u32[]{:S(2)}) copy-start(bf16[2,64,1024]{2,1,0:T(8,128)(2,1)} %ws_ref.1) | copy-start | bytes 786436
  5.9 2.2 %copy-start.1 = (bf16[2,64,576]{2,1,0:T(8,128)(2,1)S(1)}, bf16[2,64,576]{2,1,0:T(8,128)(2,1)}, u32[]{:S(2)}) copy-start(bf16[2,64,576]{2,1,0:T(8,128)(2,1)} %wd_ref.1) | copy-start | bytes 442372
  7.3 2.6 %collective-permute-start.2 = (bf16[2,528,128]{2,1,0:T(8,128)(2,1)S(1)}, bf16[2,528,128]{2,1,0:T(8,128)(2,1)S(1)}, u32[]{:S(2)}, u32[]{:S(2)}) collective-permute-start(bf16[2,528,128]{2,1,0:T(8,128)(2,1)S(1)} %get-tuple-element.67), channel_id=1, source_target_pairs={{0,2},{2,0},{4,6},{6,4},{8,10},{10,8},{12,14},{14,12},{16,18},{18,... | collective-permute-start | bytes 811016 | tf_op jit(solution)/shard_map/ppermute | solution.py:536
  8.0 5.6 %collective-permute-start = (bf16[528,128]{1,0:T(8,128)(2,1)S(1)}, bf16[528,128]{1,0:T(8,128)(2,1)S(1)}, u32[]{:S(2)}, u32[]{:S(2)}) collective-permute-start(bf16[528,128]{1,0:T(8,128)(2,1)S(1)} %get-tuple-element.65.refs_7_), channel_id=1, source_target_pairs={{0,3},{1,2},{2,1},{3,0},{4,7},{5,6},{6,5},{7,4},{8,11},{9,10},{10,... | collective-permute-start | bytes 405512 | tf_op jit(solution)/shard_map/ppermute | solution.py:532
  14.6 1.4 %collective-permute-start.3 = (bf16[4,112,128]{2,1,0:T(8,128)(2,1)S(1)}, bf16[4,112,128]{2,1,0:T(8,128)(2,1)S(1)}, u32[]{:S(2)}, u32[]{:S(2)}) collective-permute-start(bf16[4,112,128]{2,1,0:T(8,128)(2,1)S(1)} %get-tuple-element.89), channel_id=1, source_target_pairs={{0,2},{2,0},{4,6},{6,4},{8,10},{10,8},{12,14},{14,12},{16,18},{18,... | collective-permute-start | bytes 344072 | tf_op jit(solution)/shard_map/ppermute | solution.py:536
  16.0 5.4 %collective-permute-start.4 = (bf16[224,128]{1,0:T(8,128)(2,1)S(1)}, bf16[224,128]{1,0:T(8,128)(2,1)S(1)}, u32[]{:S(2)}, u32[]{:S(2)}) collective-permute-start(bf16[224,128]{1,0:T(8,128)(2,1)S(1)} %get-tuple-element.93), channel_id=1, source_target_pairs={{0,12},{2,14},{4,8},{6,10},{8,4},{10,6},{12,0},{14,2},{16,28},{18,... | collective-permute-start | bytes 172040 | tf_op jit(solution)/shard_map/ppermute | solution.py:536
  18.6 4.2 %collective-permute-start.5 = (bf16[224,128]{1,0:T(8,128)(2,1)S(1)}, bf16[224,128]{1,0:T(8,128)(2,1)S(1)}, u32[]{:S(2)}, u32[]{:S(2)}) collective-permute-start(bf16[224,128]{1,0:T(8,128)(2,1)S(1)} %get-tuple-element.94), channel_id=1, source_target_pairs={{0,8},{2,10},{4,12},{6,14},{8,0},{10,2},{12,4},{14,6},{16,24},{18,... | collective-permute-start | bytes 172040 | tf_op jit(solution)/shard_map/ppermute | solution.py:536
  19.1 4.2 %collective-permute-start.6 = (bf16[224,128]{1,0:T(8,128)(2,1)S(1)}, bf16[224,128]{1,0:T(8,128)(2,1)S(1)}, u32[]{:S(2)}, u32[]{:S(2)}) collective-permute-start(bf16[224,128]{1,0:T(8,128)(2,1)S(1)} %get-tuple-element.95), channel_id=1, source_target_pairs={{0,4},{2,6},{4,0},{6,2},{8,12},{10,14},{12,8},{14,10},{16,20},{18,... | collective-permute-start | bytes 172040 | tf_op jit(solution)/shard_map/ppermute | solution.py:536
  23.3 5.9 %collective-permute-start.7 = (bf16[112,128]{1,0:T(8,128)(2,1)S(1)}, bf16[112,128]{1,0:T(8,128)(2,1)S(1)}, u32[]{:S(2)}, u32[]{:S(2)}) collective-permute-start(bf16[112,128]{1,0:T(8,128)(2,1)S(1)} %get-tuple-element.99), channel_id=1, source_target_pairs={{0,17},{1,16},{2,19},{3,18},{4,21},{5,20},{6,23},{7,22},{8,25},{9,... | collective-permute-start | bytes 86024 | tf_op jit(solution)/shard_map/ppermute | solution.py:532
  27.0 4.8 %collective-permute-start.8 = (bf16[112,128]{1,0:T(8,128)(2,1)S(1)}, bf16[112,128]{1,0:T(8,128)(2,1)S(1)}, u32[]{:S(2)}, u32[]{:S(2)}) collective-permute-start(bf16[112,128]{1,0:T(8,128)(2,1)S(1)} %get-tuple-element.99), channel_id=1, source_target_pairs={{0,16},{1,17},{2,18},{3,19},{4,20},{5,21},{6,22},{7,23},{8,24},{9,... | collective-permute-start | bytes 86024 | tf_op jit(solution)/shard_map/ppermute | solution.py:532
  27.3 4.4 %collective-permute-start.9 = (bf16[112,128]{1,0:T(8,128)(2,1)S(1)}, bf16[112,128]{1,0:T(8,128)(2,1)S(1)}, u32[]{:S(2)}, u32[]{:S(2)}) collective-permute-start(bf16[112,128]{1,0:T(8,128)(2,1)S(1)} %get-tuple-element.100), channel_id=1, source_target_pairs={{0,1},{1,0},{2,3},{3,2},{4,5},{5,4},{6,7},{7,6},{8,9},{9,8},{10,11... | collective-permute-start | bytes 86024 | tf_op jit(solution)/shard_map/ppermute | solution.py:532
